TPU v7x, 256 devices: a whole 4x4x8 slice. The times are simulated.
256 devices in a mesh: frame: 64 (over x_lo, y, z), space: 4 (over x_hi, core).
Axes of the slice: x: 4 (x_hi: 2, x_lo: 2; x = x_hi * 2 + x_lo), y: 4, z: 8, core: 2. Of those that a mesh axis runs over, the one named last changes fastest.
Arguments:
- latent: bfloat16 [64, 48, 48, 640], P('frame', 'space'), may hold values from -41 to 41
- reference_states: bfloat16 [48, 48, 640], P('space'), may hold values from -6 to 6
- group_gain: float32 [640], replicated, may hold values from 0.1 to 1.9
- conv_weight: bfloat16 [3, 3, 640, 640], replicated, may hold values from -0.078125 to 0.078125
- norm_gain: float32 [640], replicated, may hold values from 0.1 to 1.9
- spatial_query: bfloat16 [640, 320], replicated, may hold values from -0.75 to 0.75
- spatial_key: bfloat16 [640, 320], replicated, may hold values from -0.25 to 0.25
- spatial_value: bfloat16 [640, 320], replicated, may hold values from -0.25 to 0.25
- spatial_out: bfloat16 [320, 640], replicated, may hold values from -0.3125 to 0.3125
- frame_gain: float32 [640], replicated, may hold values from 0.1 to 1.9
- temporal_query: bfloat16 [640, 320], replicated, may hold values from -0.75 to 0.75
- temporal_key: bfloat16 [640, 320], replicated, may hold values from -0.25 to 0.25
- temporal_value: bfloat16 [640, 320], replicated, may hold values from -0.25 to 0.25
- temporal_out: bfloat16 [320, 640], replicated, may hold values from -0.3125 to 0.3125
Outputs:
- output: bfloat16 [64, 48, 48, 640], P('frame', 'space')
All inputs are finite; a program needn't handle non-finite values.
Results may differ from a plain program's by a relative error of at most 0.018.
Values may be sent and summed in bfloat16 or wider, within the bound.
No kernel may reach another device: no remote copies, remote signals or barrier semaphores. Data moves between devices by JAX's collectives and lax.ppermute only.
A program may use at most 128 MiB of HBM per device.

v0:
```python
import functools

import jax
import jax.numpy as jnp
from jax import lax
from jax.experimental import pallas as pl
from jax.experimental.pallas import tpu as pltpu
from jax.sharding import PartitionSpec as P

HEADS = 4
HEAD_DIM = 80
GROUPS = 32
INNER = 320
C = 640
W = 48
STRIP = 12
CELLS = STRIP * W
FRAMES = 64
PLACES = CELLS // FRAMES
LANES = 128
SENT = 48
BACK = 24

epsilon = 1e-05
QUERY_SCALE = HEAD_DIM**-0.5 * 1.4426950408889634

KEY_WINDOW = ((0, 128), (0, 256), (128, 256), (128, 384))
VALUE_WINDOW = ((256, 512), (384, 512), (384, 640), (512, 640))
ACC_AT = (0, 256, 384, 640)
ACC_WIDTH = 768

f32 = jnp.float32
bf16 = jnp.bfloat16


def lane_iota(width, start=0):
    return lax.broadcasted_iota(jnp.int32, (1, width), 1) + start


def layer_norm(values, factor):
    centre = jnp.mean(values, axis=-1, keepdims=True)
    shifted = values - centre
    spread = jnp.mean(shifted * shifted, axis=-1, keepdims=True)
    normed = shifted * lax.rsqrt(spread + epsilon)
    return normed if factor is None else normed * factor


def dot(a, b):
    return jnp.dot(a, b, preferred_element_type=f32)


def vmem(count):
    return [pl.BlockSpec(memory_space=pltpu.VMEM)] * count


def call(body, outs, operands, scratch=(), flops=0, smem=0, limit=48):
    single = not isinstance(outs, (list, tuple))
    specs = [pl.BlockSpec(memory_space=pltpu.SMEM)] * smem + vmem(len(operands) - smem)
    return pl.pallas_call(
        body,
        out_shape=outs,
        in_specs=specs,
        out_specs=vmem(1)[0] if single else vmem(len(outs)),
        scratch_shapes=list(scratch),
        compiler_params=pltpu.CompilerParams(vmem_limit_bytes=limit * 1024 * 1024),
        cost_estimate=pl.CostEstimate(flops=flops, bytes_accessed=1 << 20, transcendentals=0),
    )(*operands)


def stats_kernel(x_ref, sums_ref, top_ref, bottom_ref):
    total = jnp.zeros((1, C), f32)
    square = jnp.zeros((1, C), f32)
    for r in range(STRIP):
        v = x_ref[r * W : (r + 1) * W, :].astype(f32)
        total = total + jnp.sum(v, axis=0, keepdims=True)
        square = square + jnp.sum(v * v, axis=0, keepdims=True)
    pieces = []
    for v in (total, square):
        high = v.astype(bf16).astype(f32)
        middle = (v - high).astype(bf16).astype(f32)
        pieces += [high, middle, v - high - middle]
    pieces += [jnp.zeros((1, C), f32)] * 2
    row = lax.broadcasted_iota(jnp.int32, (8, C), 0)
    stacked = jnp.zeros((8, C), f32)
    for i, p in enumerate(pieces):
        stacked = jnp.where(row == i, p, stacked)
    per = C // GROUPS
    column_group = jnp.floor((lane_iota(C).astype(f32) + 0.5) * (1.0 / per))
    row_at = lax.broadcasted_iota(jnp.int32, (C, 1), 0).astype(f32)
    row_group = jnp.floor((row_at + 0.5) * (1.0 / per))
    same = jnp.where(row_group == column_group, 1.0, 0.0).astype(bf16)
    grouped = dot(stacked.astype(bf16), same)
    group_sum = grouped[0:1] + grouped[1:2] + grouped[2:3]
    group_sq = grouped[3:4] + grouped[4:5] + grouped[5:6]
    sums_ref[...] = jnp.where(row == 0, group_sum, jnp.where(row == 1, group_sq, 0.0))
    top_ref[...] = x_ref[0:W, :]
    bottom_ref[...] = x_ref[CELLS - W :, :]


def reference_kernel(states_ref, weight_ref, out_ref):
    normed = layer_norm(states_ref[...].astype(f32), None).astype(bf16)
    out_ref[...] = dot(normed, weight_ref[...]).astype(bf16)


def conv_kernel(
    flags_ref,
    s0_ref,
    s1_ref,
    s2_ref,
    s3_ref,
    x_ref,
    above_ref,
    below_ref,
    gain_ref,
    kernel_ref,
    norm_gain_ref,
    query_ref,
    kv_ref,
    hidden_out,
    query_out,
    kv_out,
    lhs,
):
    sums = (s0_ref[...] + s1_ref[...]) + (s2_ref[...] + s3_ref[...])
    members = float(4 * CELLS * (C // GROUPS))
    average = sums[0:1] / members
    variance = sums[1:2] / members - average * average
    factor = lax.rsqrt(variance + epsilon) * gain_ref[...]
    at = lax.broadcasted_iota(jnp.int32, (W, 1), 0)

    def place(r, block, keep):
        v = (block.astype(f32) - average) * factor
        act = (0.5 * v) * (1.0 + jnp.tanh(0.5 * v))
        if keep is not None:
            act = jnp.where(keep > 0.5, act, 0.0)
        rows = slice(r * W, (r + 1) * W)
        lhs[rows, C : 2 * C] = act.astype(bf16)
        lhs[rows, 0:C] = jnp.where(at == 0, 0.0, pltpu.roll(act, 1, 0)).astype(bf16)
        lhs[rows, 2 * C :] = jnp.where(at == W - 1, 0.0, pltpu.roll(act, W - 1, 0)).astype(bf16)

    place(0, above_ref[...], flags_ref[0, 0])
    for r in range(STRIP):
        place(r + 1, x_ref[r * W : (r + 1) * W, :], None)
    place(STRIP + 1, below_ref[...], flags_ref[0, 1])
    total = dot(lhs[0:CELLS, :], kernel_ref[0])
    total = total + dot(lhs[W : W + CELLS, :], kernel_ref[1])
    total = total + dot(lhs[2 * W : 2 * W + CELLS, :], kernel_ref[2])
    hidden = (x_ref[...].astype(f32) + total).astype(bf16)
    hidden_out[...] = hidden
    normed = layer_norm(hidden.astype(f32), norm_gain_ref[...]).astype(bf16)
    query_out[...] = (dot(normed, query_ref[...]) * QUERY_SCALE).astype(bf16)
    kv_out[...] = dot(normed, kv_ref[...]).astype(bf16)


def head_query(query, h):
    low, high = KEY_WINDOW[h]
    lane = lane_iota(high - low, low)
    inside = (lane >= h * HEAD_DIM) & (lane < (h + 1) * HEAD_DIM)
    return jnp.where(inside, query[:, low:high], jnp.zeros((), bf16))


def inside_value(h):
    low, high = VALUE_WINDOW[h]
    lane = lane_iota(high - low, low)
    return (lane >= INNER + h * HEAD_DIM) & (lane < INNER + (h + 1) * HEAD_DIM)


def attend(query, kv_refs, tile, start):
    gathered = []
    for h in range(HEADS):
        key_low, key_high = KEY_WINDOW[h]
        low, high = VALUE_WINDOW[h]
        mine = head_query(query, h)
        inside = inside_value(h)
        acc = None if start is None else start(h)
        for ref in kv_refs:
            for first in range(0, ref.shape[0], tile):
                rows = slice(first, min(first + tile, ref.shape[0]))
                scores = lax.dot_general(
                    mine,
                    ref[rows, key_low:key_high],
                    (((1,), (1,)), ((), ())),
                    preferred_element_type=f32,
                )
                weights = jnp.exp2(scores).astype(bf16)
                values = jnp.where(inside, ref[rows, low:high], jnp.ones((), bf16))
                part = dot(weights, values)
                acc = part if acc is None else acc + part
        gathered.append(acc)
    return gathered


def normalised(gathered):
    blocks = [None, None, None]
    for h in range(HEADS):
        low, high = VALUE_WINDOW[h]
        acc = gathered[h]
        spare = 0 if INNER + h * HEAD_DIM > low else high - low - 1
        result = acc * (1.0 / acc[:, spare : spare + 1])
        result = jnp.where(inside_value(h), result, 0.0)
        for b in range((high - low) // LANES):
            at = low // LANES + b - 2
            piece = result[:, b * LANES : (b + 1) * LANES]
            blocks[at] = piece if blocks[at] is None else blocks[at] + piece
    return blocks


def attention_kernel(n_kv, has_start, tile, *refs):
    query_ref = refs[0]
    kv_refs = refs[1 : 1 + n_kv]
    start = None
    if has_start:
        acc_ref = refs[1 + n_kv]
        start = lambda h: acc_ref[:, ACC_AT[h] : ACC_AT[h] + VALUE_WINDOW[h][1] - VALUE_WINDOW[h][0]]
    out_ref = refs[-1]
    for h, acc in enumerate(attend(query_ref[...], kv_refs, tile, start)):
        out_ref[:, ACC_AT[h] : ACC_AT[h] + acc.shape[1]] = acc


def last_attention_kernel(
    n_kv, tile, query_ref, acc_ref, hidden_ref, weight_ref, gain_ref, *refs
):
    kv_refs = refs[:n_kv]
    mixed_out, sent_out, rows = refs[n_kv:]
    start = lambda h: acc_ref[:, ACC_AT[h] : ACC_AT[h] + VALUE_WINDOW[h][1] - VALUE_WINDOW[h][0]]
    blocks = normalised(attend(query_ref[...], kv_refs, tile, start))
    update = None
    for b in range(3):
        part = dot(blocks[b].astype(bf16), weight_ref[b * LANES : (b + 1) * LANES, :])
        update = part if update is None else update + part
    mixed = (hidden_ref[...].astype(f32) + update).astype(bf16)
    mixed_out[...] = mixed
    framed = layer_norm(mixed.astype(f32), gain_ref[...])
    for j in range(PLACES):
        for c in range(C // LANES):
            rows[pl.ds(j * 5 + c, FRAMES, stride=SENT), :] = framed[
                j * FRAMES : (j + 1) * FRAMES, c * LANES : (c + 1) * LANES
            ]
    for r in range(PLACES * 5, SENT):
        rows[pl.ds(r, FRAMES, stride=SENT), :] = jnp.zeros((FRAMES, LANES), f32)
    sent_out[...] = rows[...].astype(bf16)


def temporal_kernel(got_ref, query_ref, kv_weight_ref, out_ref, rows, tokens, result):
    rows[...] = got_ref[...].astype(f32)
    for j in range(PLACES):
        for c in range(C // LANES):
            tokens[j * FRAMES : (j + 1) * FRAMES, c * LANES : (c + 1) * LANES] = rows[
                pl.ds(j * 5 + c, FRAMES, stride=SENT), :
            ].astype(bf16)
    query = (dot(tokens[...], query_ref[...]) * QUERY_SCALE).astype(bf16)
    kv = dot(tokens[...], kv_weight_ref[...]).astype(bf16)
    span = 3 * FRAMES
    row_place = lax.broadcasted_iota(jnp.int32, (span, span), 0) // FRAMES
    column_place = lax.broadcasted_iota(jnp.int32, (span, span), 1) // FRAMES
    same = row_place == column_place
    for first in range(0, CELLS, span):
        gathered = []
        for h in range(HEADS):
            key_low, key_high = KEY_WINDOW[h]
            low, high = VALUE_WINDOW[h]
            scores = lax.dot_general(
                head_query(query[first : first + span], h),
                kv[first : first + span, key_low:key_high],
                (((1,), (1,)), ((), ())),
                preferred_element_type=f32,
            )
            weights = jnp.where(same, jnp.exp2(scores), 0.0).astype(bf16)
            values = jnp.where(
                inside_value(h), kv[first : first + span, low:high], jnp.ones((), bf16)
            )
            gathered.append(dot(weights, values))
        blocks = normalised(gathered)
        for b in range(3):
            result[first : first + span, b * LANES : (b + 1) * LANES] = blocks[b]
    for j in range(PLACES):
        cell = slice(j * FRAMES, (j + 1) * FRAMES)
        for b in range(2):
            rows[pl.ds(j * 2 + b, FRAMES, stride=BACK), :] = result[
                cell, (1 + b) * LANES : (2 + b) * LANES
            ]
    for pair in range((PLACES + 1) // 2):
        half = result[2 * pair * FRAMES : (2 * pair + 1) * FRAMES, 0:LANES]
        if 2 * pair + 1 < PLACES:
            other = result[(2 * pair + 1) * FRAMES : (2 * pair + 2) * FRAMES, 0:LANES]
            half = half + pltpu.roll(other, LANES // 2, 1)
        rows[pl.ds(2 * PLACES + pair, FRAMES, stride=BACK), :] = half
    rows[pl.ds(BACK - 1, FRAMES, stride=BACK), :] = jnp.zeros((FRAMES, LANES), f32)
    out_ref[...] = rows[0 : FRAMES * BACK, :].astype(bf16)


def final_kernel(got_ref, weight_ref, mixed_ref, out_ref, rows, attended):
    rows[...] = got_ref[...].astype(f32)
    upper = lane_iota(LANES) >= LANES // 2
    for j in range(PLACES):
        cell = slice(j * FRAMES, (j + 1) * FRAMES)
        for b in range(2):
            attended[cell, (1 + b) * LANES : (2 + b) * LANES] = rows[
                pl.ds(j * 2 + b, FRAMES, stride=BACK), :
            ].astype(bf16)
        half = rows[pl.ds(2 * PLACES + j // 2, FRAMES, stride=BACK), :]
        if j % 2:
            half = pltpu.roll(half, LANES // 2, 1)
        attended[cell, 0:LANES] = jnp.where(upper, half, 0.0).astype(bf16)
    update = dot(attended[...], weight_ref[...])
    out_ref[...] = (mixed_ref[...].astype(f32) + update).astype(bf16)


def struct(shape, dtype):
    return jax.ShapeDtypeStruct(shape, dtype)


def on_device(
    latent,
    reference_states,
    group_gain,
    conv_weight,
    norm_gain,
    spatial_query,
    spatial_key,
    spatial_value,
    spatial_out,
    frame_gain,
    temporal_query,
    temporal_key,
    temporal_value,
    temporal_out,
):
    x = latent.reshape(CELLS, C)
    strip_at = lax.axis_index("space")
    flags = jnp.stack([strip_at > 0, strip_at < 3]).astype(f32).reshape(1, 2)

    def swap(value, k):
        return lax.ppermute(value, "space", [(i, i ^ k) for i in range(4)])

    pad_query = lambda w: jnp.pad(w, ((0, 0), (0, 64)))
    pad_out = lambda w: jnp.pad(w, ((64, 0), (0, 0)))
    spatial_kv = jnp.concatenate([spatial_key, spatial_value], axis=1)
    temporal_kv = jnp.concatenate([temporal_key, temporal_value], axis=1)

    sums, top, bottom = call(
        stats_kernel,
        [struct((8, C), f32), struct((W, C), bf16), struct((W, C), bf16)],
        [x],
    )
    others = [swap(sums, k) for k in (2, 3, 1)]
    above = lax.ppermute(bottom, "space", [(0, 1), (1, 2), (2, 3)])
    below = lax.ppermute(top, "space", [(1, 0), (2, 1), (3, 2)])

    ref_kv = call(
        reference_kernel,
        struct((CELLS, C), bf16),
        [reference_states.reshape(CELLS, C), spatial_kv],
        flops=2 * CELLS * C * C,
    )
    ref_far = swap(ref_kv, 2)
    ref_near = swap(ref_kv, 1)
    ref_far_near = swap(ref_far, 1)

    hidden, query, kv = call(
        conv_kernel,
        [struct((CELLS, C), bf16), struct((CELLS, 384), bf16), struct((CELLS, C), bf16)],
        [
            flags,
            sums,
            *others,
            x,
            above,
            below,
            group_gain.reshape(1, C),
            conv_weight.reshape(3, 3 * C, C),
            norm_gain.reshape(1, C),
            pad_query(spatial_query),
            spatial_kv,
        ],
        scratch=[pltpu.VMEM(((STRIP + 2) * W, 3 * C), bf16)],
        flops=2 * CELLS * C * C * 11,
        smem=1,
    )
    kv_far = swap(kv, 2)
    kv_near = swap(kv, 1)
    kv_far_near = swap(kv_far, 1)

    def attention(kv_parts, start):
        keys = sum(p.shape[0] for p in kv_parts)
        return call(
            functools.partial(attention_kernel, len(kv_parts), start is not None, CELLS),
            struct((CELLS, ACC_WIDTH), f32),
            [query, *kv_parts] + ([] if start is None else [start]),
            flops=2 * CELLS * keys * 512 * HEADS,
        )

    acc = attention([kv, kv_near], None)
    acc = attention([ref_kv, ref_near, ref_far, ref_far_near], acc)
    last = [kv_far, kv_far_near]
    mixed, sent = call(
        functools.partial(last_attention_kernel, len(last), CELLS),
        [struct((CELLS, C), bf16), struct((FRAMES * SENT, LANES), bf16)],
        [query, acc, hidden, pad_out(spatial_out), frame_gain.reshape(1, C), *last],
        scratch=[pltpu.VMEM((FRAMES * SENT, LANES), f32)],
        flops=2 * CELLS * 2 * CELLS * 512 * HEADS,
    )
    got = lax.all_to_all(
        sent.reshape(FRAMES, SENT, LANES), "frame", split_axis=0, concat_axis=0, tiled=True
    )
    back = call(
        temporal_kernel,
        struct((FRAMES * BACK, LANES), bf16),
        [got.reshape(FRAMES * SENT, LANES), pad_query(temporal_query), temporal_kv],
        scratch=[
            pltpu.VMEM((FRAMES * SENT, LANES), f32),
            pltpu.VMEM((CELLS, C), bf16),
            pltpu.VMEM((CELLS, 384), f32),
        ],
        flops=2 * CELLS * C * 960,
    )
    returned = lax.all_to_all(
        back.reshape(FRAMES, BACK, LANES), "frame", split_axis=0, concat_axis=0, tiled=True
    )
    output = call(
        final_kernel,
        struct((CELLS, C), bf16),
        [returned.reshape(FRAMES * BACK, LANES), pad_out(temporal_out), mixed],
        scratch=[
            pltpu.VMEM((FRAMES * BACK, LANES), f32),
            pltpu.VMEM((CELLS, 384), bf16),
        ],
        flops=2 * CELLS * C * 384,
    )
    return output.reshape(latent.shape)


def solution(mesh):
    return jax.shard_map(
        on_device,
        mesh=mesh,
        in_specs=(P("frame", "space", None, None), P("space", None, None)) + (P(),) * 12,
        out_specs=P("frame", "space", None, None),
        check_vma=False,
    )
```

profile of v0, /device:TPU:2, one launch (start us, length us, event | category | flops | bytes accessed | tf_op | source)
XLA Modules:
  0.0 137.7 jit_solution(12281398118015450784)
XLA Ops:
  0.0 1.1 copy-done.1
  1.1 0.5 shard_map.136
  1.6 2.2 %collective-permute-start = (f32[8,640]{1,0:T(8,128)S(1)}, f32[8,640]{1,0:T(8,128)S(1)}, u32[]{:S(2)}, u32[]{:S(2)}) collective-permute-start(f32[8,640]{1,0:T(8,128)S(1)} %get-tuple-element.13.s0_ref), channel_id=1, source_target_pairs={{0,2},{1,3},{2,0},{3,1},{4,6},{5,7},{6,4},{7,5},{8,10},{9,11},{10,... | collective-permute-start | bytes 61448 | tf_op jit(solution)/shard_map/ppermute | solution.py:334
  3.8 0.6 collective-permute-start.1
  4.4 1.0 collective-permute-start.2
  5.4 1.9 %collective-permute-start.3 = (bf16[48,640]{1,0:T(8,128)(2,1)S(1)}, bf16[48,640]{1,0:T(8,128)(2,1)S(1)}, u32[]{:S(2)}, u32[]{:S(2)}) collective-permute-start(bf16[48,640]{1,0:T(8,128)(2,1)S(1)} %get-tuple-element.14), channel_id=1, source_target_pairs={{0,1},{1,2},{2,3},{4,5},{5,6},{6,7},{8,9},{9,10},{10,11},{12,13},{... | collective-permute-start | bytes 184328 | tf_op jit(solution)/shard_map/ppermute | solution.py:347
  7.3 1.3 collective-permute-start.4
  8.6 0.0 copy-start
  8.6 1.3 copy.16
  9.9 0.0 copy-done.5
  9.9 0.3 copy.17
  10.2 0.3 pad_maximum_fusion.kv_ref.weight_ref
  10.5 0.0 copy-start.10
  10.5 0.0 copy-start.11
  10.5 0.1 add_convert_fusion.flags_ref
  10.6 0.0 copy-done
  10.6 1.1 shard_map.138.refs_1_
  11.7 1.3 copy.15
  13.0 0.0 copy-done.10
  13.0 0.0 copy-done.11
  13.0 0.1 pad.14.query_ref
  13.1 0.0 collective-permute-done.s1_ref
  13.1 6.1 %collective-permute-start.6 = (bf16[576,640]{1,0:T(8,128)(2,1)S(1)}, bf16[576,640]{1,0:T(8,128)(2,1)S(1)}, u32[]{:S(2)}, u32[]{:S(2)}) collective-permute-start(bf16[576,640]{1,0:T(8,128)(2,1)S(1)} %shard_map.138.refs_1_), channel_id=1, source_target_pairs={{0,2},{1,3},{2,0},{3,1},{4,6},{5,7},{6,4},{7,5},{8,10},{9,11},{10,... | collective-permute-start | bytes 2211848 | tf_op jit(solution)/shard_map/ppermute | solution.py:334
  19.2 0.0 collective-permute-done.1.s2_ref
  19.2 0.0 collective-permute-done.2.s3_ref
  19.2 0.0 collective-permute-done.3.above_ref
  19.2 0.0 collective-permute-done.4.below_ref
  19.2 0.0 copy-done.2
  19.2 0.0 copy-start.9
  19.2 0.0 copy-start.12
  19.2 11.4 %shard_map.137 = (bf16[576,640]{1,0:T(8,128)(2,1)S(1)}, bf16[576,384]{1,0:T(8,128)(2,1)S(1)}, bf16[576,640]{1,0:T(8,128)(2,1)S(1)}) custom-call(f32[1,2]{1,0:T(1,128)S(1)} %add_convert_fusion.flags_ref, f32[8,640]{1,0:T(8,128)S(1)} %get-tuple-element.13.s0_ref, f32[8,640]{1,0:T(8,128)S(1)} %collective-permute-done.s1_ref, ...), custom_call_target="tpu_custom_call" | custom-call | flops 5190451200 | bytes 1048576 | tf_op jit(solution)/shard_map/pallas_call | solution.py:59
  30.6 0.1 collective-permute-start.9
  30.7 0.3 collective-permute-start.8
  31.0 0.5 collective-permute-start.5
  31.5 4.9 %collective-permute-done.6.refs_3_ = bf16[576,640]{1,0:T(8,128)(2,1)S(1)} collective-permute-done((bf16[576,640]{1,0:T(8,128)(2,1)S(1)}, bf16[576,640]{1,0:T(8,128)(2,1)S(1)}, u32[]{:S(2)}, u32[]{:S(2)}) %collective-permute-start.6) | collective-permute-done | bytes 737312 | tf_op jit(solution)/shard_map/ppermute | solution.py:334
  36.5 0.0 collective-permute-start.7
  36.5 0.0 copy-done.9
  36.5 0.0 copy-done.12
  36.5 15.2 %collective-permute-done.9.refs_0_ = bf16[576,640]{1,0:T(8,128)(2,1)S(1)} collective-permute-done((bf16[576,640]{1,0:T(8,128)(2,1)S(1)}, bf16[576,640]{1,0:T(8,128)(2,1)S(1)}, u32[]{:S(2)}, u32[]{:S(2)}) %collective-permute-start.9) | collective-permute-done | bytes 737312 | tf_op jit(solution)/shard_map/ppermute | solution.py:334
  51.7 0.0 collective-permute-start.10
  51.8 0.0 collective-permute-done.8.refs_2_
  51.8 3.7 %shard_map.139.refs_5_ = f32[576,768]{1,0:T(8,128)S(1)} custom-call(bf16[576,384]{1,0:T(8,128)(2,1)S(1)} %get-tuple-element.16.refs_0_.query_ref, bf16[576,640]{1,0:T(8,128)(2,1)S(1)} %get-tuple-element.17.refs_1_, bf16[576,640]{1,0:T(8,128)(2,1)S(1)} %collective-permute-done.8.refs_2_), custom_call_target="tpu_custom_call" | custom-call | flops 2717908992 | bytes 1048576 | tf_op jit(solution)/shard_map/pallas_call | solution.py:59
  55.4 0.0 copy-start.4
  55.4 1.2 copy-done.4
  56.7 0.0 collective-permute-done.5.refs_2_
  56.7 0.0 collective-permute-done.7.refs_4_
  56.7 8.7 %shard_map.140.acc_ref = f32[576,768]{1,0:T(8,128)S(1)} custom-call(bf16[576,384]{1,0:T(8,128)(2,1)S(1)} %get-tuple-element.16.refs_0_.query_ref, bf16[576,640]{1,0:T(8,128)(2,1)S(1)} %shard_map.138.refs_1_, bf16[576,640]{1,0:T(8,128)(2,1)S(1)} %collective-permute-done.5.refs_2_, bf16[576,640]{1,0:T(8,128)(2,1)S(1)} %collective-permute-done.6.refs_3_, ...), custom_call_target="tpu_custom_call" | custom-call | flops 5435817984 | bytes 1048576 | tf_op jit(solution)/shard_map/pallas_call | solution.py:59
  65.4 0.0 copy-start.3
  65.4 1.2 copy-done.3
  66.6 0.0 collective-permute-done.10.refs_1_
  66.6 7.7 %shard_map.141 = (bf16[576,640]{1,0:T(8,128)(2,1)S(1)}, bf16[3072,128]{1,0:T(8,128)(2,1)}) custom-call(bf16[576,384]{1,0:T(8,128)(2,1)S(1)} %get-tuple-element.16.refs_0_.query_ref, f32[576,768]{1,0:T(8,128)} %copy-done.3, bf16[576,640]{1,0:T(8,128)(2,1)S(1)} %get-tuple-element.18.hidden_ref, bf16[384,640]{1,0:T(8,128)(2,1)S(1)} %pad.15.weight_ref, ...), custom_call_target="tpu_custom_call" | custom-call | flops 2717908992 | bytes 1048576 | tf_op jit(solution)/shard_map/pallas_call | solution.py:59
  74.2 13.3 %all-to-all-start = ((bf16[64,48,128]{2,1,0:T(8,128)(2,1)}), bf16[64,48,128]{2,1,0:T(8,128)(2,1)S(1)}, u32[]{:S(2)}, u32[]{:S(2)}) async-start(bf16[64,48,128]{2,1,0:T(8,128)(2,1)} %bitcast.5), calls=%async_computation | async-start | bytes 1572864 | tf_op jit(solution)/shard_map/all_to_all | solution.py:403
  87.6 0.0 copy-done.6
  87.6 0.3 copy.19
  87.9 1.0 copy.20
  88.9 0.3 copy.18
  89.2 0.1 pad.16.query_ref
  89.2 1.3 pad_maximum_fusion.1.kv_weight_ref
  90.5 21.8 %all-to-all-done = bf16[64,48,128]{2,1,0:T(8,128)(2,1)S(1)} async-done(((bf16[64,48,128]{2,1,0:T(8,128)(2,1)}), bf16[64,48,128]{2,1,0:T(8,128)(2,1)S(1)}, u32[]{:S(2)}, u32[]{:S(2)}) %all-to-all-start) | async-done | bytes 786464 | tf_op jit(solution)/shard_map/all_to_all | solution.py:403
  112.3 3.2 %shard_map.142 = bf16[1536,128]{1,0:T(8,128)(2,1)} custom-call(bf16[3072,128]{1,0:T(8,128)(2,1)S(1)} %bitcast.11, bf16[640,384]{1,0:T(8,128)(2,1)S(1)} %pad.16.query_ref, bf16[640,640]{1,0:T(8,128)(2,1)S(1)} %pad_maximum_fusion.1.kv_weight_ref), custom_call_target="tpu_custom_call" | custom-call | flops 707788800 | bytes 1048576 | tf_op jit(solution)/shard_map/pallas_call | solution.py:59
  115.5 5.3 %all-to-all-start.1 = ((bf16[64,24,128]{2,1,0:T(8,128)(2,1)}), bf16[64,24,128]{2,1,0:T(8,128)(2,1)S(1)}, u32[]{:S(2)}, u32[]{:S(2)}) async-start(bf16[64,24,128]{2,1,0:T(8,128)(2,1)} %bitcast.7), calls=%async_computation.1 | async-start | bytes 786432 | tf_op jit(solution)/shard_map/all_to_all | solution.py:417
  120.8 1.0 pad.17.weight_ref
  121.9 14.3 %all-to-all-done.1 = bf16[64,24,128]{2,1,0:T(8,128)(2,1)S(1)} async-done(((bf16[64,24,128]{2,1,0:T(8,128)(2,1)}), bf16[64,24,128]{2,1,0:T(8,128)(2,1)S(1)}, u32[]{:S(2)}, u32[]{:S(2)}) %all-to-all-start.1) | async-done | bytes 393248 | tf_op jit(solution)/shard_map/all_to_all | solution.py:417
  136.2 1.5 %shard_map.143 = bf16[576,640]{1,0:T(8,128)(2,1)} custom-call(bf16[1536,128]{1,0:T(8,128)(2,1)S(1)} %bitcast.10, bf16[384,640]{1,0:T(8,128)(2,1)S(1)} %pad.17.weight_ref, bf16[576,640]{1,0:T(8,128)(2,1)S(1)} %get-tuple-element.20.mixed_ref), custom_call_target="tpu_custom_call" | custom-call | flops 283115520 | bytes 1048576 | tf_op jit(solution)/shard_map/pallas_call | solution.py:59
  (12 shorter events, 0.1 us)
Async XLA Ops:
  0.0 1.1 copy-start.1
  1.1 8.8 %copy-start.5 = (bf16[640,320]{0,1:T(8,128)(2,1)S(1)}, bf16[640,320]{0,1:T(8,128)(2,1)}, u32[]{:S(2)}) copy-start(bf16[640,320]{0,1:T(8,128)(2,1)} %param.21) | copy-start | bytes 1228804
  1.6 11.4 %collective-permute-start = (f32[8,640]{1,0:T(8,128)S(1)}, f32[8,640]{1,0:T(8,128)S(1)}, u32[]{:S(2)}, u32[]{:S(2)}) collective-permute-start(f32[8,640]{1,0:T(8,128)S(1)} %get-tuple-element.13.s0_ref), channel_id=1, source_target_pairs={{0,2},{1,3},{2,0},{3,1},{4,6},{5,7},{6,4},{7,5},{8,10},{9,11},{10,... | collective-permute-start | bytes 61448 | tf_op jit(solution)/shard_map/ppermute | solution.py:334
  3.8 15.3 %collective-permute-start.1 = (f32[8,640]{1,0:T(8,128)S(1)}, f32[8,640]{1,0:T(8,128)S(1)}, u32[]{:S(2)}, u32[]{:S(2)}) collective-permute-start(f32[8,640]{1,0:T(8,128)S(1)} %get-tuple-element.13.s0_ref), channel_id=1, source_target_pairs={{0,3},{1,2},{2,1},{3,0},{4,7},{5,6},{6,5},{7,4},{8,11},{9,10},{10,... | collective-permute-start | bytes 61448 | tf_op jit(solution)/shard_map/ppermute | solution.py:334
  4.4 14.8 %collective-permute-start.2 = (f32[8,640]{1,0:T(8,128)S(1)}, f32[8,640]{1,0:T(8,128)S(1)}, u32[]{:S(2)}, u32[]{:S(2)}) collective-permute-start(f32[8,640]{1,0:T(8,128)S(1)} %get-tuple-element.13.s0_ref), channel_id=1, source_target_pairs={{0,1},{1,0},{2,3},{3,2},{4,5},{5,4},{6,7},{7,6},{8,9},{9,8},{10,11... | collective-permute-start | bytes 61448 | tf_op jit(solution)/shard_map/ppermute | solution.py:334
  5.4 13.8 %collective-permute-start.3 = (bf16[48,640]{1,0:T(8,128)(2,1)S(1)}, bf16[48,640]{1,0:T(8,128)(2,1)S(1)}, u32[]{:S(2)}, u32[]{:S(2)}) collective-permute-start(bf16[48,640]{1,0:T(8,128)(2,1)S(1)} %get-tuple-element.14), channel_id=1, source_target_pairs={{0,1},{1,2},{2,3},{4,5},{5,6},{6,7},{8,9},{9,10},{10,11},{12,13},{... | collective-permute-start | bytes 184328 | tf_op jit(solution)/shard_map/ppermute | solution.py:347
  7.3 11.9 %collective-permute-start.4 = (bf16[48,640]{1,0:T(8,128)(2,1)S(1)}, bf16[48,640]{1,0:T(8,128)(2,1)S(1)}, u32[]{:S(2)}, u32[]{:S(2)}) collective-permute-start(bf16[48,640]{1,0:T(8,128)(2,1)S(1)} %get-tuple-element.15), channel_id=1, source_target_pairs={{1,0},{2,1},{3,2},{5,4},{6,5},{7,6},{9,8},{10,9},{11,10},{13,12},{... | collective-permute-start | bytes 184328 | tf_op jit(solution)/shard_map/ppermute | solution.py:348
  8.6 2.0 %copy-start = (bf16[12,48,640]{2,1,0:T(8,128)(2,1)S(1)}, bf16[12,48,640]{2,1,0:T(8,128)(2,1)}, u32[]{:S(2)}) copy-start(bf16[12,48,640]{2,1,0:T(8,128)(2,1)} %param.15) | copy-start | bytes 2211844
  10.5 2.5 %copy-start.10 = (f32[640]{0:T(1024)S(1)}, f32[640]{0:T(1024)}, u32[]{:S(2)}) copy-start(f32[640]{0:T(1024)} %param.16) | copy-start | bytes 7684
  10.5 2.5 %copy-start.11 = (f32[640]{0:T(1024)S(1)}, f32[640]{0:T(1024)}, u32[]{:S(2)}) copy-start(f32[640]{0:T(1024)} %param.18) | copy-start | bytes 7684
  10.6 8.6 %copy-start.2 = (bf16[1,12,48,640]{3,2,1,0:T(8,128)(2,1)S(1)}, bf16[1,12,48,640]{3,2,1,0:T(8,128)(2,1)}, u32[]{:S(2)}) copy-start(bf16[1,12,48,640]{3,2,1,0:T(8,128)(2,1)} %param.14) | copy-start | bytes 2211844
  13.1 23.4 %collective-permute-start.6 = (bf16[576,640]{1,0:T(8,128)(2,1)S(1)}, bf16[576,640]{1,0:T(8,128)(2,1)S(1)}, u32[]{:S(2)}, u32[]{:S(2)}) collective-permute-start(bf16[576,640]{1,0:T(8,128)(2,1)S(1)} %shard_map.138.refs_1_), channel_id=1, source_target_pairs={{0,2},{1,3},{2,0},{3,1},{4,6},{5,7},{6,4},{7,5},{8,10},{9,11},{10,... | collective-permute-start | bytes 2211848 | tf_op jit(solution)/shard_map/ppermute | solution.py:334
  19.2 17.3 %copy-start.9 = (bf16[320,640]{1,0:T(8,128)(2,1)S(1)}, bf16[320,640]{1,0:T(8,128)(2,1)}, u32[]{:S(2)}) copy-start(bf16[320,640]{1,0:T(8,128)(2,1)} %param.22) | copy-start | bytes 1228804
  19.2 17.3 %copy-start.12 = (f32[640]{0:T(1024)S(1)}, f32[640]{0:T(1024)}, u32[]{:S(2)}) copy-start(f32[640]{0:T(1024)} %param.23) | copy-start | bytes 7684
  30.6 21.1 %collective-permute-start.9 = (bf16[576,640]{1,0:T(8,128)(2,1)S(1)}, bf16[576,640]{1,0:T(8,128)(2,1)S(1)}, u32[]{:S(2)}, u32[]{:S(2)}) collective-permute-start(bf16[576,640]{1,0:T(8,128)(2,1)S(1)} %get-tuple-element.17.refs_1_), channel_id=1, source_target_pairs={{0,2},{1,3},{2,0},{3,1},{4,6},{5,7},{6,4},{7,5},{8,10},{9,11},{10,... | collective-permute-start | bytes 2211848 | tf_op jit(solution)/shard_map/ppermute | solution.py:334
  30.7 21.0 %collective-permute-start.8 = (bf16[576,640]{1,0:T(8,128)(2,1)S(1)}, bf16[576,640]{1,0:T(8,128)(2,1)S(1)}, u32[]{:S(2)}, u32[]{:S(2)}) collective-permute-start(bf16[576,640]{1,0:T(8,128)(2,1)S(1)} %get-tuple-element.17.refs_1_), channel_id=1, source_target_pairs={{0,1},{1,0},{2,3},{3,2},{4,5},{5,4},{6,7},{7,6},{8,9},{9,8},{10,11... | collective-permute-start | bytes 2211848 | tf_op jit(solution)/shard_map/ppermute | solution.py:334
  31.0 25.6 %collective-permute-start.5 = (bf16[576,640]{1,0:T(8,128)(2,1)S(1)}, bf16[576,640]{1,0:T(8,128)(2,1)S(1)}, u32[]{:S(2)}, u32[]{:S(2)}) collective-permute-start(bf16[576,640]{1,0:T(8,128)(2,1)S(1)} %shard_map.138.refs_1_), channel_id=1, source_target_pairs={{0,1},{1,0},{2,3},{3,2},{4,5},{5,4},{6,7},{7,6},{8,9},{9,8},{10,11... | collective-permute-start | bytes 2211848 | tf_op jit(solution)/shard_map/ppermute | solution.py:334
  36.5 20.2 %collective-permute-start.7 = (bf16[576,640]{1,0:T(8,128)(2,1)S(1)}, bf16[576,640]{1,0:T(8,128)(2,1)S(1)}, u32[]{:S(2)}, u32[]{:S(2)}) collective-permute-start(bf16[576,640]{1,0:T(8,128)(2,1)S(1)} %collective-permute-done.6.refs_3_), channel_id=1, source_target_pairs={{0,1},{1,0},{2,3},{3,2},{4,5},{5,4},{6,7},{7,6},{8,9},{9,8},{10,11... | collective-permute-start | bytes 2211848 | tf_op jit(solution)/shard_map/ppermute | solution.py:334
  51.7 14.8 %collective-permute-start.10 = (bf16[576,640]{1,0:T(8,128)(2,1)S(1)}, bf16[576,640]{1,0:T(8,128)(2,1)S(1)}, u32[]{:S(2)}, u32[]{:S(2)}) collective-permute-start(bf16[576,640]{1,0:T(8,128)(2,1)S(1)} %collective-permute-done.9.refs_0_), channel_id=1, source_target_pairs={{0,1},{1,0},{2,3},{3,2},{4,5},{5,4},{6,7},{7,6},{8,9},{9,8},{10,11... | collective-permute-start | bytes 2211848 | tf_op jit(solution)/shard_map/ppermute | solution.py:334
  55.4 1.2 copy-start.4
  65.4 1.2 copy-start.3
  74.2 13.4 %copy-start.6 = (bf16[640,320]{0,1:T(8,128)(2,1)S(1)}, bf16[640,320]{0,1:T(8,128)(2,1)}, u32[]{:S(2)}) copy-start(bf16[640,320]{0,1:T(8,128)(2,1)} %param.25) | copy-start | bytes 1228804
  74.2 13.6 %copy-start.7 = (bf16[640,320]{0,1:T(8,128)(2,1)S(1)}, bf16[640,320]{0,1:T(8,128)(2,1)}, u32[]{:S(2)}) copy-start(bf16[640,320]{0,1:T(8,128)(2,1)} %param.26) | copy-start | bytes 1228804
  74.2 14.6 %copy-start.8 = (bf16[640,320]{0,1:T(8,128)(2,1)S(1)}, bf16[640,320]{0,1:T(8,128)(2,1)}, u32[]{:S(2)}) copy-start(bf16[640,320]{0,1:T(8,128)(2,1)} %param.24) | copy-start | bytes 1228804
  74.2 38.0 %all-to-all-start = ((bf16[64,48,128]{2,1,0:T(8,128)(2,1)}), bf16[64,48,128]{2,1,0:T(8,128)(2,1)S(1)}, u32[]{:S(2)}, u32[]{:S(2)}) async-start(bf16[64,48,128]{2,1,0:T(8,128)(2,1)} %bitcast.5), calls=%async_computation | async-start | bytes 1572864 | tf_op jit(solution)/shard_map/all_to_all | solution.py:403
  115.5 20.7 %all-to-all-start.1 = ((bf16[64,24,128]{2,1,0:T(8,128)(2,1)}), bf16[64,24,128]{2,1,0:T(8,128)(2,1)S(1)}, u32[]{:S(2)}, u32[]{:S(2)}) async-start(bf16[64,24,128]{2,1,0:T(8,128)(2,1)} %bitcast.7), calls=%async_computation.1 | async-start | bytes 786432 | tf_op jit(solution)/shard_map/all_to_all | solution.py:417
where the time goes:
time: 138 us
  waiting for transfers between devices  56.3 us (41%)
  Pallas kernels  37.8 us (27%)
  starting transfers between devices  32.5 us (24%)
  local copies, waits for them, and re-layouts  9.21 us (7%)
  other arithmetic  1.64 us (1%)
    pallas_call x8, Pallas kernels, call(): pl.pallas_call(body, out_shape=outs, in_specs=specs, out_specs=vmem(1)[0]...  37.8 us
    all_to_all x1, waiting for transfers between devices, on_device(): lax.all_to_all(sent.reshape(FRAMES, SENT, LANES), 'frame', split_axis=0,...  21.8 us
    ppermute x9, waiting for transfers between devices, swap(): return lax.ppermute(value, 'space', [(i, i ^ k) for i in range(4)])  20.2 us
    all_to_all x1, waiting for transfers between devices, on_device(): lax.all_to_all(back.reshape(FRAMES, BACK, LANES), 'frame', split_axis=0,...  14.3 us
    all_to_all x1, starting transfers between devices, on_device(): lax.all_to_all(sent.reshape(FRAMES, SENT, LANES), 'frame', split_axis=0,...  13.3 us
    ppermute x9, starting transfers between devices, swap(): return lax.ppermute(value, 'space', [(i, i ^ k) for i in range(4)])  10.7 us
    unnamed x32, local copies, waits for them, and re-layouts  8 us
    all_to_all x1, starting transfers between devices, on_device(): lax.all_to_all(back.reshape(FRAMES, BACK, LANES), 'frame', split_axis=0,...  5.34 us
  transfers between devices with their start and end apart: 13, of which 4 were waited for; matrix products, arithmetic and copies ran while one was open for 5% of the time, Pallas kernels for 18%

commit v1 on v0

v1 whole, which is shorter than its diff:
```python
import functools

import jax
import jax.numpy as jnp
from jax import lax
from jax.experimental import pallas as pl
from jax.experimental.pallas import tpu as pltpu
from jax.sharding import PartitionSpec as P

HEADS = 4
HEAD_DIM = 80
GROUPS = 32
INNER = 320
C = 640
W = 48
STRIP = 12
CELLS = STRIP * W
FRAMES = 64
PLACES = CELLS // FRAMES
LANES = 128
SENT = 48
TILE = 768
HEAD = 512
CHUNKS = 4
BACK = 24

epsilon = 1e-05
QUERY_SCALE = HEAD_DIM**-0.5 * 1.4426950408889634

KEY_WINDOW = ((0, 128), (0, 256), (128, 256), (128, 384))
VALUE_WINDOW = ((256, 512), (384, 512), (384, 640), (512, 640))
ACC_AT = (0, 256, 384, 640)
ACC_WIDTH = 768

f32 = jnp.float32
bf16 = jnp.bfloat16


def lane_iota(width, start=0):
    return lax.broadcasted_iota(jnp.int32, (1, width), 1) + start


def layer_norm(values, factor):
    centre = jnp.mean(values, axis=-1, keepdims=True)
    shifted = values - centre
    spread = jnp.mean(shifted * shifted, axis=-1, keepdims=True)
    normed = shifted * lax.rsqrt(spread + epsilon)
    return normed if factor is None else normed * factor


def dot(a, b):
    return jnp.dot(a, b, preferred_element_type=f32)


def dot_t(a, b):
    return lax.dot_general(a, b, (((1,), (1,)), ((), ())), preferred_element_type=f32)


def vmem(count):
    return [pl.BlockSpec(memory_space=pltpu.VMEM)] * count


def call(body, outs, operands, scratch=(), smem=0, limit=8, anywhere=(), flops=0):
    single = not isinstance(outs, (list, tuple))
    specs = [pl.BlockSpec(memory_space=pltpu.SMEM)] * smem + vmem(len(operands) - smem)
    for i in anywhere:
        specs[i] = pl.BlockSpec(memory_space=pltpu.HBM)
    return pl.pallas_call(
        body,
        out_shape=outs,
        in_specs=specs,
        out_specs=vmem(1)[0] if single else vmem(len(outs)),
        scratch_shapes=list(scratch),
        compiler_params=pltpu.CompilerParams(vmem_limit_bytes=limit * 1024 * 1024),
        cost_estimate=pl.CostEstimate(flops=flops, bytes_accessed=0, transcendentals=0),
    )(*operands)


def pieces_of(value):
    high = value.astype(bf16).astype(f32)
    middle = (value - high).astype(bf16).astype(f32)
    return [high, middle, value - high - middle]


def stacked(rows, height):
    at = lax.broadcasted_iota(jnp.int32, (height, C), 0)
    result = jnp.zeros((height, C), f32)
    for i, row in enumerate(rows):
        result = jnp.where(at == i, row, result)
    return result


def sums_of(pieces):
    return pieces[0:1] + pieces[1:2] + pieces[2:3], pieces[3:4] + pieces[4:5] + pieces[5:6]


def stats_kernel(flags_ref, x_ref, sums_ref, near_ref, far_ref):
    total = jnp.zeros((1, C), f32)
    square = jnp.zeros((1, C), f32)
    for r in range(STRIP):
        v = x_ref[r * W : (r + 1) * W, :].astype(f32)
        total = total + jnp.sum(v, axis=0, keepdims=True)
        square = square + jnp.sum(v * v, axis=0, keepdims=True)
    per = C // GROUPS
    column_group = jnp.floor((lane_iota(C).astype(f32) + 0.5) * (1.0 / per))
    row_at = lax.broadcasted_iota(jnp.int32, (C, 1), 0).astype(f32)
    row_group = jnp.floor((row_at + 0.5) * (1.0 / per))
    same = jnp.where(row_group == column_group, 1.0, 0.0).astype(bf16)
    grouped = dot(stacked(pieces_of(total) + pieces_of(square), 16).astype(bf16), same)
    group_sum, group_sq = sums_of(grouped)
    sums_ref[...] = stacked([group_sum, group_sq], 8)
    near_ref[W:, :] = stacked(pieces_of(group_sum) + pieces_of(group_sq), 16).astype(bf16)
    odd = flags_ref[0, 2] > 0.5
    top = x_ref[0:W, :]
    bottom = x_ref[CELLS - W :, :]
    near_ref[0:W, :] = jnp.where(odd, top, bottom)
    far_ref[...] = jnp.where(odd, bottom, top)


def chip_sums_kernel(sums_ref, near_ref, edge_ref, sums_out, far_ref):
    group_sum, group_sq = sums_of(near_ref[W:, :].astype(f32))
    group_sum = group_sum + sums_ref[0:1]
    group_sq = group_sq + sums_ref[1:2]
    sums_out[...] = stacked([group_sum, group_sq], 8)
    far_ref[0:W, :] = edge_ref[...]
    far_ref[W:, :] = stacked(pieces_of(group_sum) + pieces_of(group_sq), 16).astype(bf16)


def reference_kv(weight, states):
    normed = layer_norm(states.astype(f32), None).astype(bf16)
    return dot_t(normed, weight[...]).astype(bf16)


def own_reference_kernel(
    flags_ref, states_ref, before_ref, key_ref, value_ref, out_ref, half_ref, weight
):
    half = CELLS // 2
    half_ref[...] = jnp.where(flags_ref[0, 3] > 0.5, states_ref[half:, :], states_ref[0:half, :])
    weight[0:INNER, :] = key_ref[...]
    weight[INNER:, :] = value_ref[...]
    out_ref[...] = reference_kv(weight, states_ref[...])


def far_reference_kernel(first_ref, second_ref, key_ref, value_ref, out_ref, *refs):
    chunk_refs, weight = refs[:CHUNKS], refs[CHUNKS]
    weight[0:INNER, :] = key_ref[...]
    weight[INNER:, :] = value_ref[...]
    half, size = CELLS // 2, CELLS // CHUNKS
    for i, ref in enumerate((first_ref, second_ref)):
        out = reference_kv(weight, ref[...])
        out_ref[i * half : (i + 1) * half, :] = out
        for j in range(half // size):
            chunk_refs[i * (half // size) + j][...] = out[j * size : (j + 1) * size]


def conv_kernel(
    flags_ref,
    sums_ref,
    x_ref,
    near_ref,
    far_ref,
    gain_ref,
    kernel_ref,
    norm_gain_ref,
    query_ref,
    key_ref,
    value_ref,
    hidden_out,
    query_out,
    kv_out,
    lhs,
    weight,
    taps,
    arrived,
):
    copies = [pltpu.make_async_copy(kernel_ref.at[a], taps.at[a], arrived.at[a]) for a in range(3)]
    for copy in copies:
        copy.start()
    weight[0:INNER, :] = key_ref[...]
    weight[INNER:, :] = value_ref[...]
    group_sum, group_sq = sums_of(far_ref[W:, :].astype(f32))
    members = float(4 * CELLS * (C // GROUPS))
    average = (group_sum + sums_ref[0:1]) / members
    variance = (group_sq + sums_ref[1:2]) / members - average * average
    factor = lax.rsqrt(variance + epsilon) * gain_ref[...]
    at = lax.broadcasted_iota(jnp.int32, (W, 1), 0)
    odd = flags_ref[0, 2] > 0.5

    def place(r, block, keep):
        v = (block.astype(f32) - average) * factor
        act = (0.5 * v) * (1.0 + jnp.tanh(0.5 * v))
        if keep is not None:
            act = jnp.where(keep > 0.5, act, 0.0)
        rows = slice(r * W, (r + 1) * W)
        lhs[rows, C : 2 * C] = act.astype(bf16)
        lhs[rows, 0:C] = jnp.where(at == 0, 0.0, pltpu.roll(act, 1, 0)).astype(bf16)
        lhs[rows, 2 * C :] = jnp.where(at == W - 1, 0.0, pltpu.roll(act, W - 1, 0)).astype(bf16)

    near, far = near_ref[0:W, :], far_ref[0:W, :]
    place(0, jnp.where(odd, near, far), flags_ref[0, 0])
    place(STRIP + 1, jnp.where(odd, far, near), flags_ref[0, 1])
    for r in range(STRIP):
        place(r + 1, x_ref[r * W : (r + 1) * W, :], None)
    for first in (0, CELLS // 2):
        rows = slice(first, first + CELLS // 2)
        total = None
        for a in range(3):
            if first == 0:
                copies[a].wait()
            part = dot(lhs[first + a * W : first + a * W + CELLS // 2, :], taps[a])
            total = part if total is None else total + part
        hidden_out[rows, :] = (x_ref[rows, :].astype(f32) + total).astype(bf16)
    normed = layer_norm(hidden_out[...].astype(f32), norm_gain_ref[...]).astype(bf16)
    kv_out[...] = dot_t(normed, weight[...]).astype(bf16)
    query_out[:, 0:INNER] = (dot_t(normed, query_ref[...]) * QUERY_SCALE).astype(bf16)
    query_out[:, INNER:] = jnp.zeros((CELLS, 64), bf16)


def head_query(query, h):
    low, high = KEY_WINDOW[h]
    lane = lane_iota(high - low, low)
    inside = (lane >= h * HEAD_DIM) & (lane < (h + 1) * HEAD_DIM)
    return jnp.where(inside, query[:, low:high], jnp.zeros((), bf16))


def inside_value(h):
    low, high = VALUE_WINDOW[h]
    lane = lane_iota(high - low, low)
    return (lane >= INNER + h * HEAD_DIM) & (lane < INNER + (h + 1) * HEAD_DIM)


def joined(kv_refs, ranges, scratch):
    at = 0
    for ref, (low, high) in zip(kv_refs, ranges):
        scratch[at : at + high - low, :] = ref[low:high, :]
        at += high - low
    return scratch


def attend(query, kv_ref, start):
    gathered = []
    keys = kv_ref.shape[0]
    for h in range(HEADS):
        key_low, key_high = KEY_WINDOW[h]
        low, high = VALUE_WINDOW[h]
        mine = head_query(query, h)
        inside = inside_value(h)
        acc = None if start is None else start(h)
        for first in range(0, keys, TILE):
            rows = slice(first, min(first + TILE, keys))
            weights = jnp.exp2(dot_t(mine, kv_ref[rows, key_low:key_high])).astype(bf16)
            values = jnp.where(inside, kv_ref[rows, low:high], jnp.ones((), bf16))
            part = dot(weights, values)
            acc = part if acc is None else acc + part
        gathered.append(acc)
    return gathered


def normalised(gathered):
    blocks = [None, None, None]
    for h in range(HEADS):
        low, high = VALUE_WINDOW[h]
        acc = gathered[h]
        spare = 0 if INNER + h * HEAD_DIM > low else high - low - 1
        result = acc * (1.0 / acc[:, spare : spare + 1])
        result = jnp.where(inside_value(h), result, 0.0)
        for b in range((high - low) // LANES):
            at = low // LANES + b - 2
            piece = result[:, b * LANES : (b + 1) * LANES]
            blocks[at] = piece if blocks[at] is None else blocks[at] + piece
    return blocks


def starting(acc_ref):
    return lambda h: acc_ref[:, ACC_AT[h] : ACC_AT[h] + VALUE_WINDOW[h][1] - VALUE_WINDOW[h][0]]


def attention_kernel(ranges, has_start, *refs):
    n_kv = len(ranges)
    query_ref = refs[0]
    start = starting(refs[1 + n_kv]) if has_start else None
    out_ref, scratch = refs[-2:]
    kv_ref = joined(refs[1 : 1 + n_kv], ranges, scratch)
    for h, acc in enumerate(attend(query_ref[...], kv_ref, start)):
        out_ref[:, ACC_AT[h] : ACC_AT[h] + acc.shape[1]] = acc


def last_attention_kernel(
    ranges,
    query_ref,
    acc_ref,
    first_ref,
    second_ref,
    hidden_ref,
    weight_ref,
    gain_ref,
    mixed_out,
    sent_out,
    rows,
    weight,
    scratch,
):
    kv_ref = joined((first_ref, second_ref), ranges, scratch)
    weight[0:64, :] = jnp.zeros((64, C), bf16)
    weight[64:, :] = weight_ref[...]
    blocks = normalised(attend(query_ref[...], kv_ref, starting(acc_ref)))
    update = None
    for b in range(3):
        part = dot(blocks[b].astype(bf16), weight[b * LANES : (b + 1) * LANES, :])
        update = part if update is None else update + part
    mixed = (hidden_ref[...].astype(f32) + update).astype(bf16)
    mixed_out[...] = mixed
    framed = layer_norm(mixed.astype(f32), gain_ref[...])
    for j in range(PLACES):
        for c in range(C // LANES):
            rows[pl.ds(j * 5 + c, FRAMES, stride=SENT + 1), :] = framed[
                j * FRAMES : (j + 1) * FRAMES, c * LANES : (c + 1) * LANES
            ]
    for r in range(PLACES * 5, SENT):
        rows[pl.ds(r, FRAMES, stride=SENT + 1), :] = jnp.zeros((FRAMES, LANES), f32)
    for g in range(FRAMES):
        sent_out[g * SENT : (g + 1) * SENT, :] = rows[
            g * (SENT + 1) : g * (SENT + 1) + SENT, :
        ].astype(bf16)


def temporal_kernel(
    got_ref, query_ref, key_ref, value_ref, out_ref, rows, tokens, result, weight
):
    weight[0:INNER, :] = key_ref[...]
    weight[INNER:, :] = value_ref[...]
    for g in range(FRAMES):
        rows[g * (SENT + 1) : g * (SENT + 1) + SENT, :] = got_ref[
            g * SENT : (g + 1) * SENT, :
        ].astype(f32)
    for j in range(PLACES):
        for c in range(C // LANES):
            tokens[j * FRAMES : (j + 1) * FRAMES, c * LANES : (c + 1) * LANES] = rows[
                pl.ds(j * 5 + c, FRAMES, stride=SENT + 1), :
            ].astype(bf16)
    query = (dot_t(tokens[...], query_ref[...]) * QUERY_SCALE).astype(bf16)
    query = jnp.concatenate([query, jnp.zeros((CELLS, 64), bf16)], axis=1)
    kv = dot_t(tokens[...], weight[...]).astype(bf16)
    span = 3 * FRAMES
    row_place = lax.broadcasted_iota(jnp.int32, (span, span), 0) // FRAMES
    column_place = lax.broadcasted_iota(jnp.int32, (span, span), 1) // FRAMES
    same = row_place == column_place
    for first in range(0, CELLS, span):
        gathered = []
        for h in range(HEADS):
            key_low, key_high = KEY_WINDOW[h]
            low, high = VALUE_WINDOW[h]
            scores = dot_t(
                head_query(query[first : first + span], h),
                kv[first : first + span, key_low:key_high],
            )
            weights = jnp.where(same, jnp.exp2(scores), 0.0).astype(bf16)
            values = jnp.where(
                inside_value(h), kv[first : first + span, low:high], jnp.ones((), bf16)
            )
            gathered.append(dot(weights, values))
        blocks = normalised(gathered)
        for b in range(3):
            result[first : first + span, b * LANES : (b + 1) * LANES] = blocks[b]
    for j in range(PLACES):
        cell = slice(j * FRAMES, (j + 1) * FRAMES)
        for b in range(2):
            rows[pl.ds(j * 2 + b, FRAMES, stride=BACK + 1), :] = result[
                cell, (1 + b) * LANES : (2 + b) * LANES
            ]
    for pair in range((PLACES + 1) // 2):
        half = result[2 * pair * FRAMES : (2 * pair + 1) * FRAMES, 0:LANES]
        if 2 * pair + 1 < PLACES:
            other = result[(2 * pair + 1) * FRAMES : (2 * pair + 2) * FRAMES, 0:LANES]
            half = half + pltpu.roll(other, LANES // 2, 1)
        rows[pl.ds(2 * PLACES + pair, FRAMES, stride=BACK + 1), :] = half
    rows[pl.ds(BACK - 1, FRAMES, stride=BACK + 1), :] = jnp.zeros((FRAMES, LANES), f32)
    for g in range(FRAMES):
        out_ref[g * BACK : (g + 1) * BACK, :] = rows[
            g * (BACK + 1) : g * (BACK + 1) + BACK, :
        ].astype(bf16)


def final_kernel(got_ref, weight_ref, mixed_ref, out_ref, rows, attended, weight):
    weight[0:64, :] = jnp.zeros((64, C), bf16)
    weight[64:, :] = weight_ref[...]
    for g in range(FRAMES):
        rows[g * (BACK + 1) : g * (BACK + 1) + BACK, :] = got_ref[
            g * BACK : (g + 1) * BACK, :
        ].astype(f32)
    upper = lane_iota(LANES) >= LANES // 2
    for j in range(PLACES):
        cell = slice(j * FRAMES, (j + 1) * FRAMES)
        for b in range(2):
            attended[cell, (1 + b) * LANES : (2 + b) * LANES] = rows[
                pl.ds(j * 2 + b, FRAMES, stride=BACK + 1), :
            ].astype(bf16)
        half = rows[pl.ds(2 * PLACES + j // 2, FRAMES, stride=BACK + 1), :]
        if j % 2:
            half = pltpu.roll(half, LANES // 2, 1)
        attended[cell, 0:LANES] = jnp.where(upper, half, 0.0).astype(bf16)
    update = dot(attended[...], weight[...])
    out_ref[...] = (mixed_ref[...].astype(f32) + update).astype(bf16)


def order_kernel(value_ref, before_ref, out_ref):
    pass


def after(value, before):
    return pl.pallas_call(
        order_kernel,
        out_shape=struct(value.shape, value.dtype),
        in_specs=[pl.BlockSpec(memory_space=pl.ANY)] * 2,
        out_specs=pl.BlockSpec(memory_space=pl.ANY),
        input_output_aliases={0: 0},
        compiler_params=pltpu.CompilerParams(vmem_limit_bytes=1 << 20),
        cost_estimate=pl.CostEstimate(flops=0, bytes_accessed=0, transcendentals=0),
    )(value, before)


def struct(shape, dtype):
    return jax.ShapeDtypeStruct(shape, dtype)


def on_device(
    latent,
    reference_states,
    group_gain,
    conv_weight,
    norm_gain,
    spatial_query,
    spatial_key,
    spatial_value,
    spatial_out,
    frame_gain,
    temporal_query,
    temporal_key,
    temporal_value,
    temporal_out,
):
    x = latent.reshape(CELLS, C)
    strip_at = lax.axis_index("space")
    odd_row = lax.axis_index("frame") // 8 % 2 == 1
    flags = (
        jnp.stack([strip_at > 0, strip_at < 3, strip_at % 2 == 1, odd_row])
        .astype(f32)
        .reshape(1, 4)
    )

    def swap(value, k):
        return lax.ppermute(value, "space", [(i, i ^ k) for i in range(4)])

    states = reference_states.reshape(CELLS, C)
    sums, near, edge = call(
        stats_kernel,
        [struct((8, C), f32), struct((W + 16, C), bf16), struct((W, C), bf16)],
        [flags, x],
        smem=1,
    )
    near = swap(near, 1)
    sums, far = call(
        chip_sums_kernel,
        [struct((8, C), f32), struct((W + 16, C), bf16)],
        [sums, near, edge],
    )
    far = swap(far, 3)

    ref_kv, half = call(
        own_reference_kernel,
        [struct((CELLS, C), bf16), struct((CELLS // 2, C), bf16)],
        [flags, states, sums, spatial_key.T, spatial_value.T],
        scratch=[pltpu.VMEM((C, C), bf16)],
        smem=1,
        flops=2*10**9,
    )
    half = swap(half, 2)

    hidden, query, kv = call(
        conv_kernel,
        [
            struct((CELLS, C), bf16),
            struct((CELLS, 384), bf16),
            struct((CELLS, C), bf16),
        ],
        [
            flags,
            sums,
            x,
            near,
            far,
            group_gain.reshape(1, C),
            conv_weight.reshape(3, 3 * C, C),
            norm_gain.reshape(1, C),
            spatial_query.T,
            spatial_key.T,
            spatial_value.T,
        ],
        scratch=[
            pltpu.VMEM(((STRIP + 2) * W, 3 * C), bf16),
            pltpu.VMEM((C, C), bf16),
            pltpu.VMEM((3, 3 * C, C), bf16),
            pltpu.SemaphoreType.DMA((3,)),
        ],
        smem=1,
        limit=46,
        anywhere=(6,),
    )
    ref_kv = after(ref_kv, query)
    ref_near = swap(ref_kv, 1)
    half = after(half, query)
    other_half = lax.ppermute(half, "frame", [(f, f ^ 8) for f in range(FRAMES)])
    kv_far = swap(kv, 2)
    kv_near = swap(kv, 1)

    def attention(kv_parts, start):
        ranges = [(low, high) for _, low, high in kv_parts]
        keys = sum(high - low for low, high in ranges)
        return call(
            functools.partial(attention_kernel, ranges, start is not None),
            struct((CELLS, ACC_WIDTH), f32),
            [query, *(part for part, _, _ in kv_parts)] + ([] if start is None else [start]),
            scratch=[pltpu.VMEM((keys, C), bf16)],
            limit=16,
        )

    acc = attention([(part, 0, CELLS) for part in (kv, kv_near, ref_kv, ref_near)], None)
    ref_far, *chunks = call(
        far_reference_kernel,
        [struct((CELLS, C), bf16)] + [struct((CELLS // CHUNKS, C), bf16)] * CHUNKS,
        [half, after(other_half, acc), spatial_key.T, spatial_value.T],
        scratch=[pltpu.VMEM((C, C), bf16)],
    )
    chunks = [swap(chunk, 1) for chunk in chunks]
    acc = attention([(ref_far, 0, HEAD)], acc)
    acc = attention(
        [(ref_far, HEAD, CELLS)] + [(chunk, 0, CELLS // CHUNKS) for chunk in chunks], acc
    )
    kv_far = after(kv_far, acc)
    kv_far_near = swap(kv_far, 1)
    acc = attention([(kv_far, 0, HEAD)], acc)
    ranges = [(HEAD, CELLS), (0, CELLS)]
    mixed, sent = call(
        functools.partial(last_attention_kernel, ranges),
        [struct((CELLS, C), bf16), struct((FRAMES * SENT, LANES), bf16)],
        [query, acc, kv_far, kv_far_near, hidden, spatial_out, frame_gain.reshape(1, C)],
        scratch=[
            pltpu.VMEM((FRAMES * (SENT + 1), LANES), f32),
            pltpu.VMEM((384, C), bf16),
            pltpu.VMEM((2 * CELLS - HEAD, C), bf16),
        ],
        limit=16,
    )
    got = lax.all_to_all(
        sent.reshape(FRAMES, SENT, LANES), "frame", split_axis=0, concat_axis=0, tiled=True
    )
    back = call(
        temporal_kernel,
        struct((FRAMES * BACK, LANES), bf16),
        [
            got.reshape(FRAMES * SENT, LANES),
            temporal_query.T,
            temporal_key.T,
            temporal_value.T,
        ],
        scratch=[
            pltpu.VMEM((FRAMES * (SENT + 1), LANES), f32),
            pltpu.VMEM((CELLS, C), bf16),
            pltpu.VMEM((CELLS, 384), f32),
            pltpu.VMEM((C, C), bf16),
        ],
    )
    returned = lax.all_to_all(
        back.reshape(FRAMES, BACK, LANES), "frame", split_axis=0, concat_axis=0, tiled=True
    )
    output = call(
        final_kernel,
        struct((CELLS, C), bf16),
        [returned.reshape(FRAMES * BACK, LANES), temporal_out, mixed],
        scratch=[
            pltpu.VMEM((FRAMES * (BACK + 1), LANES), f32),
            pltpu.VMEM((CELLS, 384), bf16),
            pltpu.VMEM((384, C), bf16),
        ],
    )
    return output.reshape(latent.shape)


def solution(mesh):
    return jax.shard_map(
        on_device,
        mesh=mesh,
        in_specs=(P("frame", "space", None, None), P("space", None, None)) + (P(),) * 12,
        out_specs=P("frame", "space", None, None),
        check_vma=False,
    )
```

time: 138 us -> 111 us (0.80)
  blocking collectives: 0 us -> 57.9 us
  waiting for transfers between devices: 56.3 us -> 4.89 us
  starting transfers between devices: 32.5 us -> 9.28 us
  Pallas kernels: 37.8 us -> 32.6 us
  local copies, waits for them, and re-layouts: 9.21 us -> 5.67 us
  other arithmetic: 1.64 us -> 0.08 us
    all_to_all x0 -> x2, blocking collectives: none -> 57.9 us  [the longest x1 37.6 us: on_device(): lax.all_to_all(sent.reshape(FRAMES, SENT, LANES), 'frame', split_axis=0,...]
    all_to_all x2 -> x0, waiting for transfers between devices: 36.1 us -> none  [the longest x1 21.8 us: on_device(): lax.all_to_all(sent.reshape(FRAMES, SENT, LANES), 'frame', split_axis=0,...]
    all_to_all x2 -> x0, starting transfers between devices: 18.7 us -> none  [the longest x1 13.3 us: on_device(): lax.all_to_all(sent.reshape(FRAMES, SENT, LANES), 'frame', split_axis=0,...]
    ppermute x9 -> x11, waiting for transfers between devices: 20.2 us -> 2.6 us  [swap(): return lax.ppermute(value, 'space', [(i, i ^ k) for i in range(4)])]
    pallas_call x8 -> x12, Pallas kernels: 37.8 us -> 32.6 us  [call(): pl.pallas_call(body, out_shape=outs, in_specs=specs, out_specs=vmem(1)[0]...]
    unnamed x32 -> x28, local copies, waits for them, and re-layouts: 8 us -> 4.28 us
    ppermute x9 -> x11, starting transfers between devices: 10.7 us -> 7.71 us  [swap(): return lax.ppermute(value, 'space', [(i, i ^ k) for i in range(4)])]
    ppermute x2 -> x1, waiting for transfers between devices: 0.01 us -> 2.28 us  [on_device(): lax.ppermute(half, 'frame', [(f, f ^ 8) for f in range(FRAMES)])]
  transfers between devices with their start and end apart: 13 -> 12, of which waited for: 4 -> 3; matrix products, arithmetic and copies ran while one was open for 5% -> 1% of each run, Pallas kernels for 18% -> 22%
where the time goes in v1:
time: 111 us
  blocking collectives  57.9 us (52%)
  Pallas kernels  32.6 us (29%)
  starting transfers between devices  9.28 us (8%)
  local copies, waits for them, and re-layouts  5.67 us (5%)
  waiting for transfers between devices  4.89 us (4%)
    all_to_all x1, blocking collectives, on_device(): lax.all_to_all(sent.reshape(FRAMES, SENT, LANES), 'frame', split_axis=0,...  37.6 us
    pallas_call x12, Pallas kernels, call(): pl.pallas_call(body, out_shape=outs, in_specs=specs, out_specs=vmem(1)[0]...  32.6 us
    all_to_all x1, blocking collectives, on_device(): lax.all_to_all(back.reshape(FRAMES, BACK, LANES), 'frame', split_axis=0,...  20.3 us
    ppermute x11, starting transfers between devices, swap(): return lax.ppermute(value, 'space', [(i, i ^ k) for i in range(4)])  7.71 us
    unnamed x28, local copies, waits for them, and re-layouts  4.28 us
    ppermute x11, waiting for transfers between devices, swap(): return lax.ppermute(value, 'space', [(i, i ^ k) for i in range(4)])  2.6 us
    ppermute x1, waiting for transfers between devices, on_device(): lax.ppermute(half, 'frame', [(f, f ^ 8) for f in range(FRAMES)])  2.28 us
  transfers between devices with their start and end apart: 12, of which 3 were waited for; matrix products, arithmetic and copies ran while one was open for 1% of the time, Pallas kernels for 22%

profile of v1, /device:TPU:2, one launch (start us, length us, event | category | flops | bytes accessed | tf_op | source)
XLA Modules:
  0.0 110.6 jit_solution(10893942698211759106)
XLA Ops:
  0.0 0.1 add_convert_fusion.flags_ref
  0.1 0.0 copy-start
  0.1 1.1 %copy-done = bf16[1,12,48,640]{3,2,1,0:T(8,128)(2,1)S(1)} copy-done((bf16[1,12,48,640]{3,2,1,0:T(8,128)(2,1)S(1)}, bf16[1,12,48,640]{3,2,1,0:T(8,128)(2,1)}, u32[]{:S(2)}) %copy-start) | copy-done | bytes 737304
  1.2 1.1 shard_map.136
  2.3 0.1 collective-permute-start
  2.4 0.7 reshape.94.gain_ref
  3.1 0.7 reshape.96.norm_gain_ref
  3.8 0.0 collective-permute-done.near_ref
  3.8 2.3 %collective-permute-start.1 = (bf16[64,640]{1,0:T(8,128)(2,1)S(1)}, bf16[64,640]{1,0:T(8,128)(2,1)S(1)}, u32[]{:S(2)}, u32[]{:S(2)}) collective-permute-start(bf16[64,640]{1,0:T(8,128)(2,1)S(1)} %get-tuple-element.26), channel_id=1, source_target_pairs={{0,3},{1,2},{2,1},{3,0},{4,7},{5,6},{6,5},{7,4},{8,11},{9,10},{10,... | collective-permute-start | bytes 245768 | tf_op jit(solution)/shard_map/ppermute | solution.py:452
  6.1 0.0 copy-start.2
  6.1 1.0 copy-done.2
  7.1 0.0 copy-start.4
  7.1 1.0 copy-done.4
  8.1 0.0 copy-start.12
  8.1 1.1 %copy-done.12 = bf16[12,48,640]{2,1,0:T(8,128)(2,1)S(1)} copy-done((bf16[12,48,640]{2,1,0:T(8,128)(2,1)S(1)}, bf16[12,48,640]{2,1,0:T(8,128)(2,1)}, u32[]{:S(2)}) %copy-start.12) | copy-done | bytes 737304
  9.2 0.0 copy-start.1
  9.2 1.7 %shard_map.139 = (bf16[576,640]{1,0:T(8,128)(2,1)S(1)}, bf16[288,640]{1,0:T(8,128)(2,1)S(1)}) custom-call(f32[1,4]{1,0:T(1,128)S(1)} %add_convert_fusion.flags_ref, bf16[576,640]{1,0:T(8,128)(2,1)S(1)} %bitcast.34, f32[8,640]{1,0:T(8,128)S(1)} %get-tuple-element.25.sums_ref.before_ref, bf16[320,640]{1,0:T(8,128)(2,1)S(1)} %bitcast.21, ...), custom_call_target="tpu_custom_call" | custom-call | flops 2000000000 | tf_op jit(solution)/shard_map/pallas_call | solution.py:68
  11.0 1.5 %collective-permute-start.3 = (bf16[288,640]{1,0:T(8,128)(2,1)S(1)}, bf16[288,640]{1,0:T(8,128)(2,1)S(1)}, u32[]{:S(2)}, u32[]{:S(2)}) collective-permute-start(bf16[288,640]{1,0:T(8,128)(2,1)S(1)} %get-tuple-element.29), channel_id=1, source_target_pairs={{0,2},{1,3},{2,0},{3,1},{4,6},{5,7},{6,4},{7,5},{8,10},{9,11},{10,... | collective-permute-start | bytes 1105928 | tf_op jit(solution)/shard_map/ppermute | solution.py:452
  12.5 0.0 collective-permute-done.1.far_ref
  12.5 0.0 copy-done.1
  12.5 0.0 copy-done.3
  12.5 0.0 copy-done.5
  12.5 0.0 copy-done.11
  12.5 10.1 %shard_map.138 = (bf16[576,640]{1,0:T(8,128)(2,1)S(1)}, bf16[576,384]{1,0:T(8,128)(2,1)S(1)}, bf16[576,640]{1,0:T(8,128)(2,1)S(1)}) custom-call(f32[1,4]{1,0:T(1,128)S(1)} %add_convert_fusion.flags_ref, f32[8,640]{1,0:T(8,128)S(1)} %get-tuple-element.25.sums_ref.before_ref, bf16[576,640]{1,0:T(8,128)(2,1)S(1)} %bitcast.20, ...), custom_call_target="tpu_custom_call" | custom-call | tf_op jit(solution)/shard_map/pallas_call | solution.py:68
  22.7 0.1 collective-permute-start.6
  22.8 0.5 collective-permute-start.5
  23.3 2.1 %collective-permute-start.2 = (bf16[576,640]{1,0:T(8,128)(2,1)S(1)}, bf16[576,640]{1,0:T(8,128)(2,1)S(1)}, u32[]{:S(2)}, u32[]{:S(2)}) collective-permute-start(bf16[576,640]{1,0:T(8,128)(2,1)S(1)} %get-tuple-element.28.refs_1_), channel_id=1, source_target_pairs={{0,2},{1,3},{2,0},{3,1},{4,6},{5,7},{6,4},{7,5},{8,10},{9,11},{10,... | collective-permute-start | bytes 2211848 | tf_op jit(solution)/shard_map/ppermute | solution.py:452
  25.4 0.0 collective-permute-done.3.value_ref
  25.4 1.6 %collective-permute-start.4 = (bf16[288,640]{1,0:T(8,128)(2,1)S(1)}, bf16[288,640]{1,0:T(8,128)(2,1)S(1)}, u32[]{:S(2)}, u32[]{:S(2)}) collective-permute-start(bf16[288,640]{1,0:T(8,128)(2,1)S(1)} %shard_map.140.first_ref), channel_id=1, source_target_pairs={{0,32},{4,36},{8,40},{12,44},{16,48},{20,52},{24,56},{28,60},{32,0... | collective-permute-start | bytes 1105928 | tf_op jit(solution)/shard_map/ppermute | solution.py:512
  27.0 0.0 collective-permute-done.6.refs_4_
  27.0 0.0 collective-permute-done.5.refs_2_
  27.0 6.4 %shard_map.142.before_ref.refs_2_ = f32[576,768]{1,0:T(8,128)S(1)} custom-call(bf16[576,384]{1,0:T(8,128)(2,1)S(1)} %get-tuple-element.27.before_ref.refs_0_.query_ref, bf16[576,640]{1,0:T(8,128)(2,1)S(1)} %get-tuple-element.28.refs_1_, bf16[576,640]{1,0:T(8,128)(2,1)S(1)} %collective-permute-done.5.refs_2_, bf16[576,640]{1,0:T(8,128)(2,1)S(1)} %shard_map.141.refs_3_, ...), custom_call_target="tpu_custom_call" | custom-call | tf_op jit(solution)/shard_map/pallas_call | solution.py:68
  33.4 2.3 %collective-permute-done.4.value_ref = bf16[288,640]{1,0:T(8,128)(2,1)S(1)} collective-permute-done((bf16[288,640]{1,0:T(8,128)(2,1)S(1)}, bf16[288,640]{1,0:T(8,128)(2,1)S(1)}, u32[]{:S(2)}, u32[]{:S(2)}) %collective-permute-start.4) | collective-permute-done | bytes 368672 | tf_op jit(solution)/shard_map/ppermute | solution.py:512
  35.7 1.1 shard_map.144
  36.8 0.1 collective-permute-start.10
  36.9 0.5 collective-permute-start.7
  37.4 0.1 collective-permute-start.8
  37.5 0.4 collective-permute-start.9
  37.9 1.4 %shard_map.145.refs_6_ = f32[576,768]{1,0:T(8,128)S(1)} custom-call(bf16[576,384]{1,0:T(8,128)(2,1)S(1)} %get-tuple-element.27.before_ref.refs_0_.query_ref, bf16[576,640]{1,0:T(8,128)(2,1)S(1)} %get-tuple-element.31.refs_1_, f32[576,768]{1,0:T(8,128)S(1)} %shard_map.142.before_ref.refs_2_), custom_call_target="tpu_custom_call" | custom-call | tf_op jit(solution)/shard_map/pallas_call | solution.py:68
  39.4 0.0 collective-permute-done.10.refs_5_
  39.4 0.0 collective-permute-done.7.refs_2_
  39.4 0.0 collective-permute-done.8.refs_3_
  39.4 0.0 collective-permute-done.9.refs_4_
  39.4 2.0 %shard_map.146.before_ref.refs_2_ = f32[576,768]{1,0:T(8,128)S(1)} custom-call(bf16[576,384]{1,0:T(8,128)(2,1)S(1)} %get-tuple-element.27.before_ref.refs_0_.query_ref, bf16[576,640]{1,0:T(8,128)(2,1)S(1)} %get-tuple-element.31.refs_1_, bf16[144,640]{1,0:T(8,128)(2,1)S(1)} %collective-permute-done.7.refs_2_, ...), custom_call_target="tpu_custom_call" | custom-call | tf_op jit(solution)/shard_map/pallas_call | solution.py:68
  41.4 0.0 copy-start.13
  41.4 1.8 %collective-permute-done.2.value_ref = bf16[576,640]{1,0:T(8,128)(2,1)S(1)} collective-permute-done((bf16[576,640]{1,0:T(8,128)(2,1)S(1)}, bf16[576,640]{1,0:T(8,128)(2,1)S(1)}, u32[]{:S(2)}, u32[]{:S(2)}) %collective-permute-start.2) | collective-permute-done | bytes 737312 | tf_op jit(solution)/shard_map/ppermute | solution.py:452
  43.3 0.0 collective-permute-start.11
  43.3 0.0 copy-done.13
  43.3 0.0 copy-start.6
  43.3 1.4 %shard_map.148.acc_ref = f32[576,768]{1,0:T(8,128)S(1)} custom-call(bf16[576,384]{1,0:T(8,128)(2,1)S(1)} %get-tuple-element.27.before_ref.refs_0_.query_ref, bf16[576,640]{1,0:T(8,128)(2,1)S(1)} %shard_map.147.refs_1_.first_ref, f32[576,768]{1,0:T(8,128)S(1)} %shard_map.146.before_ref.refs_2_), custom_call_target="tpu_custom_call" | custom-call | tf_op jit(solution)/shard_map/pallas_call | solution.py:68
  44.7 0.7 collective-permute-done.11.second_ref
  45.5 0.0 copy-done.6
  45.5 3.4 %shard_map.149 = (bf16[576,640]{1,0:T(8,128)(2,1)S(1)}, bf16[3072,128]{1,0:T(8,128)(2,1)S(1)}) custom-call(bf16[576,384]{1,0:T(8,128)(2,1)S(1)} %get-tuple-element.27.before_ref.refs_0_.query_ref, f32[576,768]{1,0:T(8,128)S(1)} %shard_map.148.acc_ref, bf16[576,640]{1,0:T(8,128)(2,1)S(1)} %shard_map.147.refs_1_.first_ref, ...), custom_call_target="tpu_custom_call" | custom-call | tf_op jit(solution)/shard_map/pallas_call | solution.py:68
  48.9 0.0 copy-start.7
  48.9 0.0 copy-start.8
  48.9 0.0 copy-start.9
  48.9 37.6 %all_to_all.10 = bf16[64,48,128]{2,1,0:T(8,128)(2,1)S(1)} all-to-all(bf16[64,48,128]{2,1,0:T(8,128)(2,1)S(1)} %bitcast.29), channel_id=1, replica_groups=mesh['frame'=64,'space'=4] {'frame'}, dimensions={0} | all-to-all | bytes 1572864 | tf_op jit(solution)/shard_map/all_to_all | solution.py:554
  86.5 0.0 copy-done.7
  86.5 0.0 copy-done.8
  86.5 0.0 copy-done.9
  86.5 2.3 %shard_map.150 = bf16[1536,128]{1,0:T(8,128)(2,1)S(1)} custom-call(bf16[3072,128]{1,0:T(8,128)(2,1)S(1)} %bitcast.18, bf16[320,640]{1,0:T(8,128)(2,1)S(1)} %bitcast.30, bf16[320,640]{1,0:T(8,128)(2,1)S(1)} %bitcast.31, bf16[320,640]{1,0:T(8,128)(2,1)S(1)} %bitcast.32), custom_call_target="tpu_custom_call" | custom-call | tf_op jit(solution)/shard_map/pallas_call | solution.py:68
  88.8 20.3 %all_to_all.11 = bf16[64,24,128]{2,1,0:T(8,128)(2,1)S(1)} all-to-all(bf16[64,24,128]{2,1,0:T(8,128)(2,1)S(1)} %bitcast.27), channel_id=1, replica_groups=mesh['frame'=64,'space'=4] {'frame'}, dimensions={0} | all-to-all | bytes 786432 | tf_op jit(solution)/shard_map/all_to_all | solution.py:573
  109.1 0.0 copy-done.10
  109.1 1.5 %shard_map.151 = bf16[576,640]{1,0:T(8,128)(2,1)} custom-call(bf16[1536,128]{1,0:T(8,128)(2,1)S(1)} %bitcast.28, bf16[320,640]{1,0:T(8,128)(2,1)S(1)} %copy-done.10, bf16[576,640]{1,0:T(8,128)(2,1)S(1)} %get-tuple-element.38.mixed_ref), custom_call_target="tpu_custom_call" | custom-call | tf_op jit(solution)/shard_map/pallas_call | solution.py:68
  (10 shorter events, 0.0 us)
Async XLA Ops:
  0.1 1.1 %copy-start = (bf16[1,12,48,640]{3,2,1,0:T(8,128)(2,1)S(1)}, bf16[1,12,48,640]{3,2,1,0:T(8,128)(2,1)}, u32[]{:S(2)}) copy-start(bf16[1,12,48,640]{3,2,1,0:T(8,128)(2,1)} %param.14) | copy-start | bytes 2211844
  2.3 1.5 %collective-permute-start = (bf16[64,640]{1,0:T(8,128)(2,1)S(1)}, bf16[64,640]{1,0:T(8,128)(2,1)S(1)}, u32[]{:S(2)}, u32[]{:S(2)}) collective-permute-start(bf16[64,640]{1,0:T(8,128)(2,1)S(1)} %get-tuple-element.23), channel_id=1, source_target_pairs={{0,1},{1,0},{2,3},{3,2},{4,5},{5,4},{6,7},{7,6},{8,9},{9,8},{10,11... | collective-permute-start | bytes 245768 | tf_op jit(solution)/shard_map/ppermute | solution.py:452
  3.8 8.7 %collective-permute-start.1 = (bf16[64,640]{1,0:T(8,128)(2,1)S(1)}, bf16[64,640]{1,0:T(8,128)(2,1)S(1)}, u32[]{:S(2)}, u32[]{:S(2)}) collective-permute-start(bf16[64,640]{1,0:T(8,128)(2,1)S(1)} %get-tuple-element.26), channel_id=1, source_target_pairs={{0,3},{1,2},{2,1},{3,0},{4,7},{5,6},{6,5},{7,4},{8,11},{9,10},{10,... | collective-permute-start | bytes 245768 | tf_op jit(solution)/shard_map/ppermute | solution.py:452
  6.1 1.0 copy-start.2
  7.1 1.0 copy-start.4
  8.1 1.1 %copy-start.12 = (bf16[12,48,640]{2,1,0:T(8,128)(2,1)S(1)}, bf16[12,48,640]{2,1,0:T(8,128)(2,1)}, u32[]{:S(2)}) copy-start(bf16[12,48,640]{2,1,0:T(8,128)(2,1)} %param.15) | copy-start | bytes 2211844
  9.2 3.3 %copy-start.1 = (bf16[1,12,48,640]{3,2,1,0:T(8,128)(2,1)S(1)}, bf16[1,12,48,640]{3,2,1,0:T(8,128)(2,1)}, u32[]{:S(2)}) copy-start(bf16[1,12,48,640]{3,2,1,0:T(8,128)(2,1)} %param.14) | copy-start | bytes 2211844
  9.2 3.3 %copy-start.3 = (bf16[640,320]{0,1:T(8,128)(2,1)S(1)}, bf16[640,320]{0,1:T(8,128)(2,1)}, u32[]{:S(2)}) copy-start(bf16[640,320]{0,1:T(8,128)(2,1)} %param.20) | copy-start | bytes 1228804
  9.2 3.3 %copy-start.5 = (bf16[640,320]{0,1:T(8,128)(2,1)S(1)}, bf16[640,320]{0,1:T(8,128)(2,1)}, u32[]{:S(2)}) copy-start(bf16[640,320]{0,1:T(8,128)(2,1)} %param.21) | copy-start | bytes 1228804
  9.2 3.3 %copy-start.11 = (bf16[640,320]{0,1:T(8,128)(2,1)S(1)}, bf16[640,320]{0,1:T(8,128)(2,1)}, u32[]{:S(2)}) copy-start(bf16[640,320]{0,1:T(8,128)(2,1)} %param.19) | copy-start | bytes 1228804
  11.0 14.4 %collective-permute-start.3 = (bf16[288,640]{1,0:T(8,128)(2,1)S(1)}, bf16[288,640]{1,0:T(8,128)(2,1)S(1)}, u32[]{:S(2)}, u32[]{:S(2)}) collective-permute-start(bf16[288,640]{1,0:T(8,128)(2,1)S(1)} %get-tuple-element.29), channel_id=1, source_target_pairs={{0,2},{1,3},{2,0},{3,1},{4,6},{5,7},{6,4},{7,5},{8,10},{9,11},{10,... | collective-permute-start | bytes 1105928 | tf_op jit(solution)/shard_map/ppermute | solution.py:452
  22.7 4.3 %collective-permute-start.6 = (bf16[576,640]{1,0:T(8,128)(2,1)S(1)}, bf16[576,640]{1,0:T(8,128)(2,1)S(1)}, u32[]{:S(2)}, u32[]{:S(2)}) collective-permute-start(bf16[576,640]{1,0:T(8,128)(2,1)S(1)} %shard_map.141.refs_3_), channel_id=1, source_target_pairs={{0,1},{1,0},{2,3},{3,2},{4,5},{5,4},{6,7},{7,6},{8,9},{9,8},{10,11... | collective-permute-start | bytes 2211848 | tf_op jit(solution)/shard_map/ppermute | solution.py:452
  22.8 4.2 %collective-permute-start.5 = (bf16[576,640]{1,0:T(8,128)(2,1)S(1)}, bf16[576,640]{1,0:T(8,128)(2,1)S(1)}, u32[]{:S(2)}, u32[]{:S(2)}) collective-permute-start(bf16[576,640]{1,0:T(8,128)(2,1)S(1)} %get-tuple-element.28.refs_1_), channel_id=1, source_target_pairs={{0,1},{1,0},{2,3},{3,2},{4,5},{5,4},{6,7},{7,6},{8,9},{9,8},{10,11... | collective-permute-start | bytes 2211848 | tf_op jit(solution)/shard_map/ppermute | solution.py:452
  23.3 20.0 %collective-permute-start.2 = (bf16[576,640]{1,0:T(8,128)(2,1)S(1)}, bf16[576,640]{1,0:T(8,128)(2,1)S(1)}, u32[]{:S(2)}, u32[]{:S(2)}) collective-permute-start(bf16[576,640]{1,0:T(8,128)(2,1)S(1)} %get-tuple-element.28.refs_1_), channel_id=1, source_target_pairs={{0,2},{1,3},{2,0},{3,1},{4,6},{5,7},{6,4},{7,5},{8,10},{9,11},{10,... | collective-permute-start | bytes 2211848 | tf_op jit(solution)/shard_map/ppermute | solution.py:452
  25.4 10.3 %collective-permute-start.4 = (bf16[288,640]{1,0:T(8,128)(2,1)S(1)}, bf16[288,640]{1,0:T(8,128)(2,1)S(1)}, u32[]{:S(2)}, u32[]{:S(2)}) collective-permute-start(bf16[288,640]{1,0:T(8,128)(2,1)S(1)} %shard_map.140.first_ref), channel_id=1, source_target_pairs={{0,32},{4,36},{8,40},{12,44},{16,48},{20,52},{24,56},{28,60},{32,0... | collective-permute-start | bytes 1105928 | tf_op jit(solution)/shard_map/ppermute | solution.py:512
  36.8 2.6 %collective-permute-start.10 = (bf16[144,640]{1,0:T(8,128)(2,1)S(1)}, bf16[144,640]{1,0:T(8,128)(2,1)S(1)}, u32[]{:S(2)}, u32[]{:S(2)}) collective-permute-start(bf16[144,640]{1,0:T(8,128)(2,1)S(1)} %get-tuple-element.35), channel_id=1, source_target_pairs={{0,1},{1,0},{2,3},{3,2},{4,5},{5,4},{6,7},{7,6},{8,9},{9,8},{10,11... | collective-permute-start | bytes 552968 | tf_op jit(solution)/shard_map/ppermute | solution.py:452
  36.9 2.5 %collective-permute-start.7 = (bf16[144,640]{1,0:T(8,128)(2,1)S(1)}, bf16[144,640]{1,0:T(8,128)(2,1)S(1)}, u32[]{:S(2)}, u32[]{:S(2)}) collective-permute-start(bf16[144,640]{1,0:T(8,128)(2,1)S(1)} %get-tuple-element.32), channel_id=1, source_target_pairs={{0,1},{1,0},{2,3},{3,2},{4,5},{5,4},{6,7},{7,6},{8,9},{9,8},{10,11... | collective-permute-start | bytes 552968 | tf_op jit(solution)/shard_map/ppermute | solution.py:452
  37.4 2.0 %collective-permute-start.8 = (bf16[144,640]{1,0:T(8,128)(2,1)S(1)}, bf16[144,640]{1,0:T(8,128)(2,1)S(1)}, u32[]{:S(2)}, u32[]{:S(2)}) collective-permute-start(bf16[144,640]{1,0:T(8,128)(2,1)S(1)} %get-tuple-element.33), channel_id=1, source_target_pairs={{0,1},{1,0},{2,3},{3,2},{4,5},{5,4},{6,7},{7,6},{8,9},{9,8},{10,11... | collective-permute-start | bytes 552968 | tf_op jit(solution)/shard_map/ppermute | solution.py:452
  37.5 1.9 %collective-permute-start.9 = (bf16[144,640]{1,0:T(8,128)(2,1)S(1)}, bf16[144,640]{1,0:T(8,128)(2,1)S(1)}, u32[]{:S(2)}, u32[]{:S(2)}) collective-permute-start(bf16[144,640]{1,0:T(8,128)(2,1)S(1)} %get-tuple-element.34), channel_id=1, source_target_pairs={{0,1},{1,0},{2,3},{3,2},{4,5},{5,4},{6,7},{7,6},{8,9},{9,8},{10,11... | collective-permute-start | bytes 552968 | tf_op jit(solution)/shard_map/ppermute | solution.py:452
  41.4 1.9 %copy-start.13 = (f32[640]{0:T(1024)S(1)}, f32[640]{0:T(1024)}, u32[]{:S(2)}) copy-start(f32[640]{0:T(1024)} %param.23) | copy-start | bytes 7684
  43.3 2.2 %collective-permute-start.11 = (bf16[576,640]{1,0:T(8,128)(2,1)S(1)}, bf16[576,640]{1,0:T(8,128)(2,1)S(1)}, u32[]{:S(2)}, u32[]{:S(2)}) collective-permute-start(bf16[576,640]{1,0:T(8,128)(2,1)S(1)} %shard_map.147.refs_1_.first_ref), channel_id=1, source_target_pairs={{0,1},{1,0},{2,3},{3,2},{4,5},{5,4},{6,7},{7,6},{8,9},{9,8},{10,11... | collective-permute-start | bytes 2211848 | tf_op jit(solution)/shard_map/ppermute | solution.py:452
  43.3 2.2 %copy-start.6 = (bf16[320,640]{1,0:T(8,128)(2,1)S(1)}, bf16[320,640]{1,0:T(8,128)(2,1)}, u32[]{:S(2)}) copy-start(bf16[320,640]{1,0:T(8,128)(2,1)} %weight_ref.2) | copy-start | bytes 1228804
  48.9 37.7 %copy-start.7 = (bf16[640,320]{0,1:T(8,128)(2,1)S(1)}, bf16[640,320]{0,1:T(8,128)(2,1)}, u32[]{:S(2)}) copy-start(bf16[640,320]{0,1:T(8,128)(2,1)} %param.24) | copy-start | bytes 1228804
  48.9 37.6 %copy-start.8 = (bf16[640,320]{0,1:T(8,128)(2,1)S(1)}, bf16[640,320]{0,1:T(8,128)(2,1)}, u32[]{:S(2)}) copy-start(bf16[640,320]{0,1:T(8,128)(2,1)} %param.25) | copy-start | bytes 1228804
  48.9 37.6 %copy-start.9 = (bf16[640,320]{0,1:T(8,128)(2,1)S(1)}, bf16[640,320]{0,1:T(8,128)(2,1)}, u32[]{:S(2)}) copy-start(bf16[640,320]{0,1:T(8,128)(2,1)} %param.26) | copy-start | bytes 1228804
  86.5 22.5 %copy-start.10 = (bf16[320,640]{1,0:T(8,128)(2,1)S(1)}, bf16[320,640]{1,0:T(8,128)(2,1)}, u32[]{:S(2)}) copy-start(bf16[320,640]{1,0:T(8,128)(2,1)} %weight_ref.3) | copy-start | bytes 1228804

commit v2 on v1

--- a/solution.py
+++ b/solution.py
@@ -21,7 +21,10 @@
 SENT = 48
 TILE = 768
 HEAD = 512
-CHUNKS = 4
+FIRST = 256
+PART = CELLS // 2
+CHUNK = CELLS // 4
+TAIL = 256
 BACK = 24
 
 epsilon = 1e-05
@@ -142,15 +145,20 @@
 
 
 def far_reference_kernel(first_ref, second_ref, key_ref, value_ref, out_ref, *refs):
-    chunk_refs, weight = refs[:CHUNKS], refs[CHUNKS]
+    chunk_refs, weight = refs[:-1], refs[-1]
     weight[0:INNER, :] = key_ref[...]
     weight[INNER:, :] = value_ref[...]
-    half, size = CELLS // 2, CELLS // CHUNKS
     for i, ref in enumerate((first_ref, second_ref)):
-        out = reference_kv(weight, ref[...])
-        out_ref[i * half : (i + 1) * half, :] = out
-        for j in range(half // size):
-            chunk_refs[i * (half // size) + j][...] = out[j * size : (j + 1) * size]
+        out_ref[i * PART : (i + 1) * PART, :] = reference_kv(weight, ref[...])
+    for i, ref in enumerate(chunk_refs):
+        ref[...] = out_ref[i * CHUNK : (i + 1) * CHUNK, :]
+
+
+def parts_kernel(value_ref, out_ref, *part_refs):
+    out_ref[...] = value_ref[...]
+    size = FIRST // len(part_refs)
+    for i, ref in enumerate(part_refs):
+        ref[...] = value_ref[i * size : (i + 1) * size, :]
 
 
 def conv_kernel(
@@ -168,21 +176,18 @@
     hidden_out,
     query_out,
     kv_out,
+    first_out,
+    second_out,
     lhs,
     weight,
-    taps,
-    arrived,
 ):
-    copies = [pltpu.make_async_copy(kernel_ref.at[a], taps.at[a], arrived.at[a]) for a in range(3)]
-    for copy in copies:
-        copy.start()
     weight[0:INNER, :] = key_ref[...]
     weight[INNER:, :] = value_ref[...]
     group_sum, group_sq = sums_of(far_ref[W:, :].astype(f32))
     members = float(4 * CELLS * (C // GROUPS))
     average = (group_sum + sums_ref[0:1]) / members
     variance = (group_sq + sums_ref[1:2]) / members - average * average
-    factor = lax.rsqrt(variance + epsilon) * gain_ref[...]
+    factor = lax.rsqrt(variance + epsilon) * gain_ref[...].reshape(1, C)
     at = lax.broadcasted_iota(jnp.int32, (W, 1), 0)
     odd = flags_ref[0, 2] > 0.5
 
@@ -205,13 +210,14 @@
         rows = slice(first, first + CELLS // 2)
         total = None
         for a in range(3):
-            if first == 0:
-                copies[a].wait()
-            part = dot(lhs[first + a * W : first + a * W + CELLS // 2, :], taps[a])
+            part = dot(lhs[first + a * W : first + a * W + CELLS // 2, :], kernel_ref[a])
             total = part if total is None else total + part
         hidden_out[rows, :] = (x_ref[rows, :].astype(f32) + total).astype(bf16)
-    normed = layer_norm(hidden_out[...].astype(f32), norm_gain_ref[...]).astype(bf16)
-    kv_out[...] = dot_t(normed, weight[...]).astype(bf16)
+    normed = layer_norm(hidden_out[...].astype(f32), norm_gain_ref[...].reshape(1, C)).astype(bf16)
+    kv = dot_t(normed, weight[...]).astype(bf16)
+    kv_out[...] = kv
+    first_out[...] = kv[0:FIRST]
+    second_out[...] = kv[FIRST:]
     query_out[:, 0:INNER] = (dot_t(normed, query_ref[...]) * QUERY_SCALE).astype(bf16)
     query_out[:, INNER:] = jnp.zeros((CELLS, 64), bf16)
 
@@ -310,7 +316,7 @@
         update = part if update is None else update + part
     mixed = (hidden_ref[...].astype(f32) + update).astype(bf16)
     mixed_out[...] = mixed
-    framed = layer_norm(mixed.astype(f32), gain_ref[...])
+    framed = layer_norm(mixed.astype(f32), gain_ref[...].reshape(1, C))
     for j in range(PLACES):
         for c in range(C // LANES):
             rows[pl.ds(j * 5 + c, FRAMES, stride=SENT + 1), :] = framed[
@@ -457,12 +463,14 @@
         [struct((8, C), f32), struct((W + 16, C), bf16), struct((W, C), bf16)],
         [flags, x],
         smem=1,
+        flops=2 * 10**9,
     )
     near = swap(near, 1)
     sums, far = call(
         chip_sums_kernel,
         [struct((8, C), f32), struct((W + 16, C), bf16)],
         [sums, near, edge],
+        flops=2 * 10**9,
     )
     far = swap(far, 3)
 
@@ -472,16 +480,19 @@
         [flags, states, sums, spatial_key.T, spatial_value.T],
         scratch=[pltpu.VMEM((C, C), bf16)],
         smem=1,
-        flops=2*10**9,
+        flops=2 * 10**9,
+        limit=8,
     )
     half = swap(half, 2)
 
-    hidden, query, kv = call(
+    hidden, query, kv, first, second = call(
         conv_kernel,
         [
             struct((CELLS, C), bf16),
             struct((CELLS, 384), bf16),
             struct((CELLS, C), bf16),
+            struct((FIRST, C), bf16),
+            struct((CELLS - FIRST, C), bf16),
         ],
         [
             flags,
@@ -489,9 +500,9 @@
             x,
             near,
             far,
-            group_gain.reshape(1, C),
+            group_gain,
             conv_weight.reshape(3, 3 * C, C),
-            norm_gain.reshape(1, C),
+            norm_gain,
             spatial_query.T,
             spatial_key.T,
             spatial_value.T,
@@ -499,18 +510,16 @@
         scratch=[
             pltpu.VMEM(((STRIP + 2) * W, 3 * C), bf16),
             pltpu.VMEM((C, C), bf16),
-            pltpu.VMEM((3, 3 * C, C), bf16),
-            pltpu.SemaphoreType.DMA((3,)),
         ],
         smem=1,
-        limit=46,
-        anywhere=(6,),
+        limit=16,
     )
     ref_kv = after(ref_kv, query)
     ref_near = swap(ref_kv, 1)
     half = after(half, query)
     other_half = lax.ppermute(half, "frame", [(f, f ^ 8) for f in range(FRAMES)])
-    kv_far = swap(kv, 2)
+    first = swap(first, 2)
+    second = swap(second, 2)
     kv_near = swap(kv, 1)
 
     def attention(kv_parts, start):
@@ -525,29 +534,38 @@
         )
 
     acc = attention([(part, 0, CELLS) for part in (kv, kv_near, ref_kv, ref_near)], None)
-    ref_far, *chunks = call(
+    chunk = struct((CHUNK, C), bf16)
+    ref_far, *ref_far_near = call(
         far_reference_kernel,
-        [struct((CELLS, C), bf16)] + [struct((CELLS // CHUNKS, C), bf16)] * CHUNKS,
+        [struct((CELLS, C), bf16)] + [chunk] * (CELLS // CHUNK),
         [half, after(other_half, acc), spatial_key.T, spatial_value.T],
         scratch=[pltpu.VMEM((C, C), bf16)],
     )
-    chunks = [swap(chunk, 1) for chunk in chunks]
+    ref_far_near = [swap(part, 1) for part in ref_far_near]
+    first, *first_near = call(
+        parts_kernel,
+        [struct((FIRST, C), bf16)] + [struct((FIRST // 2, C), bf16)] * 2,
+        [after(first, ref_far)],
+    )
+    first_near = [swap(part, 1) for part in first_near]
     acc = attention([(ref_far, 0, HEAD)], acc)
     acc = attention(
-        [(ref_far, HEAD, CELLS)] + [(chunk, 0, CELLS // CHUNKS) for chunk in chunks], acc
-    )
-    kv_far = after(kv_far, acc)
-    kv_far_near = swap(kv_far, 1)
-    acc = attention([(kv_far, 0, HEAD)], acc)
-    ranges = [(HEAD, CELLS), (0, CELLS)]
+        [(ref_far, HEAD, CELLS), (first, 0, FIRST)]
+        + [(part, 0, part.shape[0]) for part in ref_far_near + first_near],
+        acc,
+    )
+    second = after(second, acc)
+    second_near = swap(second, 1)
+    acc = attention([(second, 0, TAIL)], acc)
+    ranges = [(TAIL, CELLS - FIRST), (0, CELLS - FIRST)]
     mixed, sent = call(
         functools.partial(last_attention_kernel, ranges),
         [struct((CELLS, C), bf16), struct((FRAMES * SENT, LANES), bf16)],
-        [query, acc, kv_far, kv_far_near, hidden, spatial_out, frame_gain.reshape(1, C)],
+        [query, acc, second, second_near, hidden, spatial_out, frame_gain],
         scratch=[
             pltpu.VMEM((FRAMES * (SENT + 1), LANES), f32),
             pltpu.VMEM((384, C), bf16),
-            pltpu.VMEM((2 * CELLS - HEAD, C), bf16),
+            pltpu.VMEM((2 * (CELLS - FIRST) - TAIL, C), bf16),
         ],
         limit=16,
     )

time: 111 us -> 107 us (0.964)
  local copies, waits for them, and re-layouts: 5.67 us -> 1.19 us
  Pallas kernels: 32.6 us -> 30.4 us
  starting transfers between devices: 9.28 us -> 11 us
    ppermute x11 -> x14, waiting for transfers between devices: 2.6 us -> 5.84 us  [swap(): return lax.ppermute(value, 'space', [(i, i ^ k) for i in range(4)])]
    unnamed x28 -> x32, local copies, waits for them, and re-layouts: 4.28 us -> 1.19 us
    ppermute x1, waiting for transfers between devices: 2.28 us -> 0.01 us  [on_device(): lax.ppermute(half, 'frame', [(f, f ^ 8) for f in range(FRAMES)])]
    pallas_call x12 -> x13, Pallas kernels: 32.6 us -> 30.4 us  [call(): pl.pallas_call(body, out_shape=outs, in_specs=specs, out_specs=vmem(1)[0]...]
    ppermute x11 -> x14, starting transfers between devices: 7.71 us -> 9.44 us  [swap(): return lax.ppermute(value, 'space', [(i, i ^ k) for i in range(4)])]
    reshape x3 -> x0, local copies, waits for them, and re-layouts: 1.38 us -> none  [the longest x1 0.69 us: on_device(): group_gain.reshape(1, C)]
  transfers between devices with their start and end apart: 12 -> 15, of which waited for: 3 -> 8; matrix products, arithmetic and copies ran while one was open for 1% -> 0% of each run, Pallas kernels for 22% -> 22%
where the time goes in v2:
time: 107 us; the launch traced here: 106 us
  blocking collectives  57.7 us (54%)
  Pallas kernels  30.4 us (28%)
  starting transfers between devices  11 us (10%)
  waiting for transfers between devices  5.85 us (5%)
  local copies, waits for them, and re-layouts  1.19 us (1%)
    all_to_all x1, blocking collectives, on_device(): lax.all_to_all(sent.reshape(FRAMES, SENT, LANES), 'frame', split_axis=0,...  37.3 us
    pallas_call x13, Pallas kernels, call(): pl.pallas_call(body, out_shape=outs, in_specs=specs, out_specs=vmem(1)[0]...  30.4 us
    all_to_all x1, blocking collectives, on_device(): lax.all_to_all(back.reshape(FRAMES, BACK, LANES), 'frame', split_axis=0,...  20.3 us
    ppermute x14, starting transfers between devices, swap(): return lax.ppermute(value, 'space', [(i, i ^ k) for i in range(4)])  9.44 us
    ppermute x14, waiting for transfers between devices, swap(): return lax.ppermute(value, 'space', [(i, i ^ k) for i in range(4)])  5.84 us
  transfers between devices with their start and end apart: 15, of which 8 were waited for; matrix products, arithmetic and copies ran while one was open for 0% of the time, Pallas kernels for 22%

profile of v2, /device:TPU:2, one launch (start us, length us, event | category | flops | bytes accessed | tf_op | source)
XLA Modules:
  0.0 106.4 jit_solution(11635147431648277498)
XLA Ops:
  0.0 0.1 add_convert_fusion.flags_ref
  0.1 1.1 %copy-done.2 = bf16[1,12,48,640]{3,2,1,0:T(8,128)(2,1)S(1)} copy-done((bf16[1,12,48,640]{3,2,1,0:T(8,128)(2,1)S(1)}, bf16[1,12,48,640]{3,2,1,0:T(8,128)(2,1)}, u32[]{:S(2)}) %copy-start.2) | copy-done | bytes 737304
  1.2 1.1 %shard_map.136 = (f32[8,640]{1,0:T(8,128)S(1)}, bf16[64,640]{1,0:T(8,128)(2,1)S(1)}, bf16[48,640]{1,0:T(8,128)(2,1)S(1)}) custom-call(f32[1,4]{1,0:T(1,128)S(1)} %add_convert_fusion.flags_ref, bf16[576,640]{1,0:T(8,128)(2,1)S(1)} %bitcast.31), custom_call_target="tpu_custom_call" | custom-call | flops 2000000000 | tf_op jit(solution)/shard_map/pallas_call | solution.py:71
  2.3 0.1 collective-permute-start
  2.4 1.3 %collective-permute-done.near_ref = bf16[64,640]{1,0:T(8,128)(2,1)S(1)} collective-permute-done((bf16[64,640]{1,0:T(8,128)(2,1)S(1)}, bf16[64,640]{1,0:T(8,128)(2,1)S(1)}, u32[]{:S(2)}, u32[]{:S(2)}) %collective-permute-start) | collective-permute-done | bytes 81952 | tf_op jit(solution)/shard_map/ppermute | solution.py:458
  3.7 2.0 %collective-permute-start.1 = (bf16[64,640]{1,0:T(8,128)(2,1)S(1)}, bf16[64,640]{1,0:T(8,128)(2,1)S(1)}, u32[]{:S(2)}, u32[]{:S(2)}) collective-permute-start(bf16[64,640]{1,0:T(8,128)(2,1)S(1)} %get-tuple-element.31), channel_id=1, source_target_pairs={{0,3},{1,2},{2,1},{3,0},{4,7},{5,6},{6,5},{7,4},{8,11},{9,10},{10,... | collective-permute-start | bytes 245768 | tf_op jit(solution)/shard_map/ppermute | solution.py:458
  5.7 0.0 copy-done
  5.7 0.0 copy-done.1
  5.7 0.0 copy-done.13
  5.7 0.0 copy-start.9
  5.7 0.0 copy-start.10
  5.7 0.0 copy-start.11
  5.7 1.7 %shard_map.139 = (bf16[576,640]{1,0:T(8,128)(2,1)S(1)}, bf16[288,640]{1,0:T(8,128)(2,1)S(1)}) custom-call(f32[1,4]{1,0:T(1,128)S(1)} %add_convert_fusion.flags_ref, bf16[576,640]{1,0:T(8,128)(2,1)S(1)} %bitcast.37, f32[8,640]{1,0:T(8,128)S(1)} %get-tuple-element.30.sums_ref.before_ref, bf16[320,640]{1,0:T(8,128)(2,1)S(1)} %bitcast.22, ...), custom_call_target="tpu_custom_call" | custom-call | flops 2000000000 | tf_op jit(solution)/shard_map/pallas_call | solution.py:71
  7.5 1.5 %collective-permute-start.3 = (bf16[288,640]{1,0:T(8,128)(2,1)S(1)}, bf16[288,640]{1,0:T(8,128)(2,1)S(1)}, u32[]{:S(2)}, u32[]{:S(2)}) collective-permute-start(bf16[288,640]{1,0:T(8,128)(2,1)S(1)} %get-tuple-element.34), channel_id=1, source_target_pairs={{0,2},{1,3},{2,0},{3,1},{4,6},{5,7},{6,4},{7,5},{8,10},{9,11},{10,... | collective-permute-start | bytes 1105928 | tf_op jit(solution)/shard_map/ppermute | solution.py:458
  9.0 0.7 collective-permute-done.1.far_ref
  9.7 0.0 slice-done
  9.7 0.0 slice-done.1
  9.7 0.0 copy-done.3
  9.7 0.0 copy-done.9
  9.7 0.0 copy-done.10
  9.7 0.0 copy-done.11
  9.7 7.9 %shard_map.138 = (bf16[576,640]{1,0:T(8,128)(2,1)S(1)}, bf16[576,384]{1,0:T(8,128)(2,1)S(1)}, bf16[576,640]{1,0:T(8,128)(2,1)S(1)}, bf16[256,640]{1,0:T(8,128)(2,1)S(1)}, bf16[320,640]{1,0:T(8,128)(2,1)S(1)}) custom-call(f32[1,4]{1,0:T(1,128)S(1)} %add_convert_fusion.flags_ref, f32[8,640]{1,0:T(8,128)S(1)} %get-tuple-element.30.sums_ref.before_ref, ...), custom_call_target="tpu_custom_call" | custom-call | tf_op jit(solution)/shard_map/pallas_call | solution.py:71
  17.7 0.2 collective-permute-start.6
  17.9 0.4 collective-permute-start.5
  18.3 1.6 %collective-permute-done.3.value_ref = bf16[288,640]{1,0:T(8,128)(2,1)S(1)} collective-permute-done((bf16[288,640]{1,0:T(8,128)(2,1)S(1)}, bf16[288,640]{1,0:T(8,128)(2,1)S(1)}, u32[]{:S(2)}, u32[]{:S(2)}) %collective-permute-start.3) | collective-permute-done | bytes 368672 | tf_op jit(solution)/shard_map/ppermute | solution.py:458
  19.9 1.6 %collective-permute-start.4 = (bf16[288,640]{1,0:T(8,128)(2,1)S(1)}, bf16[288,640]{1,0:T(8,128)(2,1)S(1)}, u32[]{:S(2)}, u32[]{:S(2)}) collective-permute-start(bf16[288,640]{1,0:T(8,128)(2,1)S(1)} %shard_map.140.first_ref), channel_id=1, source_target_pairs={{0,32},{4,36},{8,40},{12,44},{16,48},{20,52},{24,56},{28,60},{32,0... | collective-permute-start | bytes 1105928 | tf_op jit(solution)/shard_map/ppermute | solution.py:520
  21.5 1.4 %collective-permute-start.7 = (bf16[256,640]{1,0:T(8,128)(2,1)S(1)}, bf16[256,640]{1,0:T(8,128)(2,1)S(1)}, u32[]{:S(2)}, u32[]{:S(2)}) collective-permute-start(bf16[256,640]{1,0:T(8,128)(2,1)S(1)} %get-tuple-element.38), channel_id=1, source_target_pairs={{0,2},{1,3},{2,0},{3,1},{4,6},{5,7},{6,4},{7,5},{8,10},{9,11},{10,... | collective-permute-start | bytes 983048 | tf_op jit(solution)/shard_map/ppermute | solution.py:458
  22.9 2.1 %collective-permute-start.2 = (bf16[320,640]{1,0:T(8,128)(2,1)S(1)}, bf16[320,640]{1,0:T(8,128)(2,1)S(1)}, u32[]{:S(2)}, u32[]{:S(2)}) collective-permute-start(bf16[320,640]{1,0:T(8,128)(2,1)S(1)} %get-tuple-element.33), channel_id=1, source_target_pairs={{0,2},{1,3},{2,0},{3,1},{4,6},{5,7},{6,4},{7,5},{8,10},{9,11},{10,... | collective-permute-start | bytes 1228808 | tf_op jit(solution)/shard_map/ppermute | solution.py:458
  25.0 0.0 collective-permute-done.6.refs_4_
  25.0 0.0 collective-permute-done.5.refs_2_
  25.0 6.5 %shard_map.142.before_ref.refs_2_ = f32[576,768]{1,0:T(8,128)S(1)} custom-call(bf16[576,384]{1,0:T(8,128)(2,1)S(1)} %get-tuple-element.32.before_ref.refs_0_.query_ref, bf16[576,640]{1,0:T(8,128)(2,1)S(1)} %get-tuple-element.35.refs_1_, bf16[576,640]{1,0:T(8,128)(2,1)S(1)} %collective-permute-done.5.refs_2_, bf16[576,640]{1,0:T(8,128)(2,1)S(1)} %shard_map.141.refs_3_, ...), custom_call_target="tpu_custom_call" | custom-call | tf_op jit(solution)/shard_map/pallas_call | solution.py:71
  31.5 0.0 collective-permute-done.4.value_ref
  31.5 1.2 %shard_map.144 = (bf16[576,640]{1,0:T(8,128)(2,1)S(1)}, bf16[144,640]{1,0:T(8,128)(2,1)S(1)}, bf16[144,640]{1,0:T(8,128)(2,1)S(1)}, bf16[144,640]{1,0:T(8,128)(2,1)S(1)}, bf16[144,640]{1,0:T(8,128)(2,1)S(1)}) custom-call(bf16[288,640]{1,0:T(8,128)(2,1)S(1)} %shard_map.140.first_ref, bf16[288,640]{1,0:T(8,128)(2,1)S(1)} %shard_map.143.second_ref, ...), custom_call_target="tpu_custom_call" | custom-call | tf_op jit(solution)/shard_map/pallas_call | solution.py:71
  32.7 1.0 collective-permute-done.7.value_ref
  33.6 0.1 shard_map.146
  33.7 0.1 collective-permute-start.12
  33.8 0.5 collective-permute-start.13
  34.3 0.1 collective-permute-start.10
  34.4 0.4 collective-permute-start.11
  34.8 0.4 collective-permute-done.12.refs_7_
  35.2 0.1 collective-permute-start.8
  35.3 0.1 collective-permute-done.13.refs_8_
  35.4 0.3 collective-permute-start.9
  35.7 1.4 %shard_map.147.refs_9_ = f32[576,768]{1,0:T(8,128)S(1)} custom-call(bf16[576,384]{1,0:T(8,128)(2,1)S(1)} %get-tuple-element.32.before_ref.refs_0_.query_ref, bf16[576,640]{1,0:T(8,128)(2,1)S(1)} %get-tuple-element.37.before_ref.refs_1_, f32[576,768]{1,0:T(8,128)S(1)} %shard_map.142.before_ref.refs_2_), custom_call_target="tpu_custom_call" | custom-call | tf_op jit(solution)/shard_map/pallas_call | solution.py:71
  37.1 0.0 collective-permute-done.10.refs_5_
  37.1 0.0 collective-permute-done.11.refs_6_
  37.2 0.0 collective-permute-done.8.refs_3_
  37.2 0.0 collective-permute-done.9.refs_4_
  37.2 3.3 %shard_map.148.before_ref.refs_2_ = f32[576,768]{1,0:T(8,128)S(1)} custom-call(bf16[576,384]{1,0:T(8,128)(2,1)S(1)} %get-tuple-element.32.before_ref.refs_0_.query_ref, bf16[576,640]{1,0:T(8,128)(2,1)S(1)} %get-tuple-element.37.before_ref.refs_1_, bf16[256,640]{1,0:T(8,128)(2,1)S(1)} %get-tuple-element.39.refs_2_, ...), custom_call_target="tpu_custom_call" | custom-call | tf_op jit(solution)/shard_map/pallas_call | solution.py:71
  40.5 0.2 collective-permute-done.2.value_ref
  40.6 0.2 collective-permute-start.14
  40.8 0.9 shard_map.150.acc_ref
  41.7 0.6 collective-permute-done.14.second_ref
  42.4 0.0 copy-done.4
  42.4 0.0 copy-done.12
  42.4 2.5 %shard_map.151 = (bf16[576,640]{1,0:T(8,128)(2,1)S(1)}, bf16[3072,128]{1,0:T(8,128)(2,1)S(1)}) custom-call(bf16[576,384]{1,0:T(8,128)(2,1)S(1)} %get-tuple-element.32.before_ref.refs_0_.query_ref, f32[576,768]{1,0:T(8,128)S(1)} %shard_map.150.acc_ref, bf16[320,640]{1,0:T(8,128)(2,1)S(1)} %shard_map.149.refs_1_.first_ref, ...), custom_call_target="tpu_custom_call" | custom-call | tf_op jit(solution)/shard_map/pallas_call | solution.py:71
  44.9 0.0 copy-start.5
  44.9 0.0 copy-start.6
  44.9 0.0 copy-start.7
  44.9 37.3 %all_to_all.10 = bf16[64,48,128]{2,1,0:T(8,128)(2,1)S(1)} all-to-all(bf16[64,48,128]{2,1,0:T(8,128)(2,1)S(1)} %bitcast.30), channel_id=1, replica_groups=mesh['frame'=64,'space'=4] {'frame'}, dimensions={0} | all-to-all | bytes 1572864 | tf_op jit(solution)/shard_map/all_to_all | solution.py:572
  82.3 0.0 copy-done.5
  82.3 2.3 %shard_map.152 = bf16[1536,128]{1,0:T(8,128)(2,1)S(1)} custom-call(bf16[3072,128]{1,0:T(8,128)(2,1)S(1)} %bitcast.21, bf16[320,640]{1,0:T(8,128)(2,1)S(1)} %bitcast.33, bf16[320,640]{1,0:T(8,128)(2,1)S(1)} %bitcast.34, bf16[320,640]{1,0:T(8,128)(2,1)S(1)} %bitcast.35), custom_call_target="tpu_custom_call" | custom-call | tf_op jit(solution)/shard_map/pallas_call | solution.py:71
  84.5 20.3 %all_to_all.11 = bf16[64,24,128]{2,1,0:T(8,128)(2,1)S(1)} all-to-all(bf16[64,24,128]{2,1,0:T(8,128)(2,1)S(1)} %bitcast.28), channel_id=1, replica_groups=mesh['frame'=64,'space'=4] {'frame'}, dimensions={0} | all-to-all | bytes 786432 | tf_op jit(solution)/shard_map/all_to_all | solution.py:591
  104.9 1.5 %shard_map.153 = bf16[576,640]{1,0:T(8,128)(2,1)} custom-call(bf16[1536,128]{1,0:T(8,128)(2,1)S(1)} %bitcast.29, bf16[320,640]{1,0:T(8,128)(2,1)S(1)} %copy-done.8, bf16[576,640]{1,0:T(8,128)(2,1)S(1)} %get-tuple-element.48.mixed_ref), custom_call_target="tpu_custom_call" | custom-call | tf_op jit(solution)/shard_map/pallas_call | solution.py:71
  (20 shorter events, 0.1 us)
Async XLA Ops:
  0.1 1.1 %copy-start.2 = (bf16[1,12,48,640]{3,2,1,0:T(8,128)(2,1)S(1)}, bf16[1,12,48,640]{3,2,1,0:T(8,128)(2,1)}, u32[]{:S(2)}) copy-start(bf16[1,12,48,640]{3,2,1,0:T(8,128)(2,1)} %param.14) | copy-start | bytes 2211844
  1.2 8.5 %slice-start = ((s8[7372800]{0:T(1024)(128)(4,1)}), s8[4194304]{0:T(1024)(128)(4,1)S(1)}, s32[]{:S(2)}) async-start(s8[7372800]{0:T(1024)(128)(4,1)} %bitcast.18), calls=%async_computation.2 | async-start | bytes 8388608
  2.3 1.4 %collective-permute-start = (bf16[64,640]{1,0:T(8,128)(2,1)S(1)}, bf16[64,640]{1,0:T(8,128)(2,1)S(1)}, u32[]{:S(2)}, u32[]{:S(2)}) collective-permute-start(bf16[64,640]{1,0:T(8,128)(2,1)S(1)} %get-tuple-element.28), channel_id=1, source_target_pairs={{0,1},{1,0},{2,3},{3,2},{4,5},{5,4},{6,7},{7,6},{8,9},{9,8},{10,11... | collective-permute-start | bytes 245768 | tf_op jit(solution)/shard_map/ppermute | solution.py:458
  3.6 2.0 %copy-start = (bf16[640,320]{0,1:T(8,128)(2,1)S(1)}, bf16[640,320]{0,1:T(8,128)(2,1)}, u32[]{:S(2)}) copy-start(bf16[640,320]{0,1:T(8,128)(2,1)} %param.20) | copy-start | bytes 1228804
  3.6 2.0 %copy-start.1 = (bf16[640,320]{0,1:T(8,128)(2,1)S(1)}, bf16[640,320]{0,1:T(8,128)(2,1)}, u32[]{:S(2)}) copy-start(bf16[640,320]{0,1:T(8,128)(2,1)} %param.21) | copy-start | bytes 1228804
  3.6 2.0 %copy-start.13 = (bf16[12,48,640]{2,1,0:T(8,128)(2,1)S(1)}, bf16[12,48,640]{2,1,0:T(8,128)(2,1)}, u32[]{:S(2)}) copy-start(bf16[12,48,640]{2,1,0:T(8,128)(2,1)} %param.15) | copy-start | bytes 2211844
  3.6 6.1 %slice-start.1 = ((s8[7372800]{0:T(1024)(128)(4,1)}), s8[3178496]{0:T(1024)(128)(4,1)S(1)}, s32[]{:S(2)}) async-start(s8[7372800]{0:T(1024)(128)(4,1)} %bitcast.18), calls=%async_computation.3 | async-start | bytes 6356992
  3.7 6.0 %collective-permute-start.1 = (bf16[64,640]{1,0:T(8,128)(2,1)S(1)}, bf16[64,640]{1,0:T(8,128)(2,1)S(1)}, u32[]{:S(2)}, u32[]{:S(2)}) collective-permute-start(bf16[64,640]{1,0:T(8,128)(2,1)S(1)} %get-tuple-element.31), channel_id=1, source_target_pairs={{0,3},{1,2},{2,1},{3,0},{4,7},{5,6},{6,5},{7,4},{8,11},{9,10},{10,... | collective-permute-start | bytes 245768 | tf_op jit(solution)/shard_map/ppermute | solution.py:458
  5.7 4.0 %copy-start.3 = (bf16[1,12,48,640]{3,2,1,0:T(8,128)(2,1)S(1)}, bf16[1,12,48,640]{3,2,1,0:T(8,128)(2,1)}, u32[]{:S(2)}) copy-start(bf16[1,12,48,640]{3,2,1,0:T(8,128)(2,1)} %param.14) | copy-start | bytes 2211844
  5.7 4.0 %copy-start.9 = (bf16[640,320]{0,1:T(8,128)(2,1)S(1)}, bf16[640,320]{0,1:T(8,128)(2,1)}, u32[]{:S(2)}) copy-start(bf16[640,320]{0,1:T(8,128)(2,1)} %param.19) | copy-start | bytes 1228804
  5.7 4.0 %copy-start.10 = (f32[640]{0:T(1024)S(1)}, f32[640]{0:T(1024)}, u32[]{:S(2)}) copy-start(f32[640]{0:T(1024)} %gain_ref.2) | copy-start | bytes 7684
  5.7 4.0 %copy-start.11 = (f32[640]{0:T(1024)S(1)}, f32[640]{0:T(1024)}, u32[]{:S(2)}) copy-start(f32[640]{0:T(1024)} %norm_gain_ref.1) | copy-start | bytes 7684
  7.5 12.4 %collective-permute-start.3 = (bf16[288,640]{1,0:T(8,128)(2,1)S(1)}, bf16[288,640]{1,0:T(8,128)(2,1)S(1)}, u32[]{:S(2)}, u32[]{:S(2)}) collective-permute-start(bf16[288,640]{1,0:T(8,128)(2,1)S(1)} %get-tuple-element.34), channel_id=1, source_target_pairs={{0,2},{1,3},{2,0},{3,1},{4,6},{5,7},{6,4},{7,5},{8,10},{9,11},{10,... | collective-permute-start | bytes 1105928 | tf_op jit(solution)/shard_map/ppermute | solution.py:458
  17.7 7.3 %collective-permute-start.6 = (bf16[576,640]{1,0:T(8,128)(2,1)S(1)}, bf16[576,640]{1,0:T(8,128)(2,1)S(1)}, u32[]{:S(2)}, u32[]{:S(2)}) collective-permute-start(bf16[576,640]{1,0:T(8,128)(2,1)S(1)} %shard_map.141.refs_3_), channel_id=1, source_target_pairs={{0,1},{1,0},{2,3},{3,2},{4,5},{5,4},{6,7},{7,6},{8,9},{9,8},{10,11... | collective-permute-start | bytes 2211848 | tf_op jit(solution)/shard_map/ppermute | solution.py:458
  17.9 7.1 %collective-permute-start.5 = (bf16[576,640]{1,0:T(8,128)(2,1)S(1)}, bf16[576,640]{1,0:T(8,128)(2,1)S(1)}, u32[]{:S(2)}, u32[]{:S(2)}) collective-permute-start(bf16[576,640]{1,0:T(8,128)(2,1)S(1)} %get-tuple-element.35.refs_1_), channel_id=1, source_target_pairs={{0,1},{1,0},{2,3},{3,2},{4,5},{5,4},{6,7},{7,6},{8,9},{9,8},{10,11... | collective-permute-start | bytes 2211848 | tf_op jit(solution)/shard_map/ppermute | solution.py:458
  19.9 11.6 %collective-permute-start.4 = (bf16[288,640]{1,0:T(8,128)(2,1)S(1)}, bf16[288,640]{1,0:T(8,128)(2,1)S(1)}, u32[]{:S(2)}, u32[]{:S(2)}) collective-permute-start(bf16[288,640]{1,0:T(8,128)(2,1)S(1)} %shard_map.140.first_ref), channel_id=1, source_target_pairs={{0,32},{4,36},{8,40},{12,44},{16,48},{20,52},{24,56},{28,60},{32,0... | collective-permute-start | bytes 1105928 | tf_op jit(solution)/shard_map/ppermute | solution.py:520
  21.5 12.2 %collective-permute-start.7 = (bf16[256,640]{1,0:T(8,128)(2,1)S(1)}, bf16[256,640]{1,0:T(8,128)(2,1)S(1)}, u32[]{:S(2)}, u32[]{:S(2)}) collective-permute-start(bf16[256,640]{1,0:T(8,128)(2,1)S(1)} %get-tuple-element.38), channel_id=1, source_target_pairs={{0,2},{1,3},{2,0},{3,1},{4,6},{5,7},{6,4},{7,5},{8,10},{9,11},{10,... | collective-permute-start | bytes 983048 | tf_op jit(solution)/shard_map/ppermute | solution.py:458
  22.9 17.8 %collective-permute-start.2 = (bf16[320,640]{1,0:T(8,128)(2,1)S(1)}, bf16[320,640]{1,0:T(8,128)(2,1)S(1)}, u32[]{:S(2)}, u32[]{:S(2)}) collective-permute-start(bf16[320,640]{1,0:T(8,128)(2,1)S(1)} %get-tuple-element.33), channel_id=1, source_target_pairs={{0,2},{1,3},{2,0},{3,1},{4,6},{5,7},{6,4},{7,5},{8,10},{9,11},{10,... | collective-permute-start | bytes 1228808 | tf_op jit(solution)/shard_map/ppermute | solution.py:458
  33.7 1.5 %collective-permute-start.12 = (bf16[128,640]{1,0:T(8,128)(2,1)S(1)}, bf16[128,640]{1,0:T(8,128)(2,1)S(1)}, u32[]{:S(2)}, u32[]{:S(2)}) collective-permute-start(bf16[128,640]{1,0:T(8,128)(2,1)S(1)} %get-tuple-element.44), channel_id=1, source_target_pairs={{0,1},{1,0},{2,3},{3,2},{4,5},{5,4},{6,7},{7,6},{8,9},{9,8},{10,11... | collective-permute-start | bytes 491528 | tf_op jit(solution)/shard_map/ppermute | solution.py:458
  33.8 1.6 %collective-permute-start.13 = (bf16[128,640]{1,0:T(8,128)(2,1)S(1)}, bf16[128,640]{1,0:T(8,128)(2,1)S(1)}, u32[]{:S(2)}, u32[]{:S(2)}) collective-permute-start(bf16[128,640]{1,0:T(8,128)(2,1)S(1)} %get-tuple-element.45), channel_id=1, source_target_pairs={{0,1},{1,0},{2,3},{3,2},{4,5},{5,4},{6,7},{7,6},{8,9},{9,8},{10,11... | collective-permute-start | bytes 491528 | tf_op jit(solution)/shard_map/ppermute | solution.py:458
  34.3 2.8 %collective-permute-start.10 = (bf16[144,640]{1,0:T(8,128)(2,1)S(1)}, bf16[144,640]{1,0:T(8,128)(2,1)S(1)}, u32[]{:S(2)}, u32[]{:S(2)}) collective-permute-start(bf16[144,640]{1,0:T(8,128)(2,1)S(1)} %get-tuple-element.42), channel_id=1, source_target_pairs={{0,1},{1,0},{2,3},{3,2},{4,5},{5,4},{6,7},{7,6},{8,9},{9,8},{10,11... | collective-permute-start | bytes 552968 | tf_op jit(solution)/shard_map/ppermute | solution.py:458
  34.4 2.8 %collective-permute-start.11 = (bf16[144,640]{1,0:T(8,128)(2,1)S(1)}, bf16[144,640]{1,0:T(8,128)(2,1)S(1)}, u32[]{:S(2)}, u32[]{:S(2)}) collective-permute-start(bf16[144,640]{1,0:T(8,128)(2,1)S(1)} %get-tuple-element.43), channel_id=1, source_target_pairs={{0,1},{1,0},{2,3},{3,2},{4,5},{5,4},{6,7},{7,6},{8,9},{9,8},{10,11... | collective-permute-start | bytes 552968 | tf_op jit(solution)/shard_map/ppermute | solution.py:458
  35.2 2.0 %collective-permute-start.8 = (bf16[144,640]{1,0:T(8,128)(2,1)S(1)}, bf16[144,640]{1,0:T(8,128)(2,1)S(1)}, u32[]{:S(2)}, u32[]{:S(2)}) collective-permute-start(bf16[144,640]{1,0:T(8,128)(2,1)S(1)} %get-tuple-element.40), channel_id=1, source_target_pairs={{0,1},{1,0},{2,3},{3,2},{4,5},{5,4},{6,7},{7,6},{8,9},{9,8},{10,11... | collective-permute-start | bytes 552968 | tf_op jit(solution)/shard_map/ppermute | solution.py:458
  35.4 1.8 %collective-permute-start.9 = (bf16[144,640]{1,0:T(8,128)(2,1)S(1)}, bf16[144,640]{1,0:T(8,128)(2,1)S(1)}, u32[]{:S(2)}, u32[]{:S(2)}) collective-permute-start(bf16[144,640]{1,0:T(8,128)(2,1)S(1)} %get-tuple-element.41), channel_id=1, source_target_pairs={{0,1},{1,0},{2,3},{3,2},{4,5},{5,4},{6,7},{7,6},{8,9},{9,8},{10,11... | collective-permute-start | bytes 552968 | tf_op jit(solution)/shard_map/ppermute | solution.py:458
  40.6 1.8 %copy-start.4 = (bf16[320,640]{1,0:T(8,128)(2,1)S(1)}, bf16[320,640]{1,0:T(8,128)(2,1)}, u32[]{:S(2)}) copy-start(bf16[320,640]{1,0:T(8,128)(2,1)} %weight_ref.2) | copy-start | bytes 1228804
  40.6 1.8 %copy-start.12 = (f32[640]{0:T(1024)S(1)}, f32[640]{0:T(1024)}, u32[]{:S(2)}) copy-start(f32[640]{0:T(1024)} %gain_ref.3) | copy-start | bytes 7684
  40.6 1.7 %collective-permute-start.14 = (bf16[320,640]{1,0:T(8,128)(2,1)S(1)}, bf16[320,640]{1,0:T(8,128)(2,1)S(1)}, u32[]{:S(2)}, u32[]{:S(2)}) collective-permute-start(bf16[320,640]{1,0:T(8,128)(2,1)S(1)} %shard_map.149.refs_1_.first_ref), channel_id=1, source_target_pairs={{0,1},{1,0},{2,3},{3,2},{4,5},{5,4},{6,7},{7,6},{8,9},{9,8},{10,11... | collective-permute-start | bytes 1228808 | tf_op jit(solution)/shard_map/ppermute | solution.py:458
  44.9 37.4 %copy-start.5 = (bf16[640,320]{0,1:T(8,128)(2,1)S(1)}, bf16[640,320]{0,1:T(8,128)(2,1)}, u32[]{:S(2)}) copy-start(bf16[640,320]{0,1:T(8,128)(2,1)} %param.24) | copy-start | bytes 1228804
  44.9 37.3 %copy-start.6 = (bf16[640,320]{0,1:T(8,128)(2,1)S(1)}, bf16[640,320]{0,1:T(8,128)(2,1)}, u32[]{:S(2)}) copy-start(bf16[640,320]{0,1:T(8,128)(2,1)} %param.25) | copy-start | bytes 1228804
  44.9 37.3 %copy-start.7 = (bf16[640,320]{0,1:T(8,128)(2,1)S(1)}, bf16[640,320]{0,1:T(8,128)(2,1)}, u32[]{:S(2)}) copy-start(bf16[640,320]{0,1:T(8,128)(2,1)} %param.26) | copy-start | bytes 1228804
  82.3 22.6 %copy-start.8 = (bf16[320,640]{1,0:T(8,128)(2,1)S(1)}, bf16[320,640]{1,0:T(8,128)(2,1)}, u32[]{:S(2)}) copy-start(bf16[320,640]{1,0:T(8,128)(2,1)} %weight_ref.3) | copy-start | bytes 1228804

commit v3 on v2

--- a/solution.py
+++ b/solution.py
@@ -20,11 +20,10 @@
 LANES = 128
 SENT = 48
 TILE = 768
-HEAD = 512
-FIRST = 256
+EARLY = 224
+HEAD = 48
+FIRST = 320
 PART = CELLS // 2
-CHUNK = CELLS // 4
-TAIL = 256
 BACK = 24
 
 epsilon = 1e-05
@@ -67,7 +66,7 @@
     single = not isinstance(outs, (list, tuple))
     specs = [pl.BlockSpec(memory_space=pltpu.SMEM)] * smem + vmem(len(operands) - smem)
     for i in anywhere:
-        specs[i] = pl.BlockSpec(memory_space=pltpu.HBM)
+        specs[i] = pl.BlockSpec(memory_space=pl.ANY)
     return pl.pallas_call(
         body,
         out_shape=outs,
@@ -134,31 +133,26 @@
     return dot_t(normed, weight[...]).astype(bf16)
 
 
-def own_reference_kernel(
+def reference_kernel(
     flags_ref, states_ref, before_ref, key_ref, value_ref, out_ref, half_ref, weight
 ):
-    half = CELLS // 2
-    half_ref[...] = jnp.where(flags_ref[0, 3] > 0.5, states_ref[half:, :], states_ref[0:half, :])
     weight[0:INNER, :] = key_ref[...]
     weight[INNER:, :] = value_ref[...]
     out_ref[...] = reference_kv(weight, states_ref[...])
-
-
-def far_reference_kernel(first_ref, second_ref, key_ref, value_ref, out_ref, *refs):
-    chunk_refs, weight = refs[:-1], refs[-1]
+    half_ref[...] = jnp.where(flags_ref[0, 3] > 0.5, out_ref[PART:, :], out_ref[0:PART, :])
+
+
+def parts_kernel(first_ref, second_ref, before_ref, *part_refs):
+    for i, part_ref in enumerate(part_refs):
+        ref = (first_ref, second_ref)[i // 2]
+        size = part_ref.shape[0]
+        part_ref[...] = ref[i % 2 * size : (i % 2 + 1) * size, :]
+
+
+def joined_weights(weight, key_ref, value_ref, query_ref):
     weight[0:INNER, :] = key_ref[...]
-    weight[INNER:, :] = value_ref[...]
-    for i, ref in enumerate((first_ref, second_ref)):
-        out_ref[i * PART : (i + 1) * PART, :] = reference_kv(weight, ref[...])
-    for i, ref in enumerate(chunk_refs):
-        ref[...] = out_ref[i * CHUNK : (i + 1) * CHUNK, :]
-
-
-def parts_kernel(value_ref, out_ref, *part_refs):
-    out_ref[...] = value_ref[...]
-    size = FIRST // len(part_refs)
-    for i, ref in enumerate(part_refs):
-        ref[...] = value_ref[i * size : (i + 1) * size, :]
+    weight[INNER:C, :] = value_ref[...]
+    weight[C:, :] = query_ref[...]
 
 
 def conv_kernel(
@@ -176,13 +170,14 @@
     hidden_out,
     query_out,
     kv_out,
+    low_out,
+    high_out,
     first_out,
     second_out,
     lhs,
     weight,
 ):
-    weight[0:INNER, :] = key_ref[...]
-    weight[INNER:, :] = value_ref[...]
+    joined_weights(weight, key_ref, value_ref, query_ref)
     group_sum, group_sq = sums_of(far_ref[W:, :].astype(f32))
     members = float(4 * CELLS * (C // GROUPS))
     average = (group_sum + sums_ref[0:1]) / members
@@ -214,11 +209,14 @@
             total = part if total is None else total + part
         hidden_out[rows, :] = (x_ref[rows, :].astype(f32) + total).astype(bf16)
     normed = layer_norm(hidden_out[...].astype(f32), norm_gain_ref[...].reshape(1, C)).astype(bf16)
-    kv = dot_t(normed, weight[...]).astype(bf16)
+    projected = dot_t(normed, weight[...])
+    kv = projected[:, 0:C].astype(bf16)
     kv_out[...] = kv
+    low_out[...] = kv[0:PART]
+    high_out[...] = kv[PART:]
     first_out[...] = kv[0:FIRST]
     second_out[...] = kv[FIRST:]
-    query_out[:, 0:INNER] = (dot_t(normed, query_ref[...]) * QUERY_SCALE).astype(bf16)
+    query_out[:, 0:INNER] = (projected[:, C:] * QUERY_SCALE).astype(bf16)
     query_out[:, INNER:] = jnp.zeros((CELLS, 64), bf16)
 
 
@@ -292,11 +290,9 @@
 
 
 def last_attention_kernel(
-    ranges,
     query_ref,
     acc_ref,
-    first_ref,
-    second_ref,
+    kv_ref,
     hidden_ref,
     weight_ref,
     gain_ref,
@@ -304,16 +300,12 @@
     sent_out,
     rows,
     weight,
-    scratch,
 ):
-    kv_ref = joined((first_ref, second_ref), ranges, scratch)
     weight[0:64, :] = jnp.zeros((64, C), bf16)
     weight[64:, :] = weight_ref[...]
     blocks = normalised(attend(query_ref[...], kv_ref, starting(acc_ref)))
-    update = None
-    for b in range(3):
-        part = dot(blocks[b].astype(bf16), weight[b * LANES : (b + 1) * LANES, :])
-        update = part if update is None else update + part
+    attended = jnp.concatenate([block.astype(bf16) for block in blocks], axis=1)
+    update = dot(attended, weight[...])
     mixed = (hidden_ref[...].astype(f32) + update).astype(bf16)
     mixed_out[...] = mixed
     framed = layer_norm(mixed.astype(f32), gain_ref[...].reshape(1, C))
@@ -333,8 +325,7 @@
 def temporal_kernel(
     got_ref, query_ref, key_ref, value_ref, out_ref, rows, tokens, result, weight
 ):
-    weight[0:INNER, :] = key_ref[...]
-    weight[INNER:, :] = value_ref[...]
+    joined_weights(weight, key_ref, value_ref, query_ref)
     for g in range(FRAMES):
         rows[g * (SENT + 1) : g * (SENT + 1) + SENT, :] = got_ref[
             g * SENT : (g + 1) * SENT, :
@@ -344,9 +335,10 @@
             tokens[j * FRAMES : (j + 1) * FRAMES, c * LANES : (c + 1) * LANES] = rows[
                 pl.ds(j * 5 + c, FRAMES, stride=SENT + 1), :
             ].astype(bf16)
-    query = (dot_t(tokens[...], query_ref[...]) * QUERY_SCALE).astype(bf16)
+    projected = dot_t(tokens[...], weight[...])
+    query = (projected[:, C:] * QUERY_SCALE).astype(bf16)
     query = jnp.concatenate([query, jnp.zeros((CELLS, 64), bf16)], axis=1)
-    kv = dot_t(tokens[...], weight[...]).astype(bf16)
+    kv = projected[:, 0:C].astype(bf16)
     span = 3 * FRAMES
     row_place = lax.broadcasted_iota(jnp.int32, (span, span), 0) // FRAMES
     column_place = lax.broadcasted_iota(jnp.int32, (span, span), 1) // FRAMES
@@ -475,7 +467,7 @@
     far = swap(far, 3)
 
     ref_kv, half = call(
-        own_reference_kernel,
+        reference_kernel,
         [struct((CELLS, C), bf16), struct((CELLS // 2, C), bf16)],
         [flags, states, sums, spatial_key.T, spatial_value.T],
         scratch=[pltpu.VMEM((C, C), bf16)],
@@ -485,12 +477,14 @@
     )
     half = swap(half, 2)
 
-    hidden, query, kv, first, second = call(
+    hidden, query, kv, low, high, first, second = call(
         conv_kernel,
         [
             struct((CELLS, C), bf16),
             struct((CELLS, 384), bf16),
             struct((CELLS, C), bf16),
+            struct((PART, C), bf16),
+            struct((PART, C), bf16),
             struct((FIRST, C), bf16),
             struct((CELLS - FIRST, C), bf16),
         ],
@@ -509,18 +503,19 @@
         ],
         scratch=[
             pltpu.VMEM(((STRIP + 2) * W, 3 * C), bf16),
-            pltpu.VMEM((C, C), bf16),
+            pltpu.VMEM((C + INNER, C), bf16),
         ],
         smem=1,
         limit=16,
     )
-    ref_kv = after(ref_kv, query)
+
     ref_near = swap(ref_kv, 1)
     half = after(half, query)
     other_half = lax.ppermute(half, "frame", [(f, f ^ 8) for f in range(FRAMES)])
+    half_near = swap(half, 1)
     first = swap(first, 2)
     second = swap(second, 2)
-    kv_near = swap(kv, 1)
+    kv_near = [swap(low, 1), swap(high, 1)]
 
     def attention(kv_parts, start):
         ranges = [(low, high) for _, low, high in kv_parts]
@@ -533,39 +528,34 @@
             limit=16,
         )
 
-    acc = attention([(part, 0, CELLS) for part in (kv, kv_near, ref_kv, ref_near)], None)
-    chunk = struct((CHUNK, C), bf16)
-    ref_far, *ref_far_near = call(
-        far_reference_kernel,
-        [struct((CELLS, C), bf16)] + [chunk] * (CELLS // CHUNK),
-        [half, after(other_half, acc), spatial_key.T, spatial_value.T],
-        scratch=[pltpu.VMEM((C, C), bf16)],
-    )
-    ref_far_near = [swap(part, 1) for part in ref_far_near]
-    first, *first_near = call(
+    acc = attention(
+        [(part, 0, part.shape[0]) for part in (kv, *kv_near, ref_kv, ref_near, half)]
+        + [(half_near, 0, EARLY)],
+        None,
+    )
+    sizes = (PART // 2, PART // 2, FIRST // 2, FIRST // 2)
+    parts = call(
         parts_kernel,
-        [struct((FIRST, C), bf16)] + [struct((FIRST // 2, C), bf16)] * 2,
-        [after(first, ref_far)],
-    )
-    first_near = [swap(part, 1) for part in first_near]
-    acc = attention([(ref_far, 0, HEAD)], acc)
+        [struct((size, C), bf16) for size in sizes],
+        [other_half, first, acc],
+        anywhere=(2,),
+    )
+    near_parts = [swap(part, 1) for part in parts]
     acc = attention(
-        [(ref_far, HEAD, CELLS), (first, 0, FIRST)]
-        + [(part, 0, part.shape[0]) for part in ref_far_near + first_near],
-        acc,
-    )
+        [(half_near, EARLY, PART), (parts[0], 0, PART // 2), (parts[1], 0, HEAD)], acc
+    )
+    rest = [parts[1], *near_parts[:2], *parts[2:], *near_parts[2:]]
+    acc = attention([(part, HEAD if i == 0 else 0, part.shape[0]) for i, part in enumerate(rest)], acc)
     second = after(second, acc)
     second_near = swap(second, 1)
-    acc = attention([(second, 0, TAIL)], acc)
-    ranges = [(TAIL, CELLS - FIRST), (0, CELLS - FIRST)]
+    acc = attention([(second, 0, CELLS - FIRST)], acc)
     mixed, sent = call(
-        functools.partial(last_attention_kernel, ranges),
+        last_attention_kernel,
         [struct((CELLS, C), bf16), struct((FRAMES * SENT, LANES), bf16)],
-        [query, acc, second, second_near, hidden, spatial_out, frame_gain],
+        [query, acc, second_near, hidden, spatial_out, frame_gain],
         scratch=[
             pltpu.VMEM((FRAMES * (SENT + 1), LANES), f32),
             pltpu.VMEM((384, C), bf16),
-            pltpu.VMEM((2 * (CELLS - FIRST) - TAIL, C), bf16),
         ],
         limit=16,
     )
@@ -585,7 +575,7 @@
             pltpu.VMEM((FRAMES * (SENT + 1), LANES), f32),
             pltpu.VMEM((CELLS, C), bf16),
             pltpu.VMEM((CELLS, 384), f32),
-            pltpu.VMEM((C, C), bf16),
+            pltpu.VMEM((C + INNER, C), bf16),
         ],
     )
     returned = lax.all_to_all(

time: 107 us -> 103 us (0.963)
  Pallas kernels: 30.4 us -> 28.5 us
    pallas_call x13 -> x12, Pallas kernels: 30.4 us -> 28.5 us  [call(): pl.pallas_call(body, out_shape=outs, in_specs=specs, out_specs=vmem(1)[0]...]
  transfers between devices with their start and end apart: 15 -> 15, of which waited for: 8 -> 7; matrix products, arithmetic and copies ran while one was open for 0% -> 0% of each run, Pallas kernels for 22% -> 21%
where the time goes in v3:
time: 103 us
  blocking collectives  57.7 us (56%)
  Pallas kernels  28.5 us (28%)
  starting transfers between devices  10.5 us (10%)
  waiting for transfers between devices  4.86 us (5%)
  local copies, waits for them, and re-layouts  1.18 us (1%)
    all_to_all x1, blocking collectives, on_device(): lax.all_to_all(sent.reshape(FRAMES, SENT, LANES), 'frame', split_axis=0,...  37.5 us
    pallas_call x12, Pallas kernels, call(): pl.pallas_call(body, out_shape=outs, in_specs=specs, out_specs=vmem(1)[0]...  28.5 us
    all_to_all x1, blocking collectives, on_device(): lax.all_to_all(back.reshape(FRAMES, BACK, LANES), 'frame', split_axis=0,...  20.2 us
    ppermute x14, starting transfers between devices, swap(): return lax.ppermute(value, 'space', [(i, i ^ k) for i in range(4)])  8.86 us
    ppermute x14, waiting for transfers between devices, swap(): return lax.ppermute(value, 'space', [(i, i ^ k) for i in range(4)])  4.86 us
  transfers between devices with their start and end apart: 15, of which 7 were waited for; matrix products, arithmetic and copies ran while one was open for 0% of the time, Pallas kernels for 21%

profile of v3, /device:TPU:2, one launch (start us, length us, event | category | flops | bytes accessed | tf_op | source)
XLA Modules:
  0.0 103.0 jit_solution(8754410962781057718)
XLA Ops:
  0.0 0.1 add_convert_fusion.flags_ref
  0.1 1.1 %copy-done = bf16[1,12,48,640]{3,2,1,0:T(8,128)(2,1)S(1)} copy-done((bf16[1,12,48,640]{3,2,1,0:T(8,128)(2,1)S(1)}, bf16[1,12,48,640]{3,2,1,0:T(8,128)(2,1)}, u32[]{:S(2)}) %copy-start) | copy-done | bytes 737304
  1.2 1.1 %shard_map.136 = (f32[8,640]{1,0:T(8,128)S(1)}, bf16[64,640]{1,0:T(8,128)(2,1)S(1)}, bf16[48,640]{1,0:T(8,128)(2,1)S(1)}) custom-call(f32[1,4]{1,0:T(1,128)S(1)} %add_convert_fusion.flags_ref, bf16[576,640]{1,0:T(8,128)(2,1)S(1)} %bitcast.25), custom_call_target="tpu_custom_call" | custom-call | flops 2000000000 | tf_op jit(solution)/shard_map/pallas_call | solution.py:70
  2.3 0.1 collective-permute-start
  2.4 1.3 %collective-permute-done.near_ref = bf16[64,640]{1,0:T(8,128)(2,1)S(1)} collective-permute-done((bf16[64,640]{1,0:T(8,128)(2,1)S(1)}, bf16[64,640]{1,0:T(8,128)(2,1)S(1)}, u32[]{:S(2)}, u32[]{:S(2)}) %collective-permute-start) | collective-permute-done | bytes 81952 | tf_op jit(solution)/shard_map/ppermute | solution.py:450
  3.7 2.0 %collective-permute-start.1 = (bf16[64,640]{1,0:T(8,128)(2,1)S(1)}, bf16[64,640]{1,0:T(8,128)(2,1)S(1)}, u32[]{:S(2)}, u32[]{:S(2)}) collective-permute-start(bf16[64,640]{1,0:T(8,128)(2,1)S(1)} %get-tuple-element.29), channel_id=1, source_target_pairs={{0,3},{1,2},{2,1},{3,0},{4,7},{5,6},{6,5},{7,4},{8,11},{9,10},{10,... | collective-permute-start | bytes 245768 | tf_op jit(solution)/shard_map/ppermute | solution.py:450
  5.7 0.0 copy-done.8
  5.7 0.0 copy-done.9
  5.7 0.0 copy-done.13
  5.7 0.0 copy-start.7
  5.7 0.0 copy-start.10
  5.7 0.0 copy-start.11
  5.7 1.7 %shard_map.139 = (bf16[576,640]{1,0:T(8,128)(2,1)S(1)}, bf16[288,640]{1,0:T(8,128)(2,1)S(1)}) custom-call(f32[1,4]{1,0:T(1,128)S(1)} %add_convert_fusion.flags_ref, bf16[576,640]{1,0:T(8,128)(2,1)S(1)} %bitcast.35, f32[8,640]{1,0:T(8,128)S(1)} %get-tuple-element.28.sums_ref.before_ref, bf16[320,640]{1,0:T(8,128)(2,1)S(1)} %bitcast.31, ...), custom_call_target="tpu_custom_call" | custom-call | flops 2000000000 | tf_op jit(solution)/shard_map/pallas_call | solution.py:70
  7.4 1.5 %collective-permute-start.3 = (bf16[288,640]{1,0:T(8,128)(2,1)S(1)}, bf16[288,640]{1,0:T(8,128)(2,1)S(1)}, u32[]{:S(2)}, u32[]{:S(2)}) collective-permute-start(bf16[288,640]{1,0:T(8,128)(2,1)S(1)} %get-tuple-element.32), channel_id=1, source_target_pairs={{0,2},{1,3},{2,0},{3,1},{4,6},{5,7},{6,4},{7,5},{8,10},{9,11},{10,... | collective-permute-start | bytes 1105928 | tf_op jit(solution)/shard_map/ppermute | solution.py:450
  9.0 0.1 collective-permute-start.8
  9.0 0.7 collective-permute-done.1.far_ref
  9.7 0.0 slice-done
  9.7 0.0 slice-done.1
  9.7 0.0 copy-done.1
  9.7 0.0 copy-done.7
  9.7 0.0 copy-done.10
  9.7 0.0 copy-done.11
  9.7 7.8 %shard_map.138 = (bf16[576,640]{1,0:T(8,128)(2,1)S(1)}, bf16[576,384]{1,0:T(8,128)(2,1)S(1)}, bf16[576,640]{1,0:T(8,128)(2,1)S(1)}, bf16[288,640]{1,0:T(8,128)(2...) custom-call(f32[1,4]{1,0:T(1,128)S(1)} %add_convert_fusion.flags_ref, ...), custom_call_target="tpu_custom_call" | custom-call | tf_op jit(solution)/shard_map/pallas_call | solution.py:70
  17.5 0.2 collective-permute-start.6
  17.8 0.4 collective-permute-start.7
  18.1 2.1 %collective-permute-start.5 = (bf16[320,640]{1,0:T(8,128)(2,1)S(1)}, bf16[320,640]{1,0:T(8,128)(2,1)S(1)}, u32[]{:S(2)}, u32[]{:S(2)}) collective-permute-start(bf16[320,640]{1,0:T(8,128)(2,1)S(1)} %get-tuple-element.33), channel_id=1, source_target_pairs={{0,2},{1,3},{2,0},{3,1},{4,6},{5,7},{6,4},{7,5},{8,10},{9,11},{10,... | collective-permute-start | bytes 1228808 | tf_op jit(solution)/shard_map/ppermute | solution.py:450
  20.3 0.0 collective-permute-done.3.value_ref
  20.3 0.0 collective-permute-start.9
  20.3 0.0 collective-permute-done.6.refs_2_
  20.3 1.7 %collective-permute-start.4 = (bf16[288,640]{1,0:T(8,128)(2,1)S(1)}, bf16[288,640]{1,0:T(8,128)(2,1)S(1)}, u32[]{:S(2)}, u32[]{:S(2)}) collective-permute-start(bf16[288,640]{1,0:T(8,128)(2,1)S(1)} %shard_map.140.refs_6_), channel_id=1, source_target_pairs={{0,32},{4,36},{8,40},{12,44},{16,48},{20,52},{24,56},{28,60},{32,0... | collective-permute-start | bytes 1105928 | tf_op jit(solution)/shard_map/ppermute | solution.py:514
  22.0 0.0 collective-permute-done.7.refs_3_
  22.0 1.4 %collective-permute-start.2 = (bf16[256,640]{1,0:T(8,128)(2,1)S(1)}, bf16[256,640]{1,0:T(8,128)(2,1)S(1)}, u32[]{:S(2)}, u32[]{:S(2)}) collective-permute-start(bf16[256,640]{1,0:T(8,128)(2,1)S(1)} %get-tuple-element.31), channel_id=1, source_target_pairs={{0,2},{1,3},{2,0},{3,1},{4,6},{5,7},{6,4},{7,5},{8,10},{9,11},{10,... | collective-permute-start | bytes 983048 | tf_op jit(solution)/shard_map/ppermute | solution.py:450
  23.3 0.0 collective-permute-done.9.refs_7_.refs_1_
  23.3 0.0 collective-permute-done.8.refs_5_
  23.4 7.7 %shard_map.141.before_ref.refs_4_ = f32[576,768]{1,0:T(8,128)S(1)} custom-call(bf16[576,384]{1,0:T(8,128)(2,1)S(1)} %get-tuple-element.30.before_ref.refs_0_.query_ref, bf16[576,640]{1,0:T(8,128)(2,1)S(1)} %get-tuple-element.34.refs_1_, bf16[288,640]{1,0:T(8,128)(2,1)S(1)} %collective-permute-done.6.refs_2_, ...), custom_call_target="tpu_custom_call" | custom-call | tf_op jit(solution)/shard_map/pallas_call | solution.py:70
  31.1 0.9 collective-permute-done.5.second_ref
  31.9 0.0 collective-permute-done.4.first_ref
  32.0 0.1 shard_map.142
  32.0 0.1 collective-permute-start.12
  32.1 0.5 collective-permute-start.13
  32.6 0.1 collective-permute-start.10
  32.7 0.4 collective-permute-start.11
  33.1 0.9 shard_map.143.refs_8_
  34.0 0.1 collective-permute-done.10.refs_2_
  34.1 0.3 collective-permute-done.11.refs_3_
  34.4 0.0 collective-permute-done.12.refs_6_
  34.4 0.0 collective-permute-done.13.refs_7_
  34.4 2.8 %shard_map.144.before_ref.refs_2_ = f32[576,768]{1,0:T(8,128)S(1)} custom-call(bf16[576,384]{1,0:T(8,128)(2,1)S(1)} %get-tuple-element.30.before_ref.refs_0_.query_ref, bf16[144,640]{1,0:T(8,128)(2,1)S(1)} %get-tuple-element.38.refs_3_.refs_1_, bf16[144,640]{1,0:T(8,128)(2,1)S(1)} %collective-permute-done.10.refs_2_, ...), custom_call_target="tpu_custom_call" | custom-call | tf_op jit(solution)/shard_map/pallas_call | solution.py:70
  37.2 1.0 collective-permute-done.2.value_ref
  38.2 0.0 collective-permute-start.14
  38.2 0.9 shard_map.146.acc_ref
  39.1 0.7 collective-permute-done.14.kv_ref
  39.8 0.0 copy-done.5
  39.8 0.0 copy-done.12
  39.8 0.0 copy-start.4
  39.8 1.8 %shard_map.147 = (bf16[576,640]{1,0:T(8,128)(2,1)S(1)}, bf16[3072,128]{1,0:T(8,128)(2,1)S(1)}) custom-call(bf16[576,384]{1,0:T(8,128)(2,1)S(1)} %get-tuple-element.30.before_ref.refs_0_.query_ref, f32[576,768]{1,0:T(8,128)S(1)} %shard_map.146.acc_ref, bf16[256,640]{1,0:T(8,128)(2,1)S(1)} %collective-permute-done.14.kv_ref, ...), custom_call_target="tpu_custom_call" | custom-call | tf_op jit(solution)/shard_map/pallas_call | solution.py:70
  41.7 37.5 %all_to_all.10 = bf16[64,48,128]{2,1,0:T(8,128)(2,1)S(1)} all-to-all(bf16[64,48,128]{2,1,0:T(8,128)(2,1)S(1)} %bitcast.24), channel_id=1, replica_groups=mesh['frame'=64,'space'=4] {'frame'}, dimensions={0} | all-to-all | bytes 1572864 | tf_op jit(solution)/shard_map/all_to_all | solution.py:562
  79.2 0.0 copy-done.2
  79.2 0.0 copy-done.3
  79.2 0.0 copy-done.4
  79.2 2.1 %shard_map.148 = bf16[1536,128]{1,0:T(8,128)(2,1)S(1)} custom-call(bf16[3072,128]{1,0:T(8,128)(2,1)S(1)} %bitcast.21, bf16[320,640]{1,0:T(8,128)(2,1)S(1)} %bitcast.27, bf16[320,640]{1,0:T(8,128)(2,1)S(1)} %bitcast.28, bf16[320,640]{1,0:T(8,128)(2,1)S(1)} %bitcast.29), custom_call_target="tpu_custom_call" | custom-call | tf_op jit(solution)/shard_map/pallas_call | solution.py:70
  81.3 20.2 %all_to_all.11 = bf16[64,24,128]{2,1,0:T(8,128)(2,1)S(1)} all-to-all(bf16[64,24,128]{2,1,0:T(8,128)(2,1)S(1)} %bitcast.22), channel_id=1, replica_groups=mesh['frame'=64,'space'=4] {'frame'}, dimensions={0} | all-to-all | bytes 786432 | tf_op jit(solution)/shard_map/all_to_all | solution.py:581
  101.5 0.0 copy-done.6
  101.5 1.5 %shard_map.149 = bf16[576,640]{1,0:T(8,128)(2,1)} custom-call(bf16[1536,128]{1,0:T(8,128)(2,1)S(1)} %bitcast.23, bf16[320,640]{1,0:T(8,128)(2,1)S(1)} %copy-done.6, bf16[576,640]{1,0:T(8,128)(2,1)S(1)} %get-tuple-element.44.mixed_ref), custom_call_target="tpu_custom_call" | custom-call | tf_op jit(solution)/shard_map/pallas_call | solution.py:70
  (16 shorter events, 0.1 us)
Async XLA Ops:
  0.1 1.1 %copy-start = (bf16[1,12,48,640]{3,2,1,0:T(8,128)(2,1)S(1)}, bf16[1,12,48,640]{3,2,1,0:T(8,128)(2,1)}, u32[]{:S(2)}) copy-start(bf16[1,12,48,640]{3,2,1,0:T(8,128)(2,1)} %param.14) | copy-start | bytes 2211844
  1.2 8.5 %slice-start = ((s8[7372800]{0:T(1024)(128)(4,1)}), s8[4194304]{0:T(1024)(128)(4,1)S(1)}, s32[]{:S(2)}) async-start(s8[7372800]{0:T(1024)(128)(4,1)} %bitcast.18), calls=%async_computation.2 | async-start | bytes 8388608
  2.3 1.4 %collective-permute-start = (bf16[64,640]{1,0:T(8,128)(2,1)S(1)}, bf16[64,640]{1,0:T(8,128)(2,1)S(1)}, u32[]{:S(2)}, u32[]{:S(2)}) collective-permute-start(bf16[64,640]{1,0:T(8,128)(2,1)S(1)} %get-tuple-element.26), channel_id=1, source_target_pairs={{0,1},{1,0},{2,3},{3,2},{4,5},{5,4},{6,7},{7,6},{8,9},{9,8},{10,11... | collective-permute-start | bytes 245768 | tf_op jit(solution)/shard_map/ppermute | solution.py:450
  3.6 2.0 %copy-start.8 = (bf16[640,320]{0,1:T(8,128)(2,1)S(1)}, bf16[640,320]{0,1:T(8,128)(2,1)}, u32[]{:S(2)}) copy-start(bf16[640,320]{0,1:T(8,128)(2,1)} %param.20) | copy-start | bytes 1228804
  3.6 2.0 %copy-start.9 = (bf16[640,320]{0,1:T(8,128)(2,1)S(1)}, bf16[640,320]{0,1:T(8,128)(2,1)}, u32[]{:S(2)}) copy-start(bf16[640,320]{0,1:T(8,128)(2,1)} %param.21) | copy-start | bytes 1228804
  3.6 2.0 %copy-start.13 = (bf16[12,48,640]{2,1,0:T(8,128)(2,1)S(1)}, bf16[12,48,640]{2,1,0:T(8,128)(2,1)}, u32[]{:S(2)}) copy-start(bf16[12,48,640]{2,1,0:T(8,128)(2,1)} %param.15) | copy-start | bytes 2211844
  3.6 6.1 %slice-start.1 = ((s8[7372800]{0:T(1024)(128)(4,1)}), s8[3178496]{0:T(1024)(128)(4,1)S(1)}, s32[]{:S(2)}) async-start(s8[7372800]{0:T(1024)(128)(4,1)} %bitcast.18), calls=%async_computation.3 | async-start | bytes 6356992
  3.7 6.0 %collective-permute-start.1 = (bf16[64,640]{1,0:T(8,128)(2,1)S(1)}, bf16[64,640]{1,0:T(8,128)(2,1)S(1)}, u32[]{:S(2)}, u32[]{:S(2)}) collective-permute-start(bf16[64,640]{1,0:T(8,128)(2,1)S(1)} %get-tuple-element.29), channel_id=1, source_target_pairs={{0,3},{1,2},{2,1},{3,0},{4,7},{5,6},{6,5},{7,4},{8,11},{9,10},{10,... | collective-permute-start | bytes 245768 | tf_op jit(solution)/shard_map/ppermute | solution.py:450
  5.7 4.0 %copy-start.1 = (bf16[1,12,48,640]{3,2,1,0:T(8,128)(2,1)S(1)}, bf16[1,12,48,640]{3,2,1,0:T(8,128)(2,1)}, u32[]{:S(2)}) copy-start(bf16[1,12,48,640]{3,2,1,0:T(8,128)(2,1)} %param.14) | copy-start | bytes 2211844
  5.7 4.0 %copy-start.7 = (bf16[640,320]{0,1:T(8,128)(2,1)S(1)}, bf16[640,320]{0,1:T(8,128)(2,1)}, u32[]{:S(2)}) copy-start(bf16[640,320]{0,1:T(8,128)(2,1)} %param.19) | copy-start | bytes 1228804
  5.7 4.0 %copy-start.10 = (f32[640]{0:T(1024)S(1)}, f32[640]{0:T(1024)}, u32[]{:S(2)}) copy-start(f32[640]{0:T(1024)} %gain_ref.2) | copy-start | bytes 7684
  5.7 4.0 %copy-start.11 = (f32[640]{0:T(1024)S(1)}, f32[640]{0:T(1024)}, u32[]{:S(2)}) copy-start(f32[640]{0:T(1024)} %norm_gain_ref.1) | copy-start | bytes 7684
  7.4 12.8 %collective-permute-start.3 = (bf16[288,640]{1,0:T(8,128)(2,1)S(1)}, bf16[288,640]{1,0:T(8,128)(2,1)S(1)}, u32[]{:S(2)}, u32[]{:S(2)}) collective-permute-start(bf16[288,640]{1,0:T(8,128)(2,1)S(1)} %get-tuple-element.32), channel_id=1, source_target_pairs={{0,2},{1,3},{2,0},{3,1},{4,6},{5,7},{6,4},{7,5},{8,10},{9,11},{10,... | collective-permute-start | bytes 1105928 | tf_op jit(solution)/shard_map/ppermute | solution.py:450
  9.0 14.4 %collective-permute-start.8 = (bf16[576,640]{1,0:T(8,128)(2,1)S(1)}, bf16[576,640]{1,0:T(8,128)(2,1)S(1)}, u32[]{:S(2)}, u32[]{:S(2)}) collective-permute-start(bf16[576,640]{1,0:T(8,128)(2,1)S(1)} %get-tuple-element.37.refs_4_), channel_id=1, source_target_pairs={{0,1},{1,0},{2,3},{3,2},{4,5},{5,4},{6,7},{7,6},{8,9},{9,8},{10,11... | collective-permute-start | bytes 2211848 | tf_op jit(solution)/shard_map/ppermute | solution.py:450
  17.5 2.7 %collective-permute-start.6 = (bf16[288,640]{1,0:T(8,128)(2,1)S(1)}, bf16[288,640]{1,0:T(8,128)(2,1)S(1)}, u32[]{:S(2)}, u32[]{:S(2)}) collective-permute-start(bf16[288,640]{1,0:T(8,128)(2,1)S(1)} %get-tuple-element.35), channel_id=1, source_target_pairs={{0,1},{1,0},{2,3},{3,2},{4,5},{5,4},{6,7},{7,6},{8,9},{9,8},{10,11... | collective-permute-start | bytes 1105928 | tf_op jit(solution)/shard_map/ppermute | solution.py:450
  17.8 4.2 %collective-permute-start.7 = (bf16[288,640]{1,0:T(8,128)(2,1)S(1)}, bf16[288,640]{1,0:T(8,128)(2,1)S(1)}, u32[]{:S(2)}, u32[]{:S(2)}) collective-permute-start(bf16[288,640]{1,0:T(8,128)(2,1)S(1)} %get-tuple-element.36), channel_id=1, source_target_pairs={{0,1},{1,0},{2,3},{3,2},{4,5},{5,4},{6,7},{7,6},{8,9},{9,8},{10,11... | collective-permute-start | bytes 1105928 | tf_op jit(solution)/shard_map/ppermute | solution.py:450
  18.1 13.8 %collective-permute-start.5 = (bf16[320,640]{1,0:T(8,128)(2,1)S(1)}, bf16[320,640]{1,0:T(8,128)(2,1)S(1)}, u32[]{:S(2)}, u32[]{:S(2)}) collective-permute-start(bf16[320,640]{1,0:T(8,128)(2,1)S(1)} %get-tuple-element.33), channel_id=1, source_target_pairs={{0,2},{1,3},{2,0},{3,1},{4,6},{5,7},{6,4},{7,5},{8,10},{9,11},{10,... | collective-permute-start | bytes 1228808 | tf_op jit(solution)/shard_map/ppermute | solution.py:450
  20.3 3.1 %collective-permute-start.9 = (bf16[288,640]{1,0:T(8,128)(2,1)S(1)}, bf16[288,640]{1,0:T(8,128)(2,1)S(1)}, u32[]{:S(2)}, u32[]{:S(2)}) collective-permute-start(bf16[288,640]{1,0:T(8,128)(2,1)S(1)} %shard_map.140.refs_6_), channel_id=1, source_target_pairs={{0,1},{1,0},{2,3},{3,2},{4,5},{5,4},{6,7},{7,6},{8,9},{9,8},{10,11... | collective-permute-start | bytes 1105928 | tf_op jit(solution)/shard_map/ppermute | solution.py:450
  20.3 11.7 %collective-permute-start.4 = (bf16[288,640]{1,0:T(8,128)(2,1)S(1)}, bf16[288,640]{1,0:T(8,128)(2,1)S(1)}, u32[]{:S(2)}, u32[]{:S(2)}) collective-permute-start(bf16[288,640]{1,0:T(8,128)(2,1)S(1)} %shard_map.140.refs_6_), channel_id=1, source_target_pairs={{0,32},{4,36},{8,40},{12,44},{16,48},{20,52},{24,56},{28,60},{32,0... | collective-permute-start | bytes 1105928 | tf_op jit(solution)/shard_map/ppermute | solution.py:514
  22.0 16.2 %collective-permute-start.2 = (bf16[256,640]{1,0:T(8,128)(2,1)S(1)}, bf16[256,640]{1,0:T(8,128)(2,1)S(1)}, u32[]{:S(2)}, u32[]{:S(2)}) collective-permute-start(bf16[256,640]{1,0:T(8,128)(2,1)S(1)} %get-tuple-element.31), channel_id=1, source_target_pairs={{0,2},{1,3},{2,0},{3,1},{4,6},{5,7},{6,4},{7,5},{8,10},{9,11},{10,... | collective-permute-start | bytes 983048 | tf_op jit(solution)/shard_map/ppermute | solution.py:450
  32.0 2.4 %collective-permute-start.12 = (bf16[160,640]{1,0:T(8,128)(2,1)S(1)}, bf16[160,640]{1,0:T(8,128)(2,1)S(1)}, u32[]{:S(2)}, u32[]{:S(2)}) collective-permute-start(bf16[160,640]{1,0:T(8,128)(2,1)S(1)} %get-tuple-element.40.refs_4_), channel_id=1, source_target_pairs={{0,1},{1,0},{2,3},{3,2},{4,5},{5,4},{6,7},{7,6},{8,9},{9,8},{10,11... | collective-permute-start | bytes 614408 | tf_op jit(solution)/shard_map/ppermute | solution.py:450
  32.1 2.3 %collective-permute-start.13 = (bf16[160,640]{1,0:T(8,128)(2,1)S(1)}, bf16[160,640]{1,0:T(8,128)(2,1)S(1)}, u32[]{:S(2)}, u32[]{:S(2)}) collective-permute-start(bf16[160,640]{1,0:T(8,128)(2,1)S(1)} %get-tuple-element.41.refs_5_), channel_id=1, source_target_pairs={{0,1},{1,0},{2,3},{3,2},{4,5},{5,4},{6,7},{7,6},{8,9},{9,8},{10,11... | collective-permute-start | bytes 614408 | tf_op jit(solution)/shard_map/ppermute | solution.py:450
  32.6 1.5 %collective-permute-start.10 = (bf16[144,640]{1,0:T(8,128)(2,1)S(1)}, bf16[144,640]{1,0:T(8,128)(2,1)S(1)}, u32[]{:S(2)}, u32[]{:S(2)}) collective-permute-start(bf16[144,640]{1,0:T(8,128)(2,1)S(1)} %get-tuple-element.39.refs_2_), channel_id=1, source_target_pairs={{0,1},{1,0},{2,3},{3,2},{4,5},{5,4},{6,7},{7,6},{8,9},{9,8},{10,11... | collective-permute-start | bytes 552968 | tf_op jit(solution)/shard_map/ppermute | solution.py:450
  32.7 1.7 %collective-permute-start.11 = (bf16[144,640]{1,0:T(8,128)(2,1)S(1)}, bf16[144,640]{1,0:T(8,128)(2,1)S(1)}, u32[]{:S(2)}, u32[]{:S(2)}) collective-permute-start(bf16[144,640]{1,0:T(8,128)(2,1)S(1)} %get-tuple-element.38.refs_3_.refs_1_), channel_id=1, source_target_pairs={{0,1},{1,0},{2,3},{3,2},{4,5},{5,4},{6,7},{7,6},{8,9},{9,8},{10,11... | collective-permute-start | bytes 552968 | tf_op jit(solution)/shard_map/ppermute | solution.py:450
  38.2 1.6 %copy-start.5 = (bf16[320,640]{1,0:T(8,128)(2,1)S(1)}, bf16[320,640]{1,0:T(8,128)(2,1)}, u32[]{:S(2)}) copy-start(bf16[320,640]{1,0:T(8,128)(2,1)} %weight_ref.2) | copy-start | bytes 1228804
  38.2 1.6 %copy-start.12 = (f32[640]{0:T(1024)S(1)}, f32[640]{0:T(1024)}, u32[]{:S(2)}) copy-start(f32[640]{0:T(1024)} %gain_ref.3) | copy-start | bytes 7684
  38.2 1.6 %collective-permute-start.14 = (bf16[256,640]{1,0:T(8,128)(2,1)S(1)}, bf16[256,640]{1,0:T(8,128)(2,1)S(1)}, u32[]{:S(2)}, u32[]{:S(2)}) collective-permute-start(bf16[256,640]{1,0:T(8,128)(2,1)S(1)} %shard_map.145.refs_1_), channel_id=1, source_target_pairs={{0,1},{1,0},{2,3},{3,2},{4,5},{5,4},{6,7},{7,6},{8,9},{9,8},{10,11... | collective-permute-start | bytes 983048 | tf_op jit(solution)/shard_map/ppermute | solution.py:450
  39.8 39.3 %copy-start.2 = (bf16[640,320]{0,1:T(8,128)(2,1)S(1)}, bf16[640,320]{0,1:T(8,128)(2,1)}, u32[]{:S(2)}) copy-start(bf16[640,320]{0,1:T(8,128)(2,1)} %param.24) | copy-start | bytes 1228804
  39.8 39.3 %copy-start.3 = (bf16[640,320]{0,1:T(8,128)(2,1)S(1)}, bf16[640,320]{0,1:T(8,128)(2,1)}, u32[]{:S(2)}) copy-start(bf16[640,320]{0,1:T(8,128)(2,1)} %param.25) | copy-start | bytes 1228804
  39.8 39.3 %copy-start.4 = (bf16[640,320]{0,1:T(8,128)(2,1)S(1)}, bf16[640,320]{0,1:T(8,128)(2,1)}, u32[]{:S(2)}) copy-start(bf16[640,320]{0,1:T(8,128)(2,1)} %param.26) | copy-start | bytes 1228804
  79.2 22.3 %copy-start.6 = (bf16[320,640]{1,0:T(8,128)(2,1)S(1)}, bf16[320,640]{1,0:T(8,128)(2,1)}, u32[]{:S(2)}) copy-start(bf16[320,640]{1,0:T(8,128)(2,1)} %weight_ref.3) | copy-start | bytes 1228804

commit v4 on v3

--- a/solution.py
+++ b/solution.py
@@ -34,6 +34,8 @@
 ACC_AT = (0, 256, 384, 640)
 ACC_WIDTH = 768
 
+ORDER = [(x * 4 + y) * 8 + z for z in range(8) for x in range(2) for y in range(4)]
+
 f32 = jnp.float32
 bf16 = jnp.bfloat16
 
@@ -62,7 +64,9 @@
     return [pl.BlockSpec(memory_space=pltpu.VMEM)] * count
 
 
-def call(body, outs, operands, scratch=(), smem=0, limit=8, anywhere=(), flops=0):
+def call(
+    body, outs, operands, scratch=(), smem=0, limit=8, anywhere=(), flops=0, out_anywhere=False
+):
     single = not isinstance(outs, (list, tuple))
     specs = [pl.BlockSpec(memory_space=pltpu.SMEM)] * smem + vmem(len(operands) - smem)
     for i in anywhere:
@@ -71,7 +75,11 @@
         body,
         out_shape=outs,
         in_specs=specs,
-        out_specs=vmem(1)[0] if single else vmem(len(outs)),
+        out_specs=pl.BlockSpec(memory_space=pl.ANY)
+        if out_anywhere
+        else vmem(1)[0]
+        if single
+        else vmem(len(outs)),
         scratch_shapes=list(scratch),
         compiler_params=pltpu.CompilerParams(vmem_limit_bytes=limit * 1024 * 1024),
         cost_estimate=pl.CostEstimate(flops=flops, bytes_accessed=0, transcendentals=0),
@@ -373,32 +381,43 @@
             half = half + pltpu.roll(other, LANES // 2, 1)
         rows[pl.ds(2 * PLACES + pair, FRAMES, stride=BACK + 1), :] = half
     rows[pl.ds(BACK - 1, FRAMES, stride=BACK + 1), :] = jnp.zeros((FRAMES, LANES), f32)
-    for g in range(FRAMES):
-        out_ref[g * BACK : (g + 1) * BACK, :] = rows[
-            g * (BACK + 1) : g * (BACK + 1) + BACK, :
-        ].astype(bf16)
-
-
-def final_kernel(got_ref, weight_ref, mixed_ref, out_ref, rows, attended, weight):
+    for g in range(0, FRAMES, 2):
+        pair = [rows[i * (BACK + 1) : i * (BACK + 1) + BACK, :] for i in (g, g + 1)]
+        out_ref[g * BACK : (g + 2) * BACK, :] = jnp.concatenate(pair, axis=0).astype(bf16)
+
+
+def final_kernel(got_ref, weight_ref, mixed_ref, out_ref, rows, attended, weight, staged, left):
     weight[0:64, :] = jnp.zeros((64, C), bf16)
     weight[64:, :] = weight_ref[...]
-    for g in range(FRAMES):
-        rows[g * (BACK + 1) : g * (BACK + 1) + BACK, :] = got_ref[
-            g * BACK : (g + 1) * BACK, :
-        ].astype(f32)
+    for g in range(0, FRAMES, 2):
+        pair = got_ref[g * BACK : (g + 2) * BACK, :].astype(f32)
+        for i in range(2):
+            rows[(g + i) * (BACK + 1) : (g + i) * (BACK + 1) + BACK, :] = pair[
+                i * BACK : (i + 1) * BACK, :
+            ]
     upper = lane_iota(LANES) >= LANES // 2
-    for j in range(PLACES):
-        cell = slice(j * FRAMES, (j + 1) * FRAMES)
-        for b in range(2):
-            attended[cell, (1 + b) * LANES : (2 + b) * LANES] = rows[
-                pl.ds(j * 2 + b, FRAMES, stride=BACK + 1), :
-            ].astype(bf16)
-        half = rows[pl.ds(2 * PLACES + j // 2, FRAMES, stride=BACK + 1), :]
-        if j % 2:
-            half = pltpu.roll(half, LANES // 2, 1)
-        attended[cell, 0:LANES] = jnp.where(upper, half, 0.0).astype(bf16)
-    update = dot(attended[...], weight[...])
-    out_ref[...] = (mixed_ref[...].astype(f32) + update).astype(bf16)
+    parts = 3
+    copies = []
+    for part in range(parts):
+        for j in range(part * PLACES // parts, (part + 1) * PLACES // parts):
+            cell = slice(j * FRAMES, (j + 1) * FRAMES)
+            for b in range(2):
+                attended[cell, (1 + b) * LANES : (2 + b) * LANES] = rows[
+                    pl.ds(j * 2 + b, FRAMES, stride=BACK + 1), :
+                ].astype(bf16)
+            half = rows[pl.ds(2 * PLACES + j // 2, FRAMES, stride=BACK + 1), :]
+            if j % 2:
+                half = pltpu.roll(half, LANES // 2, 1)
+            attended[cell, 0:LANES] = jnp.where(upper, half, 0.0).astype(bf16)
+        size = CELLS // parts
+        cells = slice(part * size, (part + 1) * size)
+        update = dot(attended[cells, :], weight[...])
+        staged[cells, :] = (mixed_ref[cells, :].astype(f32) + update).astype(bf16)
+        at = pl.ds(part * size, size)
+        copies.append(pltpu.make_async_copy(staged.at[at], out_ref.at[at], left.at[part]))
+        copies[-1].start()
+    for copy in copies:
+        copy.wait()
 
 
 def order_kernel(value_ref, before_ref, out_ref):
@@ -560,7 +579,7 @@
         limit=16,
     )
     got = lax.all_to_all(
-        sent.reshape(FRAMES, SENT, LANES), "frame", split_axis=0, concat_axis=0, tiled=True
+        sent.reshape(FRAMES, SENT, LANES), "frame", split_axis=0, concat_axis=0, axis_index_groups=[ORDER], tiled=True
     )
     back = call(
         temporal_kernel,
@@ -579,7 +598,7 @@
         ],
     )
     returned = lax.all_to_all(
-        back.reshape(FRAMES, BACK, LANES), "frame", split_axis=0, concat_axis=0, tiled=True
+        back.reshape(FRAMES, BACK, LANES), "frame", split_axis=0, concat_axis=0, axis_index_groups=[ORDER], tiled=True
     )
     output = call(
         final_kernel,
@@ -589,7 +608,10 @@
             pltpu.VMEM((FRAMES * (BACK + 1), LANES), f32),
             pltpu.VMEM((CELLS, 384), bf16),
             pltpu.VMEM((384, C), bf16),
+            pltpu.VMEM((CELLS, C), bf16),
+            pltpu.SemaphoreType.DMA((3,)),
         ],
+        out_anywhere=True,
     )
     return output.reshape(latent.shape)
 

time: 103 us -> 102 us (level)
    all_to_all x1, blocking collectives: 37.5 us -> 35.5 us  [on_device(): lax.all_to_all(sent.reshape(FRAMES, SENT, LANES), 'frame', split_axis=0,...]
where the time goes in v4:
time: 102 us
  blocking collectives  56.8 us (56%)
  Pallas kernels  28.3 us (28%)
  starting transfers between devices  10.5 us (10%)
  waiting for transfers between devices  4.86 us (5%)
  local copies, waits for them, and re-layouts  1.18 us (1%)
    all_to_all x1, blocking collectives, on_device(): lax.all_to_all(sent.reshape(FRAMES, SENT, LANES), 'frame', split_axis=0,...  35.5 us
    pallas_call x12, Pallas kernels, call(): pl.pallas_call(body, out_shape=outs, in_specs=specs, out_specs=pl.BlockSp...  28.3 us
    all_to_all x1, blocking collectives, on_device(): lax.all_to_all(back.reshape(FRAMES, BACK, LANES), 'frame', split_axis=0,...  21.2 us
    ppermute x14, starting transfers between devices, swap(): return lax.ppermute(value, 'space', [(i, i ^ k) for i in range(4)])  8.86 us
    ppermute x14, waiting for transfers between devices, swap(): return lax.ppermute(value, 'space', [(i, i ^ k) for i in range(4)])  4.86 us
  transfers between devices with their start and end apart: 15, of which 7 were waited for; matrix products, arithmetic and copies ran while one was open for 0% of the time, Pallas kernels for 21%

profile of v4, /device:TPU:2, one launch (start us, length us, event | category | flops | bytes accessed | tf_op | source)
XLA Modules:
  0.0 102.1 jit_solution(1830137822815841063)
XLA Ops:
  0.0 0.1 add_convert_fusion.flags_ref
  0.1 1.1 %copy-done = bf16[1,12,48,640]{3,2,1,0:T(8,128)(2,1)S(1)} copy-done((bf16[1,12,48,640]{3,2,1,0:T(8,128)(2,1)S(1)}, bf16[1,12,48,640]{3,2,1,0:T(8,128)(2,1)}, u32[]{:S(2)}) %copy-start) | copy-done | bytes 737304
  1.2 1.1 %shard_map.136 = (f32[8,640]{1,0:T(8,128)S(1)}, bf16[64,640]{1,0:T(8,128)(2,1)S(1)}, bf16[48,640]{1,0:T(8,128)(2,1)S(1)}) custom-call(f32[1,4]{1,0:T(1,128)S(1)} %add_convert_fusion.flags_ref, bf16[576,640]{1,0:T(8,128)(2,1)S(1)} %bitcast.25), custom_call_target="tpu_custom_call" | custom-call | flops 2000000000 | tf_op jit(solution)/shard_map/pallas_call | solution.py:74
  2.3 0.1 collective-permute-start
  2.4 1.3 %collective-permute-done.near_ref = bf16[64,640]{1,0:T(8,128)(2,1)S(1)} collective-permute-done((bf16[64,640]{1,0:T(8,128)(2,1)S(1)}, bf16[64,640]{1,0:T(8,128)(2,1)S(1)}, u32[]{:S(2)}, u32[]{:S(2)}) %collective-permute-start) | collective-permute-done | bytes 81952 | tf_op jit(solution)/shard_map/ppermute | solution.py:469
  3.7 2.0 %collective-permute-start.1 = (bf16[64,640]{1,0:T(8,128)(2,1)S(1)}, bf16[64,640]{1,0:T(8,128)(2,1)S(1)}, u32[]{:S(2)}, u32[]{:S(2)}) collective-permute-start(bf16[64,640]{1,0:T(8,128)(2,1)S(1)} %get-tuple-element.29), channel_id=1, source_target_pairs={{0,3},{1,2},{2,1},{3,0},{4,7},{5,6},{6,5},{7,4},{8,11},{9,10},{10,... | collective-permute-start | bytes 245768 | tf_op jit(solution)/shard_map/ppermute | solution.py:469
  5.7 0.0 copy-done.8
  5.7 0.0 copy-done.9
  5.7 0.0 copy-done.13
  5.7 0.0 copy-start.7
  5.7 0.0 copy-start.10
  5.7 0.0 copy-start.11
  5.7 1.7 %shard_map.139 = (bf16[576,640]{1,0:T(8,128)(2,1)S(1)}, bf16[288,640]{1,0:T(8,128)(2,1)S(1)}) custom-call(f32[1,4]{1,0:T(1,128)S(1)} %add_convert_fusion.flags_ref, bf16[576,640]{1,0:T(8,128)(2,1)S(1)} %bitcast.35, f32[8,640]{1,0:T(8,128)S(1)} %get-tuple-element.28.sums_ref.before_ref, bf16[320,640]{1,0:T(8,128)(2,1)S(1)} %bitcast.31, ...), custom_call_target="tpu_custom_call" | custom-call | flops 2000000000 | tf_op jit(solution)/shard_map/pallas_call | solution.py:74
  7.4 1.5 %collective-permute-start.3 = (bf16[288,640]{1,0:T(8,128)(2,1)S(1)}, bf16[288,640]{1,0:T(8,128)(2,1)S(1)}, u32[]{:S(2)}, u32[]{:S(2)}) collective-permute-start(bf16[288,640]{1,0:T(8,128)(2,1)S(1)} %get-tuple-element.32), channel_id=1, source_target_pairs={{0,2},{1,3},{2,0},{3,1},{4,6},{5,7},{6,4},{7,5},{8,10},{9,11},{10,... | collective-permute-start | bytes 1105928 | tf_op jit(solution)/shard_map/ppermute | solution.py:469
  9.0 0.1 collective-permute-start.8
  9.0 0.7 collective-permute-done.1.far_ref
  9.7 0.0 slice-done
  9.7 0.0 slice-done.1
  9.7 0.0 copy-done.1
  9.7 0.0 copy-done.7
  9.7 0.0 copy-done.10
  9.7 0.0 copy-done.11
  9.7 7.8 %shard_map.138 = (bf16[576,640]{1,0:T(8,128)(2,1)S(1)}, bf16[576,384]{1,0:T(8,128)(2,1)S(1)}, bf16[576,640]{1,0:T(8,128)(2,1)S(1)}, bf16[288,640]{1,0:T(8,128)(2...) custom-call(f32[1,4]{1,0:T(1,128)S(1)} %add_convert_fusion.flags_ref, ...), custom_call_target="tpu_custom_call" | custom-call | tf_op jit(solution)/shard_map/pallas_call | solution.py:74
  17.5 0.2 collective-permute-start.6
  17.8 0.4 collective-permute-start.7
  18.1 2.1 %collective-permute-start.5 = (bf16[320,640]{1,0:T(8,128)(2,1)S(1)}, bf16[320,640]{1,0:T(8,128)(2,1)S(1)}, u32[]{:S(2)}, u32[]{:S(2)}) collective-permute-start(bf16[320,640]{1,0:T(8,128)(2,1)S(1)} %get-tuple-element.33), channel_id=1, source_target_pairs={{0,2},{1,3},{2,0},{3,1},{4,6},{5,7},{6,4},{7,5},{8,10},{9,11},{10,... | collective-permute-start | bytes 1228808 | tf_op jit(solution)/shard_map/ppermute | solution.py:469
  20.3 0.0 collective-permute-done.3.value_ref
  20.3 0.0 collective-permute-start.9
  20.3 0.0 collective-permute-done.6.refs_2_
  20.3 1.7 %collective-permute-start.4 = (bf16[288,640]{1,0:T(8,128)(2,1)S(1)}, bf16[288,640]{1,0:T(8,128)(2,1)S(1)}, u32[]{:S(2)}, u32[]{:S(2)}) collective-permute-start(bf16[288,640]{1,0:T(8,128)(2,1)S(1)} %shard_map.140.refs_6_), channel_id=1, source_target_pairs={{0,32},{4,36},{8,40},{12,44},{16,48},{20,52},{24,56},{28,60},{32,0... | collective-permute-start | bytes 1105928 | tf_op jit(solution)/shard_map/ppermute | solution.py:533
  22.0 0.0 collective-permute-done.7.refs_3_
  22.0 1.4 %collective-permute-start.2 = (bf16[256,640]{1,0:T(8,128)(2,1)S(1)}, bf16[256,640]{1,0:T(8,128)(2,1)S(1)}, u32[]{:S(2)}, u32[]{:S(2)}) collective-permute-start(bf16[256,640]{1,0:T(8,128)(2,1)S(1)} %get-tuple-element.31), channel_id=1, source_target_pairs={{0,2},{1,3},{2,0},{3,1},{4,6},{5,7},{6,4},{7,5},{8,10},{9,11},{10,... | collective-permute-start | bytes 983048 | tf_op jit(solution)/shard_map/ppermute | solution.py:469
  23.3 0.0 collective-permute-done.9.refs_7_.refs_1_
  23.3 0.0 collective-permute-done.8.refs_5_
  23.4 7.7 %shard_map.141.before_ref.refs_4_ = f32[576,768]{1,0:T(8,128)S(1)} custom-call(bf16[576,384]{1,0:T(8,128)(2,1)S(1)} %get-tuple-element.30.before_ref.refs_0_.query_ref, bf16[576,640]{1,0:T(8,128)(2,1)S(1)} %get-tuple-element.34.refs_1_, bf16[288,640]{1,0:T(8,128)(2,1)S(1)} %collective-permute-done.6.refs_2_, ...), custom_call_target="tpu_custom_call" | custom-call | tf_op jit(solution)/shard_map/pallas_call | solution.py:74
  31.1 0.9 collective-permute-done.5.second_ref
  31.9 0.0 collective-permute-done.4.first_ref
  32.0 0.1 shard_map.142
  32.0 0.1 collective-permute-start.12
  32.1 0.5 collective-permute-start.13
  32.6 0.1 collective-permute-start.10
  32.7 0.4 collective-permute-start.11
  33.1 0.9 shard_map.143.refs_8_
  34.0 0.1 collective-permute-done.10.refs_2_
  34.1 0.3 collective-permute-done.11.refs_3_
  34.4 0.0 collective-permute-done.12.refs_6_
  34.4 0.0 collective-permute-done.13.refs_7_
  34.4 2.8 %shard_map.144.before_ref.refs_2_ = f32[576,768]{1,0:T(8,128)S(1)} custom-call(bf16[576,384]{1,0:T(8,128)(2,1)S(1)} %get-tuple-element.30.before_ref.refs_0_.query_ref, bf16[144,640]{1,0:T(8,128)(2,1)S(1)} %get-tuple-element.38.refs_3_.refs_1_, bf16[144,640]{1,0:T(8,128)(2,1)S(1)} %collective-permute-done.10.refs_2_, ...), custom_call_target="tpu_custom_call" | custom-call | tf_op jit(solution)/shard_map/pallas_call | solution.py:74
  37.2 1.0 collective-permute-done.2.value_ref
  38.2 0.0 collective-permute-start.14
  38.2 0.9 shard_map.146.acc_ref
  39.1 0.7 collective-permute-done.14.kv_ref
  39.8 0.0 copy-done.5
  39.8 0.0 copy-done.12
  39.8 0.0 copy-start.4
  39.8 1.8 %shard_map.147 = (bf16[576,640]{1,0:T(8,128)(2,1)S(1)}, bf16[3072,128]{1,0:T(8,128)(2,1)S(1)}) custom-call(bf16[576,384]{1,0:T(8,128)(2,1)S(1)} %get-tuple-element.30.before_ref.refs_0_.query_ref, f32[576,768]{1,0:T(8,128)S(1)} %shard_map.146.acc_ref, bf16[256,640]{1,0:T(8,128)(2,1)S(1)} %collective-permute-done.14.kv_ref, ...), custom_call_target="tpu_custom_call" | custom-call | tf_op jit(solution)/shard_map/pallas_call | solution.py:74
  41.7 35.5 %all_to_all.10 = bf16[64,48,128]{2,1,0:T(8,128)(2,1)S(1)} all-to-all(bf16[64,48,128]{2,1,0:T(8,128)(2,1)S(1)} %bitcast.24), channel_id=1, replica_groups={{0,32,64,96,128,160,192,224,4,36,68,100,132,164,196,228,8,40,72,104,136..., dimensions={0} | all-to-all | bytes 1572864 | tf_op jit(solution)/shard_map/all_to_all | solution.py:581
  77.2 0.0 copy-done.2
  77.2 0.0 copy-done.3
  77.2 0.0 copy-done.4
  77.2 2.1 %shard_map.148 = bf16[1536,128]{1,0:T(8,128)(2,1)S(1)} custom-call(bf16[3072,128]{1,0:T(8,128)(2,1)S(1)} %bitcast.21, bf16[320,640]{1,0:T(8,128)(2,1)S(1)} %bitcast.27, bf16[320,640]{1,0:T(8,128)(2,1)S(1)} %bitcast.28, bf16[320,640]{1,0:T(8,128)(2,1)S(1)} %bitcast.29), custom_call_target="tpu_custom_call" | custom-call | tf_op jit(solution)/shard_map/pallas_call | solution.py:74
  79.3 21.2 %all_to_all.11 = bf16[64,24,128]{2,1,0:T(8,128)(2,1)S(1)} all-to-all(bf16[64,24,128]{2,1,0:T(8,128)(2,1)S(1)} %bitcast.22), channel_id=1, replica_groups={{0,32,64,96,128,160,192,224,4,36,68,100,132,164,196,228,8,40,72,104,136..., dimensions={0} | all-to-all | bytes 786432 | tf_op jit(solution)/shard_map/all_to_all | solution.py:600
  100.5 0.0 copy-done.6
  100.5 1.4 %shard_map.149 = bf16[576,640]{1,0:T(8,128)(2,1)} custom-call(bf16[1536,128]{1,0:T(8,128)(2,1)S(1)} %bitcast.23, bf16[320,640]{1,0:T(8,128)(2,1)S(1)} %copy-done.6, bf16[576,640]{1,0:T(8,128)(2,1)S(1)} %get-tuple-element.44.mixed_ref), custom_call_target="tpu_custom_call" | custom-call | tf_op jit(solution)/shard_map/pallas_call | solution.py:74
  (16 shorter events, 0.1 us)
Async XLA Ops:
  0.1 1.1 %copy-start = (bf16[1,12,48,640]{3,2,1,0:T(8,128)(2,1)S(1)}, bf16[1,12,48,640]{3,2,1,0:T(8,128)(2,1)}, u32[]{:S(2)}) copy-start(bf16[1,12,48,640]{3,2,1,0:T(8,128)(2,1)} %param.14) | copy-start | bytes 2211844
  1.2 8.5 %slice-start = ((s8[7372800]{0:T(1024)(128)(4,1)}), s8[4194304]{0:T(1024)(128)(4,1)S(1)}, s32[]{:S(2)}) async-start(s8[7372800]{0:T(1024)(128)(4,1)} %bitcast.18), calls=%async_computation.2 | async-start | bytes 8388608
  2.3 1.4 %collective-permute-start = (bf16[64,640]{1,0:T(8,128)(2,1)S(1)}, bf16[64,640]{1,0:T(8,128)(2,1)S(1)}, u32[]{:S(2)}, u32[]{:S(2)}) collective-permute-start(bf16[64,640]{1,0:T(8,128)(2,1)S(1)} %get-tuple-element.26), channel_id=1, source_target_pairs={{0,1},{1,0},{2,3},{3,2},{4,5},{5,4},{6,7},{7,6},{8,9},{9,8},{10,11... | collective-permute-start | bytes 245768 | tf_op jit(solution)/shard_map/ppermute | solution.py:469
  3.6 2.0 %copy-start.8 = (bf16[640,320]{0,1:T(8,128)(2,1)S(1)}, bf16[640,320]{0,1:T(8,128)(2,1)}, u32[]{:S(2)}) copy-start(bf16[640,320]{0,1:T(8,128)(2,1)} %param.20) | copy-start | bytes 1228804
  3.6 2.0 %copy-start.9 = (bf16[640,320]{0,1:T(8,128)(2,1)S(1)}, bf16[640,320]{0,1:T(8,128)(2,1)}, u32[]{:S(2)}) copy-start(bf16[640,320]{0,1:T(8,128)(2,1)} %param.21) | copy-start | bytes 1228804
  3.6 2.0 %copy-start.13 = (bf16[12,48,640]{2,1,0:T(8,128)(2,1)S(1)}, bf16[12,48,640]{2,1,0:T(8,128)(2,1)}, u32[]{:S(2)}) copy-start(bf16[12,48,640]{2,1,0:T(8,128)(2,1)} %param.15) | copy-start | bytes 2211844
  3.6 6.1 %slice-start.1 = ((s8[7372800]{0:T(1024)(128)(4,1)}), s8[3178496]{0:T(1024)(128)(4,1)S(1)}, s32[]{:S(2)}) async-start(s8[7372800]{0:T(1024)(128)(4,1)} %bitcast.18), calls=%async_computation.3 | async-start | bytes 6356992
  3.7 6.0 %collective-permute-start.1 = (bf16[64,640]{1,0:T(8,128)(2,1)S(1)}, bf16[64,640]{1,0:T(8,128)(2,1)S(1)}, u32[]{:S(2)}, u32[]{:S(2)}) collective-permute-start(bf16[64,640]{1,0:T(8,128)(2,1)S(1)} %get-tuple-element.29), channel_id=1, source_target_pairs={{0,3},{1,2},{2,1},{3,0},{4,7},{5,6},{6,5},{7,4},{8,11},{9,10},{10,... | collective-permute-start | bytes 245768 | tf_op jit(solution)/shard_map/ppermute | solution.py:469
  5.7 4.0 %copy-start.1 = (bf16[1,12,48,640]{3,2,1,0:T(8,128)(2,1)S(1)}, bf16[1,12,48,640]{3,2,1,0:T(8,128)(2,1)}, u32[]{:S(2)}) copy-start(bf16[1,12,48,640]{3,2,1,0:T(8,128)(2,1)} %param.14) | copy-start | bytes 2211844
  5.7 4.0 %copy-start.7 = (bf16[640,320]{0,1:T(8,128)(2,1)S(1)}, bf16[640,320]{0,1:T(8,128)(2,1)}, u32[]{:S(2)}) copy-start(bf16[640,320]{0,1:T(8,128)(2,1)} %param.19) | copy-start | bytes 1228804
  5.7 4.0 %copy-start.10 = (f32[640]{0:T(1024)S(1)}, f32[640]{0:T(1024)}, u32[]{:S(2)}) copy-start(f32[640]{0:T(1024)} %gain_ref.2) | copy-start | bytes 7684
  5.7 4.0 %copy-start.11 = (f32[640]{0:T(1024)S(1)}, f32[640]{0:T(1024)}, u32[]{:S(2)}) copy-start(f32[640]{0:T(1024)} %norm_gain_ref.1) | copy-start | bytes 7684
  7.4 12.8 %collective-permute-start.3 = (bf16[288,640]{1,0:T(8,128)(2,1)S(1)}, bf16[288,640]{1,0:T(8,128)(2,1)S(1)}, u32[]{:S(2)}, u32[]{:S(2)}) collective-permute-start(bf16[288,640]{1,0:T(8,128)(2,1)S(1)} %get-tuple-element.32), channel_id=1, source_target_pairs={{0,2},{1,3},{2,0},{3,1},{4,6},{5,7},{6,4},{7,5},{8,10},{9,11},{10,... | collective-permute-start | bytes 1105928 | tf_op jit(solution)/shard_map/ppermute | solution.py:469
  9.0 14.4 %collective-permute-start.8 = (bf16[576,640]{1,0:T(8,128)(2,1)S(1)}, bf16[576,640]{1,0:T(8,128)(2,1)S(1)}, u32[]{:S(2)}, u32[]{:S(2)}) collective-permute-start(bf16[576,640]{1,0:T(8,128)(2,1)S(1)} %get-tuple-element.37.refs_4_), channel_id=1, source_target_pairs={{0,1},{1,0},{2,3},{3,2},{4,5},{5,4},{6,7},{7,6},{8,9},{9,8},{10,11... | collective-permute-start | bytes 2211848 | tf_op jit(solution)/shard_map/ppermute | solution.py:469
  17.5 2.7 %collective-permute-start.6 = (bf16[288,640]{1,0:T(8,128)(2,1)S(1)}, bf16[288,640]{1,0:T(8,128)(2,1)S(1)}, u32[]{:S(2)}, u32[]{:S(2)}) collective-permute-start(bf16[288,640]{1,0:T(8,128)(2,1)S(1)} %get-tuple-element.35), channel_id=1, source_target_pairs={{0,1},{1,0},{2,3},{3,2},{4,5},{5,4},{6,7},{7,6},{8,9},{9,8},{10,11... | collective-permute-start | bytes 1105928 | tf_op jit(solution)/shard_map/ppermute | solution.py:469
  17.8 4.2 %collective-permute-start.7 = (bf16[288,640]{1,0:T(8,128)(2,1)S(1)}, bf16[288,640]{1,0:T(8,128)(2,1)S(1)}, u32[]{:S(2)}, u32[]{:S(2)}) collective-permute-start(bf16[288,640]{1,0:T(8,128)(2,1)S(1)} %get-tuple-element.36), channel_id=1, source_target_pairs={{0,1},{1,0},{2,3},{3,2},{4,5},{5,4},{6,7},{7,6},{8,9},{9,8},{10,11... | collective-permute-start | bytes 1105928 | tf_op jit(solution)/shard_map/ppermute | solution.py:469
  18.1 13.8 %collective-permute-start.5 = (bf16[320,640]{1,0:T(8,128)(2,1)S(1)}, bf16[320,640]{1,0:T(8,128)(2,1)S(1)}, u32[]{:S(2)}, u32[]{:S(2)}) collective-permute-start(bf16[320,640]{1,0:T(8,128)(2,1)S(1)} %get-tuple-element.33), channel_id=1, source_target_pairs={{0,2},{1,3},{2,0},{3,1},{4,6},{5,7},{6,4},{7,5},{8,10},{9,11},{10,... | collective-permute-start | bytes 1228808 | tf_op jit(solution)/shard_map/ppermute | solution.py:469
  20.3 3.1 %collective-permute-start.9 = (bf16[288,640]{1,0:T(8,128)(2,1)S(1)}, bf16[288,640]{1,0:T(8,128)(2,1)S(1)}, u32[]{:S(2)}, u32[]{:S(2)}) collective-permute-start(bf16[288,640]{1,0:T(8,128)(2,1)S(1)} %shard_map.140.refs_6_), channel_id=1, source_target_pairs={{0,1},{1,0},{2,3},{3,2},{4,5},{5,4},{6,7},{7,6},{8,9},{9,8},{10,11... | collective-permute-start | bytes 1105928 | tf_op jit(solution)/shard_map/ppermute | solution.py:469
  20.3 11.7 %collective-permute-start.4 = (bf16[288,640]{1,0:T(8,128)(2,1)S(1)}, bf16[288,640]{1,0:T(8,128)(2,1)S(1)}, u32[]{:S(2)}, u32[]{:S(2)}) collective-permute-start(bf16[288,640]{1,0:T(8,128)(2,1)S(1)} %shard_map.140.refs_6_), channel_id=1, source_target_pairs={{0,32},{4,36},{8,40},{12,44},{16,48},{20,52},{24,56},{28,60},{32,0... | collective-permute-start | bytes 1105928 | tf_op jit(solution)/shard_map/ppermute | solution.py:533
  22.0 16.2 %collective-permute-start.2 = (bf16[256,640]{1,0:T(8,128)(2,1)S(1)}, bf16[256,640]{1,0:T(8,128)(2,1)S(1)}, u32[]{:S(2)}, u32[]{:S(2)}) collective-permute-start(bf16[256,640]{1,0:T(8,128)(2,1)S(1)} %get-tuple-element.31), channel_id=1, source_target_pairs={{0,2},{1,3},{2,0},{3,1},{4,6},{5,7},{6,4},{7,5},{8,10},{9,11},{10,... | collective-permute-start | bytes 983048 | tf_op jit(solution)/shard_map/ppermute | solution.py:469
  32.0 2.4 %collective-permute-start.12 = (bf16[160,640]{1,0:T(8,128)(2,1)S(1)}, bf16[160,640]{1,0:T(8,128)(2,1)S(1)}, u32[]{:S(2)}, u32[]{:S(2)}) collective-permute-start(bf16[160,640]{1,0:T(8,128)(2,1)S(1)} %get-tuple-element.40.refs_4_), channel_id=1, source_target_pairs={{0,1},{1,0},{2,3},{3,2},{4,5},{5,4},{6,7},{7,6},{8,9},{9,8},{10,11... | collective-permute-start | bytes 614408 | tf_op jit(solution)/shard_map/ppermute | solution.py:469
  32.1 2.3 %collective-permute-start.13 = (bf16[160,640]{1,0:T(8,128)(2,1)S(1)}, bf16[160,640]{1,0:T(8,128)(2,1)S(1)}, u32[]{:S(2)}, u32[]{:S(2)}) collective-permute-start(bf16[160,640]{1,0:T(8,128)(2,1)S(1)} %get-tuple-element.41.refs_5_), channel_id=1, source_target_pairs={{0,1},{1,0},{2,3},{3,2},{4,5},{5,4},{6,7},{7,6},{8,9},{9,8},{10,11... | collective-permute-start | bytes 614408 | tf_op jit(solution)/shard_map/ppermute | solution.py:469
  32.6 1.5 %collective-permute-start.10 = (bf16[144,640]{1,0:T(8,128)(2,1)S(1)}, bf16[144,640]{1,0:T(8,128)(2,1)S(1)}, u32[]{:S(2)}, u32[]{:S(2)}) collective-permute-start(bf16[144,640]{1,0:T(8,128)(2,1)S(1)} %get-tuple-element.39.refs_2_), channel_id=1, source_target_pairs={{0,1},{1,0},{2,3},{3,2},{4,5},{5,4},{6,7},{7,6},{8,9},{9,8},{10,11... | collective-permute-start | bytes 552968 | tf_op jit(solution)/shard_map/ppermute | solution.py:469
  32.7 1.7 %collective-permute-start.11 = (bf16[144,640]{1,0:T(8,128)(2,1)S(1)}, bf16[144,640]{1,0:T(8,128)(2,1)S(1)}, u32[]{:S(2)}, u32[]{:S(2)}) collective-permute-start(bf16[144,640]{1,0:T(8,128)(2,1)S(1)} %get-tuple-element.38.refs_3_.refs_1_), channel_id=1, source_target_pairs={{0,1},{1,0},{2,3},{3,2},{4,5},{5,4},{6,7},{7,6},{8,9},{9,8},{10,11... | collective-permute-start | bytes 552968 | tf_op jit(solution)/shard_map/ppermute | solution.py:469
  38.2 1.6 %copy-start.5 = (bf16[320,640]{1,0:T(8,128)(2,1)S(1)}, bf16[320,640]{1,0:T(8,128)(2,1)}, u32[]{:S(2)}) copy-start(bf16[320,640]{1,0:T(8,128)(2,1)} %weight_ref.2) | copy-start | bytes 1228804
  38.2 1.6 %copy-start.12 = (f32[640]{0:T(1024)S(1)}, f32[640]{0:T(1024)}, u32[]{:S(2)}) copy-start(f32[640]{0:T(1024)} %gain_ref.3) | copy-start | bytes 7684
  38.2 1.6 %collective-permute-start.14 = (bf16[256,640]{1,0:T(8,128)(2,1)S(1)}, bf16[256,640]{1,0:T(8,128)(2,1)S(1)}, u32[]{:S(2)}, u32[]{:S(2)}) collective-permute-start(bf16[256,640]{1,0:T(8,128)(2,1)S(1)} %shard_map.145.refs_1_), channel_id=1, source_target_pairs={{0,1},{1,0},{2,3},{3,2},{4,5},{5,4},{6,7},{7,6},{8,9},{9,8},{10,11... | collective-permute-start | bytes 983048 | tf_op jit(solution)/shard_map/ppermute | solution.py:469
  39.8 37.4 %copy-start.2 = (bf16[640,320]{0,1:T(8,128)(2,1)S(1)}, bf16[640,320]{0,1:T(8,128)(2,1)}, u32[]{:S(2)}) copy-start(bf16[640,320]{0,1:T(8,128)(2,1)} %param.24) | copy-start | bytes 1228804
  39.8 37.4 %copy-start.3 = (bf16[640,320]{0,1:T(8,128)(2,1)S(1)}, bf16[640,320]{0,1:T(8,128)(2,1)}, u32[]{:S(2)}) copy-start(bf16[640,320]{0,1:T(8,128)(2,1)} %param.25) | copy-start | bytes 1228804
  39.8 37.4 %copy-start.4 = (bf16[640,320]{0,1:T(8,128)(2,1)S(1)}, bf16[640,320]{0,1:T(8,128)(2,1)}, u32[]{:S(2)}) copy-start(bf16[640,320]{0,1:T(8,128)(2,1)} %param.26) | copy-start | bytes 1228804
  77.2 23.3 %copy-start.6 = (bf16[320,640]{1,0:T(8,128)(2,1)S(1)}, bf16[320,640]{1,0:T(8,128)(2,1)}, u32[]{:S(2)}) copy-start(bf16[320,640]{1,0:T(8,128)(2,1)} %weight_ref.3) | copy-start | bytes 1228804

commit v5 on v4

--- a/solution.py
+++ b/solution.py
@@ -19,6 +19,7 @@
 PLACES = CELLS // FRAMES
 LANES = 128
 SENT = 48
+WHOLE = 256
 TILE = 768
 EARLY = 224
 HEAD = 48
@@ -34,7 +35,7 @@
 ACC_AT = (0, 256, 384, 640)
 ACC_WIDTH = 768
 
-ORDER = [(x * 4 + y) * 8 + z for z in range(8) for x in range(2) for y in range(4)]
+ORDER = [(x * 4 + y) * 8 + z for z in range(8) for y in range(4) for x in range(2)]
 
 f32 = jnp.float32
 bf16 = jnp.bfloat16
@@ -241,27 +242,31 @@
     return (lane >= INNER + h * HEAD_DIM) & (lane < INNER + (h + 1) * HEAD_DIM)
 
 
-def joined(kv_refs, ranges, scratch):
+def tiles_of(kv_refs, ranges, scratch):
+    tiles = []
     at = 0
     for ref, (low, high) in zip(kv_refs, ranges):
-        scratch[at : at + high - low, :] = ref[low:high, :]
-        at += high - low
-    return scratch
-
-
-def attend(query, kv_ref, start):
+        whole = (high - low) // WHOLE * WHOLE
+        if whole == 2 * WHOLE or whole == high - low:
+            tiles.append((ref, low, low + whole))
+            low += whole
+        if low < high:
+            scratch[at : at + high - low, :] = ref[low:high, :]
+            at += high - low
+    return tiles + [(scratch, low, min(low + TILE, at)) for low in range(0, at, TILE)]
+
+
+def attend(query, tiles, start):
     gathered = []
-    keys = kv_ref.shape[0]
     for h in range(HEADS):
         key_low, key_high = KEY_WINDOW[h]
         low, high = VALUE_WINDOW[h]
         mine = head_query(query, h)
         inside = inside_value(h)
         acc = None if start is None else start(h)
-        for first in range(0, keys, TILE):
-            rows = slice(first, min(first + TILE, keys))
-            weights = jnp.exp2(dot_t(mine, kv_ref[rows, key_low:key_high])).astype(bf16)
-            values = jnp.where(inside, kv_ref[rows, low:high], jnp.ones((), bf16))
+        for ref, first, last in tiles:
+            weights = jnp.exp2(dot_t(mine, ref[first:last, key_low:key_high])).astype(bf16)
+            values = jnp.where(inside, ref[first:last, low:high], jnp.ones((), bf16))
             part = dot(weights, values)
             acc = part if acc is None else acc + part
         gathered.append(acc)
@@ -292,8 +297,8 @@
     query_ref = refs[0]
     start = starting(refs[1 + n_kv]) if has_start else None
     out_ref, scratch = refs[-2:]
-    kv_ref = joined(refs[1 : 1 + n_kv], ranges, scratch)
-    for h, acc in enumerate(attend(query_ref[...], kv_ref, start)):
+    tiles = tiles_of(refs[1 : 1 + n_kv], ranges, scratch)
+    for h, acc in enumerate(attend(query_ref[...], tiles, start)):
         out_ref[:, ACC_AT[h] : ACC_AT[h] + acc.shape[1]] = acc
 
 
@@ -311,7 +316,7 @@
 ):
     weight[0:64, :] = jnp.zeros((64, C), bf16)
     weight[64:, :] = weight_ref[...]
-    blocks = normalised(attend(query_ref[...], kv_ref, starting(acc_ref)))
+    blocks = normalised(attend(query_ref[...], [(kv_ref, 0, kv_ref.shape[0])], starting(acc_ref)))
     attended = jnp.concatenate([block.astype(bf16) for block in blocks], axis=1)
     update = dot(attended, weight[...])
     mixed = (hidden_ref[...].astype(f32) + update).astype(bf16)

time: 102 us -> 102 us (level)
  no operation moved by 1% of the time
where the time goes in v5:
time: 102 us
  blocking collectives  56.5 us (55%)
  Pallas kernels  28 us (27%)
  starting transfers between devices  10.5 us (10%)
  waiting for transfers between devices  5.14 us (5%)
  local copies, waits for them, and re-layouts  1.18 us (1%)
    all_to_all x1, blocking collectives, on_device(): lax.all_to_all(sent.reshape(FRAMES, SENT, LANES), 'frame', split_axis=0,...  35.5 us
    pallas_call x12, Pallas kernels, call(): pl.pallas_call(body, out_shape=outs, in_specs=specs, out_specs=pl.BlockSp...  28 us
    all_to_all x1, blocking collectives, on_device(): lax.all_to_all(back.reshape(FRAMES, BACK, LANES), 'frame', split_axis=0,...  21 us
    ppermute x14, starting transfers between devices, swap(): return lax.ppermute(value, 'space', [(i, i ^ k) for i in range(4)])  8.86 us
    ppermute x14, waiting for transfers between devices, swap(): return lax.ppermute(value, 'space', [(i, i ^ k) for i in range(4)])  5.14 us
  transfers between devices with their start and end apart: 15, of which 7 were waited for; matrix products, arithmetic and copies ran while one was open for 0% of the time, Pallas kernels for 21%

profile of v5, /device:TPU:2, one launch (start us, length us, event | category | flops | bytes accessed | tf_op | source)
XLA Modules:
  0.0 101.8 jit_solution(7829139813372598181)
XLA Ops:
  0.0 0.1 add_convert_fusion.flags_ref
  0.1 1.1 %copy-done = bf16[1,12,48,640]{3,2,1,0:T(8,128)(2,1)S(1)} copy-done((bf16[1,12,48,640]{3,2,1,0:T(8,128)(2,1)S(1)}, bf16[1,12,48,640]{3,2,1,0:T(8,128)(2,1)}, u32[]{:S(2)}) %copy-start) | copy-done | bytes 737304
  1.2 1.1 %shard_map.136 = (f32[8,640]{1,0:T(8,128)S(1)}, bf16[64,640]{1,0:T(8,128)(2,1)S(1)}, bf16[48,640]{1,0:T(8,128)(2,1)S(1)}) custom-call(f32[1,4]{1,0:T(1,128)S(1)} %add_convert_fusion.flags_ref, bf16[576,640]{1,0:T(8,128)(2,1)S(1)} %bitcast.25), custom_call_target="tpu_custom_call" | custom-call | flops 2000000000 | tf_op jit(solution)/shard_map/pallas_call | solution.py:75
  2.3 0.1 collective-permute-start
  2.4 1.3 %collective-permute-done.near_ref = bf16[64,640]{1,0:T(8,128)(2,1)S(1)} collective-permute-done((bf16[64,640]{1,0:T(8,128)(2,1)S(1)}, bf16[64,640]{1,0:T(8,128)(2,1)S(1)}, u32[]{:S(2)}, u32[]{:S(2)}) %collective-permute-start) | collective-permute-done | bytes 81952 | tf_op jit(solution)/shard_map/ppermute | solution.py:474
  3.7 2.0 %collective-permute-start.1 = (bf16[64,640]{1,0:T(8,128)(2,1)S(1)}, bf16[64,640]{1,0:T(8,128)(2,1)S(1)}, u32[]{:S(2)}, u32[]{:S(2)}) collective-permute-start(bf16[64,640]{1,0:T(8,128)(2,1)S(1)} %get-tuple-element.29), channel_id=1, source_target_pairs={{0,3},{1,2},{2,1},{3,0},{4,7},{5,6},{6,5},{7,4},{8,11},{9,10},{10,... | collective-permute-start | bytes 245768 | tf_op jit(solution)/shard_map/ppermute | solution.py:474
  5.7 0.0 copy-done.8
  5.7 0.0 copy-done.9
  5.7 0.0 copy-done.13
  5.7 0.0 copy-start.7
  5.7 0.0 copy-start.10
  5.7 0.0 copy-start.11
  5.7 1.7 %shard_map.139 = (bf16[576,640]{1,0:T(8,128)(2,1)S(1)}, bf16[288,640]{1,0:T(8,128)(2,1)S(1)}) custom-call(f32[1,4]{1,0:T(1,128)S(1)} %add_convert_fusion.flags_ref, bf16[576,640]{1,0:T(8,128)(2,1)S(1)} %bitcast.35, f32[8,640]{1,0:T(8,128)S(1)} %get-tuple-element.28.sums_ref.before_ref, bf16[320,640]{1,0:T(8,128)(2,1)S(1)} %bitcast.31, ...), custom_call_target="tpu_custom_call" | custom-call | flops 2000000000 | tf_op jit(solution)/shard_map/pallas_call | solution.py:75
  7.4 1.5 %collective-permute-start.3 = (bf16[288,640]{1,0:T(8,128)(2,1)S(1)}, bf16[288,640]{1,0:T(8,128)(2,1)S(1)}, u32[]{:S(2)}, u32[]{:S(2)}) collective-permute-start(bf16[288,640]{1,0:T(8,128)(2,1)S(1)} %get-tuple-element.32), channel_id=1, source_target_pairs={{0,2},{1,3},{2,0},{3,1},{4,6},{5,7},{6,4},{7,5},{8,10},{9,11},{10,... | collective-permute-start | bytes 1105928 | tf_op jit(solution)/shard_map/ppermute | solution.py:474
  9.0 0.1 collective-permute-start.8
  9.0 0.7 collective-permute-done.1.far_ref
  9.7 0.0 slice-done
  9.7 0.0 slice-done.1
  9.7 0.0 copy-done.1
  9.7 0.0 copy-done.7
  9.7 0.0 copy-done.10
  9.7 0.0 copy-done.11
  9.7 7.8 %shard_map.138 = (bf16[576,640]{1,0:T(8,128)(2,1)S(1)}, bf16[576,384]{1,0:T(8,128)(2,1)S(1)}, bf16[576,640]{1,0:T(8,128)(2,1)S(1)}, bf16[288,640]{1,0:T(8,128)(2...) custom-call(f32[1,4]{1,0:T(1,128)S(1)} %add_convert_fusion.flags_ref, ...), custom_call_target="tpu_custom_call" | custom-call | tf_op jit(solution)/shard_map/pallas_call | solution.py:75
  17.5 0.2 collective-permute-start.6
  17.8 0.4 collective-permute-start.7
  18.1 2.1 %collective-permute-start.5 = (bf16[320,640]{1,0:T(8,128)(2,1)S(1)}, bf16[320,640]{1,0:T(8,128)(2,1)S(1)}, u32[]{:S(2)}, u32[]{:S(2)}) collective-permute-start(bf16[320,640]{1,0:T(8,128)(2,1)S(1)} %get-tuple-element.33), channel_id=1, source_target_pairs={{0,2},{1,3},{2,0},{3,1},{4,6},{5,7},{6,4},{7,5},{8,10},{9,11},{10,... | collective-permute-start | bytes 1228808 | tf_op jit(solution)/shard_map/ppermute | solution.py:474
  20.3 0.0 collective-permute-done.3.value_ref
  20.3 0.0 collective-permute-start.9
  20.3 0.0 collective-permute-done.6.refs_2_
  20.3 1.7 %collective-permute-start.4 = (bf16[288,640]{1,0:T(8,128)(2,1)S(1)}, bf16[288,640]{1,0:T(8,128)(2,1)S(1)}, u32[]{:S(2)}, u32[]{:S(2)}) collective-permute-start(bf16[288,640]{1,0:T(8,128)(2,1)S(1)} %shard_map.140.refs_6_), channel_id=1, source_target_pairs={{0,32},{4,36},{8,40},{12,44},{16,48},{20,52},{24,56},{28,60},{32,0... | collective-permute-start | bytes 1105928 | tf_op jit(solution)/shard_map/ppermute | solution.py:538
  22.0 0.0 collective-permute-done.7.refs_3_
  22.0 1.4 %collective-permute-start.2 = (bf16[256,640]{1,0:T(8,128)(2,1)S(1)}, bf16[256,640]{1,0:T(8,128)(2,1)S(1)}, u32[]{:S(2)}, u32[]{:S(2)}) collective-permute-start(bf16[256,640]{1,0:T(8,128)(2,1)S(1)} %get-tuple-element.31), channel_id=1, source_target_pairs={{0,2},{1,3},{2,0},{3,1},{4,6},{5,7},{6,4},{7,5},{8,10},{9,11},{10,... | collective-permute-start | bytes 983048 | tf_op jit(solution)/shard_map/ppermute | solution.py:474
  23.3 0.0 collective-permute-done.9.refs_7_.refs_1_
  23.3 0.0 collective-permute-done.8.refs_5_
  23.4 7.5 %shard_map.141.before_ref.refs_4_ = f32[576,768]{1,0:T(8,128)S(1)} custom-call(bf16[576,384]{1,0:T(8,128)(2,1)S(1)} %get-tuple-element.30.before_ref.refs_0_.query_ref, bf16[576,640]{1,0:T(8,128)(2,1)S(1)} %get-tuple-element.34.refs_1_, bf16[288,640]{1,0:T(8,128)(2,1)S(1)} %collective-permute-done.6.refs_2_, ...), custom_call_target="tpu_custom_call" | custom-call | tf_op jit(solution)/shard_map/pallas_call | solution.py:75
  30.8 1.1 %collective-permute-done.5.second_ref = bf16[320,640]{1,0:T(8,128)(2,1)S(1)} collective-permute-done((bf16[320,640]{1,0:T(8,128)(2,1)S(1)}, bf16[320,640]{1,0:T(8,128)(2,1)S(1)}, u32[]{:S(2)}, u32[]{:S(2)}) %collective-permute-start.5) | collective-permute-done | bytes 409632 | tf_op jit(solution)/shard_map/ppermute | solution.py:474
  31.9 0.0 collective-permute-done.4.first_ref
  32.0 0.1 shard_map.142
  32.0 0.1 collective-permute-start.12
  32.1 0.5 collective-permute-start.13
  32.6 0.1 collective-permute-start.10
  32.7 0.4 collective-permute-start.11
  33.1 0.9 shard_map.143.refs_8_
  34.0 0.1 collective-permute-done.10.refs_2_
  34.1 0.3 collective-permute-done.11.refs_3_
  34.4 0.0 collective-permute-done.12.refs_6_
  34.4 0.0 collective-permute-done.13.refs_7_
  34.4 2.8 %shard_map.144.before_ref.refs_2_ = f32[576,768]{1,0:T(8,128)S(1)} custom-call(bf16[576,384]{1,0:T(8,128)(2,1)S(1)} %get-tuple-element.30.before_ref.refs_0_.query_ref, bf16[144,640]{1,0:T(8,128)(2,1)S(1)} %get-tuple-element.38.refs_3_.refs_1_, bf16[144,640]{1,0:T(8,128)(2,1)S(1)} %collective-permute-done.10.refs_2_, ...), custom_call_target="tpu_custom_call" | custom-call | tf_op jit(solution)/shard_map/pallas_call | solution.py:75
  37.2 1.0 collective-permute-done.2.value_ref
  38.2 0.0 collective-permute-start.14
  38.2 0.9 shard_map.146.acc_ref
  39.1 0.7 collective-permute-done.14.kv_ref
  39.8 0.0 copy-done.5
  39.8 0.0 copy-done.12
  39.8 0.0 copy-start.4
  39.8 1.8 %shard_map.147 = (bf16[576,640]{1,0:T(8,128)(2,1)S(1)}, bf16[3072,128]{1,0:T(8,128)(2,1)S(1)}) custom-call(bf16[576,384]{1,0:T(8,128)(2,1)S(1)} %get-tuple-element.30.before_ref.refs_0_.query_ref, f32[576,768]{1,0:T(8,128)S(1)} %shard_map.146.acc_ref, bf16[256,640]{1,0:T(8,128)(2,1)S(1)} %collective-permute-done.14.kv_ref, ...), custom_call_target="tpu_custom_call" | custom-call | tf_op jit(solution)/shard_map/pallas_call | solution.py:75
  41.7 35.5 %all_to_all.10 = bf16[64,48,128]{2,1,0:T(8,128)(2,1)S(1)} all-to-all(bf16[64,48,128]{2,1,0:T(8,128)(2,1)S(1)} %bitcast.24), channel_id=1, replica_groups={{0,128,32,160,64,192,96,224,4,132,36,164,68,196,100,228,8,136,40,168,72..., dimensions={0} | all-to-all | bytes 1572864 | tf_op jit(solution)/shard_map/all_to_all | solution.py:586
  77.2 0.0 copy-done.2
  77.2 0.0 copy-done.3
  77.2 0.0 copy-done.4
  77.2 2.1 %shard_map.148 = bf16[1536,128]{1,0:T(8,128)(2,1)S(1)} custom-call(bf16[3072,128]{1,0:T(8,128)(2,1)S(1)} %bitcast.21, bf16[320,640]{1,0:T(8,128)(2,1)S(1)} %bitcast.27, bf16[320,640]{1,0:T(8,128)(2,1)S(1)} %bitcast.28, bf16[320,640]{1,0:T(8,128)(2,1)S(1)} %bitcast.29), custom_call_target="tpu_custom_call" | custom-call | tf_op jit(solution)/shard_map/pallas_call | solution.py:75
  79.3 21.0 %all_to_all.11 = bf16[64,24,128]{2,1,0:T(8,128)(2,1)S(1)} all-to-all(bf16[64,24,128]{2,1,0:T(8,128)(2,1)S(1)} %bitcast.22), channel_id=1, replica_groups={{0,128,32,160,64,192,96,224,4,132,36,164,68,196,100,228,8,136,40,168,72..., dimensions={0} | all-to-all | bytes 786432 | tf_op jit(solution)/shard_map/all_to_all | solution.py:605
  100.3 0.0 copy-done.6
  100.3 1.4 %shard_map.149 = bf16[576,640]{1,0:T(8,128)(2,1)} custom-call(bf16[1536,128]{1,0:T(8,128)(2,1)S(1)} %bitcast.23, bf16[320,640]{1,0:T(8,128)(2,1)S(1)} %copy-done.6, bf16[576,640]{1,0:T(8,128)(2,1)S(1)} %get-tuple-element.44.mixed_ref), custom_call_target="tpu_custom_call" | custom-call | tf_op jit(solution)/shard_map/pallas_call | solution.py:75
  (16 shorter events, 0.1 us)
Async XLA Ops:
  0.1 1.1 %copy-start = (bf16[1,12,48,640]{3,2,1,0:T(8,128)(2,1)S(1)}, bf16[1,12,48,640]{3,2,1,0:T(8,128)(2,1)}, u32[]{:S(2)}) copy-start(bf16[1,12,48,640]{3,2,1,0:T(8,128)(2,1)} %param.14) | copy-start | bytes 2211844
  1.2 8.5 %slice-start = ((s8[7372800]{0:T(1024)(128)(4,1)}), s8[4194304]{0:T(1024)(128)(4,1)S(1)}, s32[]{:S(2)}) async-start(s8[7372800]{0:T(1024)(128)(4,1)} %bitcast.18), calls=%async_computation.2 | async-start | bytes 8388608
  2.3 1.4 %collective-permute-start = (bf16[64,640]{1,0:T(8,128)(2,1)S(1)}, bf16[64,640]{1,0:T(8,128)(2,1)S(1)}, u32[]{:S(2)}, u32[]{:S(2)}) collective-permute-start(bf16[64,640]{1,0:T(8,128)(2,1)S(1)} %get-tuple-element.26), channel_id=1, source_target_pairs={{0,1},{1,0},{2,3},{3,2},{4,5},{5,4},{6,7},{7,6},{8,9},{9,8},{10,11... | collective-permute-start | bytes 245768 | tf_op jit(solution)/shard_map/ppermute | solution.py:474
  3.6 2.0 %copy-start.8 = (bf16[640,320]{0,1:T(8,128)(2,1)S(1)}, bf16[640,320]{0,1:T(8,128)(2,1)}, u32[]{:S(2)}) copy-start(bf16[640,320]{0,1:T(8,128)(2,1)} %param.20) | copy-start | bytes 1228804
  3.6 2.0 %copy-start.9 = (bf16[640,320]{0,1:T(8,128)(2,1)S(1)}, bf16[640,320]{0,1:T(8,128)(2,1)}, u32[]{:S(2)}) copy-start(bf16[640,320]{0,1:T(8,128)(2,1)} %param.21) | copy-start | bytes 1228804
  3.6 2.0 %copy-start.13 = (bf16[12,48,640]{2,1,0:T(8,128)(2,1)S(1)}, bf16[12,48,640]{2,1,0:T(8,128)(2,1)}, u32[]{:S(2)}) copy-start(bf16[12,48,640]{2,1,0:T(8,128)(2,1)} %param.15) | copy-start | bytes 2211844
  3.6 6.1 %slice-start.1 = ((s8[7372800]{0:T(1024)(128)(4,1)}), s8[3178496]{0:T(1024)(128)(4,1)S(1)}, s32[]{:S(2)}) async-start(s8[7372800]{0:T(1024)(128)(4,1)} %bitcast.18), calls=%async_computation.3 | async-start | bytes 6356992
  3.7 6.0 %collective-permute-start.1 = (bf16[64,640]{1,0:T(8,128)(2,1)S(1)}, bf16[64,640]{1,0:T(8,128)(2,1)S(1)}, u32[]{:S(2)}, u32[]{:S(2)}) collective-permute-start(bf16[64,640]{1,0:T(8,128)(2,1)S(1)} %get-tuple-element.29), channel_id=1, source_target_pairs={{0,3},{1,2},{2,1},{3,0},{4,7},{5,6},{6,5},{7,4},{8,11},{9,10},{10,... | collective-permute-start | bytes 245768 | tf_op jit(solution)/shard_map/ppermute | solution.py:474
  5.7 4.0 %copy-start.1 = (bf16[1,12,48,640]{3,2,1,0:T(8,128)(2,1)S(1)}, bf16[1,12,48,640]{3,2,1,0:T(8,128)(2,1)}, u32[]{:S(2)}) copy-start(bf16[1,12,48,640]{3,2,1,0:T(8,128)(2,1)} %param.14) | copy-start | bytes 2211844
  5.7 4.0 %copy-start.7 = (bf16[640,320]{0,1:T(8,128)(2,1)S(1)}, bf16[640,320]{0,1:T(8,128)(2,1)}, u32[]{:S(2)}) copy-start(bf16[640,320]{0,1:T(8,128)(2,1)} %param.19) | copy-start | bytes 1228804
  5.7 4.0 %copy-start.10 = (f32[640]{0:T(1024)S(1)}, f32[640]{0:T(1024)}, u32[]{:S(2)}) copy-start(f32[640]{0:T(1024)} %gain_ref.2) | copy-start | bytes 7684
  5.7 4.0 %copy-start.11 = (f32[640]{0:T(1024)S(1)}, f32[640]{0:T(1024)}, u32[]{:S(2)}) copy-start(f32[640]{0:T(1024)} %norm_gain_ref.1) | copy-start | bytes 7684
  7.4 12.8 %collective-permute-start.3 = (bf16[288,640]{1,0:T(8,128)(2,1)S(1)}, bf16[288,640]{1,0:T(8,128)(2,1)S(1)}, u32[]{:S(2)}, u32[]{:S(2)}) collective-permute-start(bf16[288,640]{1,0:T(8,128)(2,1)S(1)} %get-tuple-element.32), channel_id=1, source_target_pairs={{0,2},{1,3},{2,0},{3,1},{4,6},{5,7},{6,4},{7,5},{8,10},{9,11},{10,... | collective-permute-start | bytes 1105928 | tf_op jit(solution)/shard_map/ppermute | solution.py:474
  9.0 14.4 %collective-permute-start.8 = (bf16[576,640]{1,0:T(8,128)(2,1)S(1)}, bf16[576,640]{1,0:T(8,128)(2,1)S(1)}, u32[]{:S(2)}, u32[]{:S(2)}) collective-permute-start(bf16[576,640]{1,0:T(8,128)(2,1)S(1)} %get-tuple-element.37.refs_4_), channel_id=1, source_target_pairs={{0,1},{1,0},{2,3},{3,2},{4,5},{5,4},{6,7},{7,6},{8,9},{9,8},{10,11... | collective-permute-start | bytes 2211848 | tf_op jit(solution)/shard_map/ppermute | solution.py:474
  17.5 2.7 %collective-permute-start.6 = (bf16[288,640]{1,0:T(8,128)(2,1)S(1)}, bf16[288,640]{1,0:T(8,128)(2,1)S(1)}, u32[]{:S(2)}, u32[]{:S(2)}) collective-permute-start(bf16[288,640]{1,0:T(8,128)(2,1)S(1)} %get-tuple-element.35), channel_id=1, source_target_pairs={{0,1},{1,0},{2,3},{3,2},{4,5},{5,4},{6,7},{7,6},{8,9},{9,8},{10,11... | collective-permute-start | bytes 1105928 | tf_op jit(solution)/shard_map/ppermute | solution.py:474
  17.8 4.2 %collective-permute-start.7 = (bf16[288,640]{1,0:T(8,128)(2,1)S(1)}, bf16[288,640]{1,0:T(8,128)(2,1)S(1)}, u32[]{:S(2)}, u32[]{:S(2)}) collective-permute-start(bf16[288,640]{1,0:T(8,128)(2,1)S(1)} %get-tuple-element.36), channel_id=1, source_target_pairs={{0,1},{1,0},{2,3},{3,2},{4,5},{5,4},{6,7},{7,6},{8,9},{9,8},{10,11... | collective-permute-start | bytes 1105928 | tf_op jit(solution)/shard_map/ppermute | solution.py:474
  18.1 13.8 %collective-permute-start.5 = (bf16[320,640]{1,0:T(8,128)(2,1)S(1)}, bf16[320,640]{1,0:T(8,128)(2,1)S(1)}, u32[]{:S(2)}, u32[]{:S(2)}) collective-permute-start(bf16[320,640]{1,0:T(8,128)(2,1)S(1)} %get-tuple-element.33), channel_id=1, source_target_pairs={{0,2},{1,3},{2,0},{3,1},{4,6},{5,7},{6,4},{7,5},{8,10},{9,11},{10,... | collective-permute-start | bytes 1228808 | tf_op jit(solution)/shard_map/ppermute | solution.py:474
  20.3 3.1 %collective-permute-start.9 = (bf16[288,640]{1,0:T(8,128)(2,1)S(1)}, bf16[288,640]{1,0:T(8,128)(2,1)S(1)}, u32[]{:S(2)}, u32[]{:S(2)}) collective-permute-start(bf16[288,640]{1,0:T(8,128)(2,1)S(1)} %shard_map.140.refs_6_), channel_id=1, source_target_pairs={{0,1},{1,0},{2,3},{3,2},{4,5},{5,4},{6,7},{7,6},{8,9},{9,8},{10,11... | collective-permute-start | bytes 1105928 | tf_op jit(solution)/shard_map/ppermute | solution.py:474
  20.3 11.7 %collective-permute-start.4 = (bf16[288,640]{1,0:T(8,128)(2,1)S(1)}, bf16[288,640]{1,0:T(8,128)(2,1)S(1)}, u32[]{:S(2)}, u32[]{:S(2)}) collective-permute-start(bf16[288,640]{1,0:T(8,128)(2,1)S(1)} %shard_map.140.refs_6_), channel_id=1, source_target_pairs={{0,32},{4,36},{8,40},{12,44},{16,48},{20,52},{24,56},{28,60},{32,0... | collective-permute-start | bytes 1105928 | tf_op jit(solution)/shard_map/ppermute | solution.py:538
  22.0 16.2 %collective-permute-start.2 = (bf16[256,640]{1,0:T(8,128)(2,1)S(1)}, bf16[256,640]{1,0:T(8,128)(2,1)S(1)}, u32[]{:S(2)}, u32[]{:S(2)}) collective-permute-start(bf16[256,640]{1,0:T(8,128)(2,1)S(1)} %get-tuple-element.31), channel_id=1, source_target_pairs={{0,2},{1,3},{2,0},{3,1},{4,6},{5,7},{6,4},{7,5},{8,10},{9,11},{10,... | collective-permute-start | bytes 983048 | tf_op jit(solution)/shard_map/ppermute | solution.py:474
  32.0 2.4 %collective-permute-start.12 = (bf16[160,640]{1,0:T(8,128)(2,1)S(1)}, bf16[160,640]{1,0:T(8,128)(2,1)S(1)}, u32[]{:S(2)}, u32[]{:S(2)}) collective-permute-start(bf16[160,640]{1,0:T(8,128)(2,1)S(1)} %get-tuple-element.40.refs_4_), channel_id=1, source_target_pairs={{0,1},{1,0},{2,3},{3,2},{4,5},{5,4},{6,7},{7,6},{8,9},{9,8},{10,11... | collective-permute-start | bytes 614408 | tf_op jit(solution)/shard_map/ppermute | solution.py:474
  32.1 2.3 %collective-permute-start.13 = (bf16[160,640]{1,0:T(8,128)(2,1)S(1)}, bf16[160,640]{1,0:T(8,128)(2,1)S(1)}, u32[]{:S(2)}, u32[]{:S(2)}) collective-permute-start(bf16[160,640]{1,0:T(8,128)(2,1)S(1)} %get-tuple-element.41.refs_5_), channel_id=1, source_target_pairs={{0,1},{1,0},{2,3},{3,2},{4,5},{5,4},{6,7},{7,6},{8,9},{9,8},{10,11... | collective-permute-start | bytes 614408 | tf_op jit(solution)/shard_map/ppermute | solution.py:474
  32.6 1.5 %collective-permute-start.10 = (bf16[144,640]{1,0:T(8,128)(2,1)S(1)}, bf16[144,640]{1,0:T(8,128)(2,1)S(1)}, u32[]{:S(2)}, u32[]{:S(2)}) collective-permute-start(bf16[144,640]{1,0:T(8,128)(2,1)S(1)} %get-tuple-element.39.refs_2_), channel_id=1, source_target_pairs={{0,1},{1,0},{2,3},{3,2},{4,5},{5,4},{6,7},{7,6},{8,9},{9,8},{10,11... | collective-permute-start | bytes 552968 | tf_op jit(solution)/shard_map/ppermute | solution.py:474
  32.7 1.7 %collective-permute-start.11 = (bf16[144,640]{1,0:T(8,128)(2,1)S(1)}, bf16[144,640]{1,0:T(8,128)(2,1)S(1)}, u32[]{:S(2)}, u32[]{:S(2)}) collective-permute-start(bf16[144,640]{1,0:T(8,128)(2,1)S(1)} %get-tuple-element.38.refs_3_.refs_1_), channel_id=1, source_target_pairs={{0,1},{1,0},{2,3},{3,2},{4,5},{5,4},{6,7},{7,6},{8,9},{9,8},{10,11... | collective-permute-start | bytes 552968 | tf_op jit(solution)/shard_map/ppermute | solution.py:474
  38.2 1.6 %copy-start.5 = (bf16[320,640]{1,0:T(8,128)(2,1)S(1)}, bf16[320,640]{1,0:T(8,128)(2,1)}, u32[]{:S(2)}) copy-start(bf16[320,640]{1,0:T(8,128)(2,1)} %weight_ref.2) | copy-start | bytes 1228804
  38.2 1.6 %copy-start.12 = (f32[640]{0:T(1024)S(1)}, f32[640]{0:T(1024)}, u32[]{:S(2)}) copy-start(f32[640]{0:T(1024)} %gain_ref.3) | copy-start | bytes 7684
  38.2 1.6 %collective-permute-start.14 = (bf16[256,640]{1,0:T(8,128)(2,1)S(1)}, bf16[256,640]{1,0:T(8,128)(2,1)S(1)}, u32[]{:S(2)}, u32[]{:S(2)}) collective-permute-start(bf16[256,640]{1,0:T(8,128)(2,1)S(1)} %shard_map.145.refs_1_), channel_id=1, source_target_pairs={{0,1},{1,0},{2,3},{3,2},{4,5},{5,4},{6,7},{7,6},{8,9},{9,8},{10,11... | collective-permute-start | bytes 983048 | tf_op jit(solution)/shard_map/ppermute | solution.py:474
  39.8 37.4 %copy-start.2 = (bf16[640,320]{0,1:T(8,128)(2,1)S(1)}, bf16[640,320]{0,1:T(8,128)(2,1)}, u32[]{:S(2)}) copy-start(bf16[640,320]{0,1:T(8,128)(2,1)} %param.24) | copy-start | bytes 1228804
  39.8 37.4 %copy-start.3 = (bf16[640,320]{0,1:T(8,128)(2,1)S(1)}, bf16[640,320]{0,1:T(8,128)(2,1)}, u32[]{:S(2)}) copy-start(bf16[640,320]{0,1:T(8,128)(2,1)} %param.25) | copy-start | bytes 1228804
  39.8 37.4 %copy-start.4 = (bf16[640,320]{0,1:T(8,128)(2,1)S(1)}, bf16[640,320]{0,1:T(8,128)(2,1)}, u32[]{:S(2)}) copy-start(bf16[640,320]{0,1:T(8,128)(2,1)} %param.26) | copy-start | bytes 1228804
  77.2 23.1 %copy-start.6 = (bf16[320,640]{1,0:T(8,128)(2,1)S(1)}, bf16[320,640]{1,0:T(8,128)(2,1)}, u32[]{:S(2)}) copy-start(bf16[320,640]{1,0:T(8,128)(2,1)} %weight_ref.3) | copy-start | bytes 1228804

commit v6 on v5

--- a/solution.py
+++ b/solution.py
@@ -143,11 +143,10 @@
 
 
 def reference_kernel(
-    flags_ref, states_ref, before_ref, key_ref, value_ref, out_ref, half_ref, weight
+    flags_ref, states_ref, before_ref, key_ref, value_ref, query_ref, out_ref, half_ref, weight
 ):
-    weight[0:INNER, :] = key_ref[...]
-    weight[INNER:, :] = value_ref[...]
-    out_ref[...] = reference_kv(weight, states_ref[...])
+    joined_weights(weight, key_ref, value_ref, query_ref)
+    out_ref[...] = reference_kv(weight.at[0:C], states_ref[...])
     half_ref[...] = jnp.where(flags_ref[0, 3] > 0.5, out_ref[PART:, :], out_ref[0:PART, :])
 
 
@@ -173,9 +172,7 @@
     gain_ref,
     kernel_ref,
     norm_gain_ref,
-    query_ref,
-    key_ref,
-    value_ref,
+    weight,
     hidden_out,
     query_out,
     kv_out,
@@ -184,9 +181,7 @@
     first_out,
     second_out,
     lhs,
-    weight,
 ):
-    joined_weights(weight, key_ref, value_ref, query_ref)
     group_sum, group_sq = sums_of(far_ref[W:, :].astype(f32))
     members = float(4 * CELLS * (C // GROUPS))
     average = (group_sum + sums_ref[0:1]) / members
@@ -490,11 +485,10 @@
     )
     far = swap(far, 3)
 
-    ref_kv, half = call(
+    ref_kv, half, weight = call(
         reference_kernel,
-        [struct((CELLS, C), bf16), struct((CELLS // 2, C), bf16)],
-        [flags, states, sums, spatial_key.T, spatial_value.T],
-        scratch=[pltpu.VMEM((C, C), bf16)],
+        [struct((CELLS, C), bf16), struct((PART, C), bf16), struct((C + INNER, C), bf16)],
+        [flags, states, sums, spatial_key.T, spatial_value.T, spatial_query.T],
         smem=1,
         flops=2 * 10**9,
         limit=8,
@@ -521,13 +515,10 @@
             group_gain,
             conv_weight.reshape(3, 3 * C, C),
             norm_gain,
-            spatial_query.T,
-            spatial_key.T,
-            spatial_value.T,
+            weight,
         ],
         scratch=[
             pltpu.VMEM(((STRIP + 2) * W, 3 * C), bf16),
-            pltpu.VMEM((C + INNER, C), bf16),
         ],
         smem=1,
         limit=16,

time: 102 us -> 102 us (level)
  no operation moved by 1% of the time
where the time goes in v6:
time: 102 us
  blocking collectives  56.5 us (55%)
  Pallas kernels  28 us (27%)
  starting transfers between devices  10.6 us (10%)
  waiting for transfers between devices  5.09 us (5%)
  local copies, waits for them, and re-layouts  1.19 us (1%)
    all_to_all x1, blocking collectives, on_device(): lax.all_to_all(sent.reshape(FRAMES, SENT, LANES), 'frame', split_axis=0,...  35.5 us
    pallas_call x12, Pallas kernels, call(): pl.pallas_call(body, out_shape=outs, in_specs=specs, out_specs=pl.BlockSp...  28 us
    all_to_all x1, blocking collectives, on_device(): lax.all_to_all(back.reshape(FRAMES, BACK, LANES), 'frame', split_axis=0,...  21 us
    ppermute x14, starting transfers between devices, swap(): return lax.ppermute(value, 'space', [(i, i ^ k) for i in range(4)])  8.91 us
    ppermute x14, waiting for transfers between devices, swap(): return lax.ppermute(value, 'space', [(i, i ^ k) for i in range(4)])  5.09 us
  transfers between devices with their start and end apart: 15, of which 7 were waited for; matrix products, arithmetic and copies ran while one was open for 0% of the time, Pallas kernels for 21%

profile of v6, /device:TPU:2, one launch (start us, length us, event | category | flops | bytes accessed | tf_op | source)
XLA Modules:
  0.0 101.8 jit_solution(85979987811449991)
XLA Ops:
  0.0 0.1 add_convert_fusion.flags_ref
  0.1 1.1 %copy-done = bf16[1,12,48,640]{3,2,1,0:T(8,128)(2,1)S(1)} copy-done((bf16[1,12,48,640]{3,2,1,0:T(8,128)(2,1)S(1)}, bf16[1,12,48,640]{3,2,1,0:T(8,128)(2,1)}, u32[]{:S(2)}) %copy-start) | copy-done | bytes 737304
  1.2 1.1 %shard_map.136 = (f32[8,640]{1,0:T(8,128)S(1)}, bf16[64,640]{1,0:T(8,128)(2,1)S(1)}, bf16[48,640]{1,0:T(8,128)(2,1)S(1)}) custom-call(f32[1,4]{1,0:T(1,128)S(1)} %add_convert_fusion.flags_ref, bf16[576,640]{1,0:T(8,128)(2,1)S(1)} %bitcast.25), custom_call_target="tpu_custom_call" | custom-call | flops 2000000000 | tf_op jit(solution)/shard_map/pallas_call | solution.py:75
  2.3 0.1 collective-permute-start
  2.4 1.3 %collective-permute-done.near_ref = bf16[64,640]{1,0:T(8,128)(2,1)S(1)} collective-permute-done((bf16[64,640]{1,0:T(8,128)(2,1)S(1)}, bf16[64,640]{1,0:T(8,128)(2,1)S(1)}, u32[]{:S(2)}, u32[]{:S(2)}) %collective-permute-start) | collective-permute-done | bytes 81952 | tf_op jit(solution)/shard_map/ppermute | solution.py:469
  3.7 0.0 slice-start.1
  3.7 2.0 %collective-permute-start.1 = (bf16[64,640]{1,0:T(8,128)(2,1)S(1)}, bf16[64,640]{1,0:T(8,128)(2,1)S(1)}, u32[]{:S(2)}, u32[]{:S(2)}) collective-permute-start(bf16[64,640]{1,0:T(8,128)(2,1)S(1)} %get-tuple-element.30), channel_id=1, source_target_pairs={{0,3},{1,2},{2,1},{3,0},{4,7},{5,6},{6,5},{7,4},{8,11},{9,10},{10,... | collective-permute-start | bytes 245768 | tf_op jit(solution)/shard_map/ppermute | solution.py:469
  5.7 0.0 copy-done.10
  5.7 0.0 copy-done.11
  5.7 0.0 copy-done.12
  5.7 0.0 copy-done.13
  5.7 0.0 copy-start.1
  5.7 0.0 copy-start.7
  5.7 0.0 copy-start.8
  5.7 1.7 %shard_map.138 = (bf16[576,640]{1,0:T(8,128)(2,1)S(1)}, bf16[288,640]{1,0:T(8,128)(2,1)S(1)}, bf16[960,640]{1,0:T(8,128)(2,1)S(1)}) custom-call(f32[1,4]{1,0:T(1,128)S(1)} %add_convert_fusion.flags_ref, bf16[576,640]{1,0:T(8,128)(2,1)S(1)} %bitcast.30, f32[8,640]{1,0:T(8,128)S(1)} %get-tuple-element.29.before_ref.sums_ref, bf16[320,640]{1,0:T(8,128)(2,1)S(1)} %bitcast.31, ...), custom_call_target="tpu_custom_call" | custom-call | flops 2000000000 | tf_op jit(solution)/shard_map/pallas_call | solution.py:75
  7.5 1.6 %collective-permute-start.3 = (bf16[288,640]{1,0:T(8,128)(2,1)S(1)}, bf16[288,640]{1,0:T(8,128)(2,1)S(1)}, u32[]{:S(2)}, u32[]{:S(2)}) collective-permute-start(bf16[288,640]{1,0:T(8,128)(2,1)S(1)} %get-tuple-element.34), channel_id=1, source_target_pairs={{0,2},{1,3},{2,0},{3,1},{4,6},{5,7},{6,4},{7,5},{8,10},{9,11},{10,... | collective-permute-start | bytes 1105928 | tf_op jit(solution)/shard_map/ppermute | solution.py:469
  9.1 0.0 collective-permute-start.8
  9.1 0.6 collective-permute-done.1.far_ref
  9.7 0.0 slice-done
  9.7 0.0 slice-done.1
  9.7 0.0 copy-done.1
  9.7 0.0 copy-done.7
  9.7 0.0 copy-done.8
  9.8 7.7 %shard_map.139 = (bf16[576,640]{1,0:T(8,128)(2,1)S(1)}, bf16[576,384]{1,0:T(8,128)(2,1)S(1)}, bf16[576,640]{1,0:T(8,128)(2,1)S(1)}, bf16[288,640]{1,0:T(8,128)(2...) custom-call(f32[1,4]{1,0:T(1,128)S(1)} %add_convert_fusion.flags_ref, ...), custom_call_target="tpu_custom_call" | custom-call | tf_op jit(solution)/shard_map/pallas_call | solution.py:75
  17.5 0.2 collective-permute-start.6
  17.7 0.4 collective-permute-start.7
  18.1 2.1 %collective-permute-start.5 = (bf16[320,640]{1,0:T(8,128)(2,1)S(1)}, bf16[320,640]{1,0:T(8,128)(2,1)S(1)}, u32[]{:S(2)}, u32[]{:S(2)}) collective-permute-start(bf16[320,640]{1,0:T(8,128)(2,1)S(1)} %get-tuple-element.35), channel_id=1, source_target_pairs={{0,2},{1,3},{2,0},{3,1},{4,6},{5,7},{6,4},{7,5},{8,10},{9,11},{10,... | collective-permute-start | bytes 1228808 | tf_op jit(solution)/shard_map/ppermute | solution.py:469
  20.2 0.0 collective-permute-done.3.value_ref
  20.2 0.0 collective-permute-start.9
  20.2 0.0 collective-permute-done.6.refs_2_
  20.2 1.7 %collective-permute-start.4 = (bf16[288,640]{1,0:T(8,128)(2,1)S(1)}, bf16[288,640]{1,0:T(8,128)(2,1)S(1)}, u32[]{:S(2)}, u32[]{:S(2)}) collective-permute-start(bf16[288,640]{1,0:T(8,128)(2,1)S(1)} %shard_map.140.refs_6_), channel_id=1, source_target_pairs={{0,32},{4,36},{8,40},{12,44},{16,48},{20,52},{24,56},{28,60},{32,0... | collective-permute-start | bytes 1105928 | tf_op jit(solution)/shard_map/ppermute | solution.py:529
  21.9 0.0 collective-permute-done.7.refs_3_
  21.9 1.4 %collective-permute-start.2 = (bf16[256,640]{1,0:T(8,128)(2,1)S(1)}, bf16[256,640]{1,0:T(8,128)(2,1)S(1)}, u32[]{:S(2)}, u32[]{:S(2)}) collective-permute-start(bf16[256,640]{1,0:T(8,128)(2,1)S(1)} %get-tuple-element.33), channel_id=1, source_target_pairs={{0,2},{1,3},{2,0},{3,1},{4,6},{5,7},{6,4},{7,5},{8,10},{9,11},{10,... | collective-permute-start | bytes 983048 | tf_op jit(solution)/shard_map/ppermute | solution.py:469
  23.3 0.0 collective-permute-done.9.refs_7_.refs_1_
  23.3 0.0 collective-permute-done.8.refs_5_
  23.3 7.5 %shard_map.141.before_ref.refs_4_ = f32[576,768]{1,0:T(8,128)S(1)} custom-call(bf16[576,384]{1,0:T(8,128)(2,1)S(1)} %get-tuple-element.32.before_ref.refs_0_.query_ref, bf16[576,640]{1,0:T(8,128)(2,1)S(1)} %get-tuple-element.36.refs_1_, bf16[288,640]{1,0:T(8,128)(2,1)S(1)} %collective-permute-done.6.refs_2_, ...), custom_call_target="tpu_custom_call" | custom-call | tf_op jit(solution)/shard_map/pallas_call | solution.py:75
  30.8 1.1 %collective-permute-done.5.second_ref = bf16[320,640]{1,0:T(8,128)(2,1)S(1)} collective-permute-done((bf16[320,640]{1,0:T(8,128)(2,1)S(1)}, bf16[320,640]{1,0:T(8,128)(2,1)S(1)}, u32[]{:S(2)}, u32[]{:S(2)}) %collective-permute-start.5) | collective-permute-done | bytes 409632 | tf_op jit(solution)/shard_map/ppermute | solution.py:469
  31.9 0.0 collective-permute-done.4.first_ref
  31.9 0.1 shard_map.142
  32.0 0.1 collective-permute-start.12
  32.1 0.5 collective-permute-start.13
  32.6 0.1 collective-permute-start.10
  32.7 0.4 collective-permute-start.11
  33.1 0.9 shard_map.143.refs_8_
  34.0 0.1 collective-permute-done.10.refs_2_
  34.1 0.3 collective-permute-done.11.refs_3_
  34.3 0.0 collective-permute-done.12.refs_6_
  34.3 0.0 collective-permute-done.13.refs_7_
  34.3 2.8 %shard_map.144.before_ref.refs_2_ = f32[576,768]{1,0:T(8,128)S(1)} custom-call(bf16[576,384]{1,0:T(8,128)(2,1)S(1)} %get-tuple-element.32.before_ref.refs_0_.query_ref, bf16[144,640]{1,0:T(8,128)(2,1)S(1)} %get-tuple-element.40.refs_3_.refs_1_, bf16[144,640]{1,0:T(8,128)(2,1)S(1)} %collective-permute-done.10.refs_2_, ...), custom_call_target="tpu_custom_call" | custom-call | tf_op jit(solution)/shard_map/pallas_call | solution.py:75
  37.2 1.0 collective-permute-done.2.value_ref
  38.1 0.0 collective-permute-start.14
  38.2 0.9 shard_map.146.acc_ref
  39.1 0.7 collective-permute-done.14.kv_ref
  39.8 0.0 copy-done.5
  39.8 0.0 copy-done.9
  39.8 0.0 copy-start.4
  39.8 1.8 %shard_map.147 = (bf16[576,640]{1,0:T(8,128)(2,1)S(1)}, bf16[3072,128]{1,0:T(8,128)(2,1)S(1)}) custom-call(bf16[576,384]{1,0:T(8,128)(2,1)S(1)} %get-tuple-element.32.before_ref.refs_0_.query_ref, f32[576,768]{1,0:T(8,128)S(1)} %shard_map.146.acc_ref, bf16[256,640]{1,0:T(8,128)(2,1)S(1)} %collective-permute-done.14.kv_ref, ...), custom_call_target="tpu_custom_call" | custom-call | tf_op jit(solution)/shard_map/pallas_call | solution.py:75
  41.6 35.5 %all_to_all.10 = bf16[64,48,128]{2,1,0:T(8,128)(2,1)S(1)} all-to-all(bf16[64,48,128]{2,1,0:T(8,128)(2,1)S(1)} %bitcast.24), channel_id=1, replica_groups={{0,128,32,160,64,192,96,224,4,132,36,164,68,196,100,228,8,136,40,168,72..., dimensions={0} | all-to-all | bytes 1572864 | tf_op jit(solution)/shard_map/all_to_all | solution.py:577
  77.1 0.0 copy-done.2
  77.1 0.0 copy-done.3
  77.1 0.0 copy-done.4
  77.1 2.1 %shard_map.148 = bf16[1536,128]{1,0:T(8,128)(2,1)S(1)} custom-call(bf16[3072,128]{1,0:T(8,128)(2,1)S(1)} %bitcast.21, bf16[320,640]{1,0:T(8,128)(2,1)S(1)} %bitcast.27, bf16[320,640]{1,0:T(8,128)(2,1)S(1)} %bitcast.28, bf16[320,640]{1,0:T(8,128)(2,1)S(1)} %bitcast.29), custom_call_target="tpu_custom_call" | custom-call | tf_op jit(solution)/shard_map/pallas_call | solution.py:75
  79.2 21.0 %all_to_all.11 = bf16[64,24,128]{2,1,0:T(8,128)(2,1)S(1)} all-to-all(bf16[64,24,128]{2,1,0:T(8,128)(2,1)S(1)} %bitcast.22), channel_id=1, replica_groups={{0,128,32,160,64,192,96,224,4,132,36,164,68,196,100,228,8,136,40,168,72..., dimensions={0} | all-to-all | bytes 786432 | tf_op jit(solution)/shard_map/all_to_all | solution.py:596
  100.2 1.4 %shard_map.149 = bf16[576,640]{1,0:T(8,128)(2,1)} custom-call(bf16[1536,128]{1,0:T(8,128)(2,1)S(1)} %bitcast.23, bf16[320,640]{1,0:T(8,128)(2,1)S(1)} %copy-done.6, bf16[576,640]{1,0:T(8,128)(2,1)S(1)} %get-tuple-element.46.mixed_ref), custom_call_target="tpu_custom_call" | custom-call | tf_op jit(solution)/shard_map/pallas_call | solution.py:75
  (16 shorter events, 0.1 us)
Async XLA Ops:
  0.1 1.1 %copy-start = (bf16[1,12,48,640]{3,2,1,0:T(8,128)(2,1)S(1)}, bf16[1,12,48,640]{3,2,1,0:T(8,128)(2,1)}, u32[]{:S(2)}) copy-start(bf16[1,12,48,640]{3,2,1,0:T(8,128)(2,1)} %param.14) | copy-start | bytes 2211844
  1.2 8.5 %slice-start = ((s8[7372800]{0:T(1024)(128)(4,1)}), s8[4194304]{0:T(1024)(128)(4,1)S(1)}, s32[]{:S(2)}) async-start(s8[7372800]{0:T(1024)(128)(4,1)} %bitcast.18), calls=%async_computation.2 | async-start | bytes 8388608
  2.3 1.4 %collective-permute-start = (bf16[64,640]{1,0:T(8,128)(2,1)S(1)}, bf16[64,640]{1,0:T(8,128)(2,1)S(1)}, u32[]{:S(2)}, u32[]{:S(2)}) collective-permute-start(bf16[64,640]{1,0:T(8,128)(2,1)S(1)} %get-tuple-element.27), channel_id=1, source_target_pairs={{0,1},{1,0},{2,3},{3,2},{4,5},{5,4},{6,7},{7,6},{8,9},{9,8},{10,11... | collective-permute-start | bytes 245768 | tf_op jit(solution)/shard_map/ppermute | solution.py:469
  3.6 2.0 %copy-start.10 = (bf16[12,48,640]{2,1,0:T(8,128)(2,1)S(1)}, bf16[12,48,640]{2,1,0:T(8,128)(2,1)}, u32[]{:S(2)}) copy-start(bf16[12,48,640]{2,1,0:T(8,128)(2,1)} %param.15) | copy-start | bytes 2211844
  3.6 2.0 %copy-start.11 = (bf16[640,320]{0,1:T(8,128)(2,1)S(1)}, bf16[640,320]{0,1:T(8,128)(2,1)}, u32[]{:S(2)}) copy-start(bf16[640,320]{0,1:T(8,128)(2,1)} %param.20) | copy-start | bytes 1228804
  3.6 2.0 %copy-start.12 = (bf16[640,320]{0,1:T(8,128)(2,1)S(1)}, bf16[640,320]{0,1:T(8,128)(2,1)}, u32[]{:S(2)}) copy-start(bf16[640,320]{0,1:T(8,128)(2,1)} %param.21) | copy-start | bytes 1228804
  3.6 2.0 %copy-start.13 = (bf16[640,320]{0,1:T(8,128)(2,1)S(1)}, bf16[640,320]{0,1:T(8,128)(2,1)}, u32[]{:S(2)}) copy-start(bf16[640,320]{0,1:T(8,128)(2,1)} %param.19) | copy-start | bytes 1228804
  3.7 6.1 %slice-start.1 = ((s8[7372800]{0:T(1024)(128)(4,1)}), s8[3178496]{0:T(1024)(128)(4,1)S(1)}, s32[]{:S(2)}) async-start(s8[7372800]{0:T(1024)(128)(4,1)} %bitcast.18), calls=%async_computation.3 | async-start | bytes 6356992
  3.7 6.0 %collective-permute-start.1 = (bf16[64,640]{1,0:T(8,128)(2,1)S(1)}, bf16[64,640]{1,0:T(8,128)(2,1)S(1)}, u32[]{:S(2)}, u32[]{:S(2)}) collective-permute-start(bf16[64,640]{1,0:T(8,128)(2,1)S(1)} %get-tuple-element.30), channel_id=1, source_target_pairs={{0,3},{1,2},{2,1},{3,0},{4,7},{5,6},{6,5},{7,4},{8,11},{9,10},{10,... | collective-permute-start | bytes 245768 | tf_op jit(solution)/shard_map/ppermute | solution.py:469
  5.7 4.0 %copy-start.1 = (bf16[1,12,48,640]{3,2,1,0:T(8,128)(2,1)S(1)}, bf16[1,12,48,640]{3,2,1,0:T(8,128)(2,1)}, u32[]{:S(2)}) copy-start(bf16[1,12,48,640]{3,2,1,0:T(8,128)(2,1)} %param.14) | copy-start | bytes 2211844
  5.7 4.0 %copy-start.7 = (f32[640]{0:T(1024)S(1)}, f32[640]{0:T(1024)}, u32[]{:S(2)}) copy-start(f32[640]{0:T(1024)} %gain_ref.2) | copy-start | bytes 7684
  5.7 4.0 %copy-start.8 = (f32[640]{0:T(1024)S(1)}, f32[640]{0:T(1024)}, u32[]{:S(2)}) copy-start(f32[640]{0:T(1024)} %norm_gain_ref.1) | copy-start | bytes 7684
  7.5 12.8 %collective-permute-start.3 = (bf16[288,640]{1,0:T(8,128)(2,1)S(1)}, bf16[288,640]{1,0:T(8,128)(2,1)S(1)}, u32[]{:S(2)}, u32[]{:S(2)}) collective-permute-start(bf16[288,640]{1,0:T(8,128)(2,1)S(1)} %get-tuple-element.34), channel_id=1, source_target_pairs={{0,2},{1,3},{2,0},{3,1},{4,6},{5,7},{6,4},{7,5},{8,10},{9,11},{10,... | collective-permute-start | bytes 1105928 | tf_op jit(solution)/shard_map/ppermute | solution.py:469
  9.1 14.2 %collective-permute-start.8 = (bf16[576,640]{1,0:T(8,128)(2,1)S(1)}, bf16[576,640]{1,0:T(8,128)(2,1)S(1)}, u32[]{:S(2)}, u32[]{:S(2)}) collective-permute-start(bf16[576,640]{1,0:T(8,128)(2,1)S(1)} %get-tuple-element.39.refs_4_), channel_id=1, source_target_pairs={{0,1},{1,0},{2,3},{3,2},{4,5},{5,4},{6,7},{7,6},{8,9},{9,8},{10,11... | collective-permute-start | bytes 2211848 | tf_op jit(solution)/shard_map/ppermute | solution.py:469
  17.5 2.7 %collective-permute-start.6 = (bf16[288,640]{1,0:T(8,128)(2,1)S(1)}, bf16[288,640]{1,0:T(8,128)(2,1)S(1)}, u32[]{:S(2)}, u32[]{:S(2)}) collective-permute-start(bf16[288,640]{1,0:T(8,128)(2,1)S(1)} %get-tuple-element.37), channel_id=1, source_target_pairs={{0,1},{1,0},{2,3},{3,2},{4,5},{5,4},{6,7},{7,6},{8,9},{9,8},{10,11... | collective-permute-start | bytes 1105928 | tf_op jit(solution)/shard_map/ppermute | solution.py:469
  17.7 4.2 %collective-permute-start.7 = (bf16[288,640]{1,0:T(8,128)(2,1)S(1)}, bf16[288,640]{1,0:T(8,128)(2,1)S(1)}, u32[]{:S(2)}, u32[]{:S(2)}) collective-permute-start(bf16[288,640]{1,0:T(8,128)(2,1)S(1)} %get-tuple-element.38), channel_id=1, source_target_pairs={{0,1},{1,0},{2,3},{3,2},{4,5},{5,4},{6,7},{7,6},{8,9},{9,8},{10,11... | collective-permute-start | bytes 1105928 | tf_op jit(solution)/shard_map/ppermute | solution.py:469
  18.1 13.8 %collective-permute-start.5 = (bf16[320,640]{1,0:T(8,128)(2,1)S(1)}, bf16[320,640]{1,0:T(8,128)(2,1)S(1)}, u32[]{:S(2)}, u32[]{:S(2)}) collective-permute-start(bf16[320,640]{1,0:T(8,128)(2,1)S(1)} %get-tuple-element.35), channel_id=1, source_target_pairs={{0,2},{1,3},{2,0},{3,1},{4,6},{5,7},{6,4},{7,5},{8,10},{9,11},{10,... | collective-permute-start | bytes 1228808 | tf_op jit(solution)/shard_map/ppermute | solution.py:469
  20.2 3.1 %collective-permute-start.9 = (bf16[288,640]{1,0:T(8,128)(2,1)S(1)}, bf16[288,640]{1,0:T(8,128)(2,1)S(1)}, u32[]{:S(2)}, u32[]{:S(2)}) collective-permute-start(bf16[288,640]{1,0:T(8,128)(2,1)S(1)} %shard_map.140.refs_6_), channel_id=1, source_target_pairs={{0,1},{1,0},{2,3},{3,2},{4,5},{5,4},{6,7},{7,6},{8,9},{9,8},{10,11... | collective-permute-start | bytes 1105928 | tf_op jit(solution)/shard_map/ppermute | solution.py:469
  20.2 11.7 %collective-permute-start.4 = (bf16[288,640]{1,0:T(8,128)(2,1)S(1)}, bf16[288,640]{1,0:T(8,128)(2,1)S(1)}, u32[]{:S(2)}, u32[]{:S(2)}) collective-permute-start(bf16[288,640]{1,0:T(8,128)(2,1)S(1)} %shard_map.140.refs_6_), channel_id=1, source_target_pairs={{0,32},{4,36},{8,40},{12,44},{16,48},{20,52},{24,56},{28,60},{32,0... | collective-permute-start | bytes 1105928 | tf_op jit(solution)/shard_map/ppermute | solution.py:529
  21.9 16.2 %collective-permute-start.2 = (bf16[256,640]{1,0:T(8,128)(2,1)S(1)}, bf16[256,640]{1,0:T(8,128)(2,1)S(1)}, u32[]{:S(2)}, u32[]{:S(2)}) collective-permute-start(bf16[256,640]{1,0:T(8,128)(2,1)S(1)} %get-tuple-element.33), channel_id=1, source_target_pairs={{0,2},{1,3},{2,0},{3,1},{4,6},{5,7},{6,4},{7,5},{8,10},{9,11},{10,... | collective-permute-start | bytes 983048 | tf_op jit(solution)/shard_map/ppermute | solution.py:469
  32.0 2.4 %collective-permute-start.12 = (bf16[160,640]{1,0:T(8,128)(2,1)S(1)}, bf16[160,640]{1,0:T(8,128)(2,1)S(1)}, u32[]{:S(2)}, u32[]{:S(2)}) collective-permute-start(bf16[160,640]{1,0:T(8,128)(2,1)S(1)} %get-tuple-element.42.refs_4_), channel_id=1, source_target_pairs={{0,1},{1,0},{2,3},{3,2},{4,5},{5,4},{6,7},{7,6},{8,9},{9,8},{10,11... | collective-permute-start | bytes 614408 | tf_op jit(solution)/shard_map/ppermute | solution.py:469
  32.1 2.3 %collective-permute-start.13 = (bf16[160,640]{1,0:T(8,128)(2,1)S(1)}, bf16[160,640]{1,0:T(8,128)(2,1)S(1)}, u32[]{:S(2)}, u32[]{:S(2)}) collective-permute-start(bf16[160,640]{1,0:T(8,128)(2,1)S(1)} %get-tuple-element.43.refs_5_), channel_id=1, source_target_pairs={{0,1},{1,0},{2,3},{3,2},{4,5},{5,4},{6,7},{7,6},{8,9},{9,8},{10,11... | collective-permute-start | bytes 614408 | tf_op jit(solution)/shard_map/ppermute | solution.py:469
  32.6 1.5 %collective-permute-start.10 = (bf16[144,640]{1,0:T(8,128)(2,1)S(1)}, bf16[144,640]{1,0:T(8,128)(2,1)S(1)}, u32[]{:S(2)}, u32[]{:S(2)}) collective-permute-start(bf16[144,640]{1,0:T(8,128)(2,1)S(1)} %get-tuple-element.41.refs_2_), channel_id=1, source_target_pairs={{0,1},{1,0},{2,3},{3,2},{4,5},{5,4},{6,7},{7,6},{8,9},{9,8},{10,11... | collective-permute-start | bytes 552968 | tf_op jit(solution)/shard_map/ppermute | solution.py:469
  32.7 1.7 %collective-permute-start.11 = (bf16[144,640]{1,0:T(8,128)(2,1)S(1)}, bf16[144,640]{1,0:T(8,128)(2,1)S(1)}, u32[]{:S(2)}, u32[]{:S(2)}) collective-permute-start(bf16[144,640]{1,0:T(8,128)(2,1)S(1)} %get-tuple-element.40.refs_3_.refs_1_), channel_id=1, source_target_pairs={{0,1},{1,0},{2,3},{3,2},{4,5},{5,4},{6,7},{7,6},{8,9},{9,8},{10,11... | collective-permute-start | bytes 552968 | tf_op jit(solution)/shard_map/ppermute | solution.py:469
  38.1 1.6 %copy-start.5 = (bf16[320,640]{1,0:T(8,128)(2,1)S(1)}, bf16[320,640]{1,0:T(8,128)(2,1)}, u32[]{:S(2)}) copy-start(bf16[320,640]{1,0:T(8,128)(2,1)} %weight_ref.2) | copy-start | bytes 1228804
  38.1 1.6 %copy-start.9 = (f32[640]{0:T(1024)S(1)}, f32[640]{0:T(1024)}, u32[]{:S(2)}) copy-start(f32[640]{0:T(1024)} %gain_ref.3) | copy-start | bytes 7684
  38.1 1.6 %collective-permute-start.14 = (bf16[256,640]{1,0:T(8,128)(2,1)S(1)}, bf16[256,640]{1,0:T(8,128)(2,1)S(1)}, u32[]{:S(2)}, u32[]{:S(2)}) collective-permute-start(bf16[256,640]{1,0:T(8,128)(2,1)S(1)} %shard_map.145.refs_1_), channel_id=1, source_target_pairs={{0,1},{1,0},{2,3},{3,2},{4,5},{5,4},{6,7},{7,6},{8,9},{9,8},{10,11... | collective-permute-start | bytes 983048 | tf_op jit(solution)/shard_map/ppermute | solution.py:469
  39.8 37.3 %copy-start.2 = (bf16[640,320]{0,1:T(8,128)(2,1)S(1)}, bf16[640,320]{0,1:T(8,128)(2,1)}, u32[]{:S(2)}) copy-start(bf16[640,320]{0,1:T(8,128)(2,1)} %param.24) | copy-start | bytes 1228804
  39.8 37.3 %copy-start.3 = (bf16[640,320]{0,1:T(8,128)(2,1)S(1)}, bf16[640,320]{0,1:T(8,128)(2,1)}, u32[]{:S(2)}) copy-start(bf16[640,320]{0,1:T(8,128)(2,1)} %param.25) | copy-start | bytes 1228804
  39.8 37.3 %copy-start.4 = (bf16[640,320]{0,1:T(8,128)(2,1)S(1)}, bf16[640,320]{0,1:T(8,128)(2,1)}, u32[]{:S(2)}) copy-start(bf16[640,320]{0,1:T(8,128)(2,1)} %param.26) | copy-start | bytes 1228804
  77.1 23.1 %copy-start.6 = (bf16[320,640]{1,0:T(8,128)(2,1)S(1)}, bf16[320,640]{1,0:T(8,128)(2,1)}, u32[]{:S(2)}) copy-start(bf16[320,640]{1,0:T(8,128)(2,1)} %weight_ref.3) | copy-start | bytes 1228804
